TPU v7x, 32 devices: a whole 2x2x4 slice. The times are simulated.
32 devices in a mesh: gx: 4 (over y, core), gy: 8 (over z, x).
Axes of the slice: x: 2, y: 2, z: 4, core: 2. Of those that a mesh axis runs over, the one named last changes fastest.
Arguments:
- inputs: bfloat16 [64, 128, 8, 256], P('gx', 'gy'), may hold values from -6 to 6
- preact: bfloat16 [64, 128, 8, 256], P('gx', 'gy'), may hold values from -6 to 6
- out_grad: bfloat16 [64, 128, 8, 256], P('gx', 'gy'), may hold values from -6 to 6
- weight_one: bfloat16 [6912, 256], P('gx', 'gy'), may hold values from -0.078125 to 0.078125
- weight_two: bfloat16 [6912, 256], P('gx', 'gy'), may hold values from -0.078125 to 0.078125
- occupancy: int32 [8, 16, 1], P('gx', 'gy'), may hold values from 0 to 1, as said below
Outputs:
- input_grad: bfloat16 [64, 128, 8, 256], P('gx', 'gy')
- weight_one_grad: float32 [6912, 256], P('gx', 'gy')
- weight_two_grad: float32 [6912, 256], P('gx', 'gy')
Inputs may be any that keep to these rules, and one draw needn't show every extreme that they name: `occupancy`: among the 2 x 2 x 1 block of one device's tile at most 2 are occupied, and in every draw some device's tile has exactly 2.
All inputs are finite; a program needn't handle non-finite values.
Results may differ from a plain program's by a relative error of at most 0.005.
Values may be sent and summed in bfloat16 or wider, within the bound.
No kernel may reach another device: no remote copies, remote signals or barrier semaphores. Data moves between devices by JAX's collectives and lax.ppermute only.
A program may use at most 128 MiB of HBM per device.

v0:
```python
import jax
import jax.numpy as jnp
from jax import lax
from jax.sharding import PartitionSpec as P

B = 8
AMAX = 2


stencil_taps = [
    (shift_x, shift_y, shift_z)
    for shift_x in (-1, 0, 1)
    for shift_y in (-1, 0, 1)
    for shift_z in (-1, 0, 1)
]


def extended(x, sides, width):
    for axis, dim in sides:
        size, length = (lax.axis_size(axis), x.shape[dim])
        up = [(i, (i + 1) % size) for i in range(size - 1)]
        down = [(j, i) for i, j in up]
        last = lax.slice_in_dim(x, length - width, length, axis=dim)
        initial = lax.slice_in_dim(x, 0, width, axis=dim)
        before = lax.ppermute(last, axis, up)
        after = lax.ppermute(initial, axis, down)
        x = jnp.concatenate([before, x, after], axis=dim)
    return x


def block_work(pad_in, pad_grad, weight, corner, valid, edge, totals):
    chans = pad_in.shape[-1]
    sizes = (edge + 2, edge + 2, edge + 2, chans)
    patch_in = lax.dynamic_slice(pad_in, corner, sizes)
    patch_grad = lax.dynamic_slice(pad_grad, corner, sizes)
    center = patch_grad[1 : edge + 1, 1 : edge + 1, 1 : edge + 1, :].reshape(
        edge * edge * edge, chans
    )
    center = jnp.where(valid, center, jnp.zeros_like(center))
    back = jnp.zeros((edge * edge * edge, chans), jnp.float32)
    fresh = []
    for index, (shift_x, shift_y, shift_z) in enumerate(stencil_taps):
        piece_in = patch_in[
            1 + shift_x : 1 + shift_x + edge,
            1 + shift_y : 1 + shift_y + edge,
            1 + shift_z : 1 + shift_z + edge,
            :,
        ].reshape(edge * edge * edge, chans)
        fresh.append(
            totals[index]
            + lax.dot_general(
                piece_in, center, (((0,), (0,)), ((), ())), preferred_element_type=jnp.float32
            )
        )
        piece_grad = patch_grad[
            1 - shift_x : 1 - shift_x + edge,
            1 - shift_y : 1 - shift_y + edge,
            1 - shift_z : 1 - shift_z + edge,
            :,
        ].reshape(edge * edge * edge, chans)
        tap_rows = weight[index * chans : (index + 1) * chans, :]
        back = back + lax.dot_general(
            piece_grad, tap_rows, (((1,), (1,)), ((), ())), preferred_element_type=jnp.float32
        )
    return (tuple(fresh), back)


def place(tile, values, corner, valid, edge):
    block = values.reshape(edge, edge, edge, values.shape[-1])
    old = lax.dynamic_slice(tile, corner, block.shape)
    return lax.dynamic_update_slice(tile, jnp.where(valid, block, old), corner)


def fetch_kernels(weight_one, weight_two):
    rows_full = (
        lax.all_gather(weight_one, "gx", axis=0, tiled=True),
        lax.all_gather(weight_two, "gx", axis=0, tiled=True),
    )
    return (
        lax.all_gather(rows_full[0], "gy", axis=1, tiled=True),
        lax.all_gather(rows_full[1], "gy", axis=1, tiled=True),
    )


def reduce_kernels(sum_one, sum_two):
    by_cols = (
        lax.psum_scatter(sum_one, "gy", scatter_dimension=1, tiled=True),
        lax.psum_scatter(sum_two, "gy", scatter_dimension=1, tiled=True),
    )
    return (
        lax.psum_scatter(by_cols[0], "gx", scatter_dimension=0, tiled=True),
        lax.psum_scatter(by_cols[1], "gx", scatter_dimension=0, tiled=True),
    )


def body(inputs, preact, out_grad, weight_one, weight_two, occupancy):
    edge = B
    chans = inputs.shape[-1]
    mask = jnp.repeat(jnp.repeat(jnp.repeat(occupancy, edge, 0), edge, 1), edge, 2)
    active = (mask > 0)[..., None]
    zero = jnp.zeros((), jnp.bfloat16)
    second_in = jnp.where(active & (preact > 0), preact, zero)
    first_in = jnp.where(active, inputs, zero)
    grad_two = jnp.where(active, out_grad, zero)
    stacked = jnp.stack([second_in, first_in, grad_two])
    rimmed = extended(stacked, (("gx", 1), ("gy", 2)), 1)
    rimmed = jnp.pad(rimmed, ((0, 0), (0, 0), (0, 0), (1, 1), (0, 0)))
    pad_second = rimmed[0]
    pad_first = rimmed[1]
    pad_grad = rimmed[2]
    full_one, full_two = fetch_kernels(weight_one, weight_two)
    flat = occupancy.reshape(-1)
    found = jnp.nonzero(flat, size=AMAX, fill_value=0)[0].astype(jnp.int32)
    valid = jnp.arange(AMAX) < jnp.sum(flat)
    span_y = occupancy.shape[1]
    span_z = occupancy.shape[2]
    corner_x = found // (span_y * span_z) * edge
    corner_y = found // span_z % span_y * edge
    corner_z = found % span_z * edge
    anchor = jnp.zeros((), jnp.int32)
    empty_sums = tuple((jnp.zeros((chans, chans), jnp.float32) for _ in range(27)))

    def first_pass(carry, item):
        totals, grad_tile = carry
        cx, cy, cz, okay = item
        corner = (cx, cy, cz, anchor)
        totals, back = block_work(pad_second, pad_grad, full_two, corner, okay, edge, totals)
        pre_block = lax.dynamic_slice(preact, corner, (edge, edge, edge, chans)).reshape(
            edge * edge * edge, chans
        )
        gated = jnp.where(pre_block > 0, back, jnp.zeros_like(back)).astype(jnp.bfloat16)
        return ((totals, place(grad_tile, gated, corner, okay, edge)), None)

    start = (empty_sums, jnp.zeros(inputs.shape, jnp.bfloat16))
    (sums_two, grad_one), _ = lax.scan(first_pass, start, (corner_x, corner_y, corner_z, valid))
    pad_one = extended(grad_one, (("gx", 0), ("gy", 1)), 1)
    pad_one = jnp.pad(pad_one, ((0, 0), (0, 0), (1, 1), (0, 0)))

    def second_pass(carry, item):
        totals, out_tile = carry
        cx, cy, cz, okay = item
        corner = (cx, cy, cz, anchor)
        totals, back = block_work(pad_first, pad_one, full_one, corner, okay, edge, totals)
        return ((totals, place(out_tile, back.astype(jnp.bfloat16), corner, okay, edge)), None)

    start = (empty_sums, jnp.zeros(inputs.shape, jnp.bfloat16))
    (sums_one, input_grad), _ = lax.scan(second_pass, start, (corner_x, corner_y, corner_z, valid))
    sum_one = jnp.concatenate(sums_one, axis=0)
    sum_two = jnp.concatenate(sums_two, axis=0)
    reduced_one, reduced_two = reduce_kernels(sum_one, sum_two)
    scale = float(lax.axis_size("gx") * lax.axis_size("gy") * B**3) ** (-0.5)
    return (input_grad, reduced_one * scale, reduced_two * scale)


def solution(mesh):
    return jax.shard_map(
        body,
        mesh=mesh,
        in_specs=(
            P("gx", "gy", None, None),
            P("gx", "gy", None, None),
            P("gx", "gy", None, None),
            P("gx", "gy"),
            P("gx", "gy"),
            P("gx", "gy", None),
        ),
        out_specs=(P("gx", "gy", None, None), P("gx", "gy"), P("gx", "gy")),
        check_vma=False,
    )
```

profile of v0, /device:TPU:0, one launch (start us, length us, event | category | flops | bytes accessed | tf_op | source)
XLA Modules:
  0.0 679.0 jit_solution(18084767164537101921)
XLA Ops:
  7.2 8.5 %all-gather = bf16[4,1728,32]{1,2,0:T(8,128)(2,1)S(1)} all-gather(bf16[1,1728,32]{1,2,0:T(8,128)(2,1)} %bitcast.871), channel_id=1, replica_groups=mesh['gx'=4,'gy'=8] {'gx'}, dimensions={0}, use_global_device_ids=true | all-gather | bytes 552960 | tf_op jit(solution)/shard_map/all_gather | solution.py:77
  18.4 2.7 fusion.237
  21.9 2.2 collective-permute-start
  25.4 10.2 %all-gather.1 = bf16[4,1728,32]{1,2,0:T(8,128)(2,1)S(1)} all-gather(bf16[1,1728,32]{1,2,0:T(8,128)(2,1)S(1)} %bitcast.872), channel_id=1, replica_groups=mesh['gx'=4,'gy'=8] {'gx'}, dimensions={0}, use_global_device_ids=true | all-gather | bytes 552960 | tf_op jit(solution)/shard_map/all_gather | solution.py:76
  36.8 2.2 reshape.439
  42.7 3.4 collective-permute-start.2
  47.5 7.5 %collective-permute-done.2 = bf16[3,18,1,8,256]{4,3,2,1,0:T(8,128)(2,1)S(1)} collective-permute-done((bf16[3,18,1,8,256]{4,3,2,1,0:T(8,128)(2,1)S(1)}, bf16[3,18,1,8,256]{4,3,2,1,0:T(8,128)(2,1)S(1)}, u32[]{:S(2)}, u32[]{:S(2)}) %collective-permute-start.2) | collective-permute-done | bytes 221216 | tf_op jit(solution)/shard_map/ppermute | solution.py:25
  55.0 5.2 collective-permute-done.3
  60.2 11.0 %select_maximum_fusion = bf16[3,18,18,10,256]{4,3,2,1,0:T(8,128)(2,1)S(1)} fusion(bf16[3,18,1,8,256]{4,3,2,1,0:T(8,128)(2,1)S(1)} %collective-permute-done.3, bf16[3,18,1,8,256]{4,3,2,1,0:T(8,128)(2,1)S(1)} %collective-permute-done.2, bf16[3,1,16,8,256]{4,3,2,1,0:T(8,128)(2,1)S(1)} %collective-permute-done.1, ...), kind=kLoop, calls=%fused_computation.392 | loop fusion | flops 59719680 | bytes 8957952 | tf_op jit(solution)/shard_map/concatenate | solution.py:27
  71.2 2.6 slice_bitcast_fusion
  73.8 16.9 %all-gather.5.cloned.1.call-done = bf16[6912,256]{0,1:T(8,128)(2,1)} async-done(((bf16[6912,32]{0,1:T(8,128)(2,1)}), bf16[6912,256]{0,1:T(8,128)(2,1)}) %all-gather.5.cloned.1.call-update) | async-done | bytes 3538960 | tf_op jit(solution)/shard_map/all_gather | solution.py:81
  90.7 6.0 copy.186
  97.8 124.7 %while.132 = (s32[]{:T(128)}, f32[256,256]{1,0:T(8,128)}, f32[256,256]{1,0:T(8,128)}, f32[256,256]{1,0:T(8,128)}, f32[256,256]{1,0:T(8,128)}, /*index=5*/f32[256...) while((s32[]{:T(128)}, f32[256,256]{1,0:T(8,128)}, ...), condition=%wide.region_6.7_spmd.clone, body=%wide.region_5.6_spmd.clone.sunk | while | flops 3634888704 | bytes 159338048 | solution.py:135
  103.2 2.1 constant_dynamic-slice_fusion.56
  117.7 2.4 select_dynamic-update-slice_fusion.4
  120.1 3.5 fusion.617
  159.1 2.1 constant_dynamic-slice_fusion.56
  173.6 2.4 select_dynamic-update-slice_fusion.4
  176.0 3.1 fusion.617
  222.5 1.9 copy.216
  224.5 1.8 copy.217
  226.3 1.8 copy.218
  228.1 1.9 copy.219
  230.0 1.8 copy.220
  231.8 1.8 copy.221
  233.7 1.8 copy.222
  252.9 1.4 collective-permute-start.4
  254.3 1.4 collective-permute-start.5
  255.8 1.7 constant_dynamic-update-slice_fusion.56
  257.4 1.7 constant_dynamic-update-slice_fusion.55
  259.2 1.7 constant_dynamic-update-slice_fusion.54
  260.9 1.7 constant_dynamic-update-slice_fusion.53
  262.6 1.7 constant_dynamic-update-slice_fusion.52
  264.3 1.7 constant_dynamic-update-slice_fusion.51
  282.2 1.7 collective-permute-start.6
  286.1 6.0 copy.188
  292.0 2.4 fusion.236
  295.5 103.9 %while.133 = (s32[]{:T(128)}, f32[256,256]{1,0:T(8,128)S(1)}, f32[256,256]{1,0:T(8,128)}, f32[256,256]{1,0:T(8,128)}, f32[256,256]{1,0:T(8,128)}, /*index=5*/f32...) while((s32[]{:T(128)}, f32[256,256]{1,0:T(8,128)S(1)}, ...), condition=%wide.region_8.9_spmd.clone, body=%wide.region_7.8_spmd.clone.sunk | while | flops 3634626560 | bytes 154619312 | solution.py:147
  300.6 2.1 constant_dynamic-slice_fusion.57
  313.2 2.4 select_dynamic-update-slice_fusion.5
  315.6 3.0 fusion.727
  352.5 2.1 constant_dynamic-slice_fusion.57
  365.1 2.4 select_dynamic-update-slice_fusion.5
  367.5 3.0 fusion.727
  400.4 1.8 copy.190
  402.3 1.8 copy.191
  404.1 1.8 copy.192
  405.9 1.8 copy.193
  407.7 1.8 copy.194
  409.5 1.8 copy.195
  425.7 1.8 constant_dynamic-update-slice_fusion.29
  427.5 1.7 constant_dynamic-update-slice_fusion.28
  429.2 1.7 constant_dynamic-update-slice_fusion.27
  430.9 1.7 constant_dynamic-update-slice_fusion.26
  432.7 1.7 constant_dynamic-update-slice_fusion.25
  434.4 1.7 constant_dynamic-update-slice_fusion.24
  436.0 1.7 constant_dynamic-update-slice_fusion.23
  452.7 3.4 copy.300
  456.2 128.5 %reduce-scatter.9.cloned.1.call-done = f32[6912,32]{0,1:T(8,128)} async-done(((f32[6912,256]{0,1:T(8,128)}), f32[6912,32]{0,1:T(8,128)}) %reduce-scatter.9.cloned.1.call-update) | async-done | bytes 884752 | tf_op jit(solution)/shard_map/reduce_scatter | solution.py:87
  584.7 3.4 copy.298
  588.1 38.5 %reduce-scatter.15.cloned.1.call-done = f32[1728,32]{1,0:T(8,128)} async-done(((f32[6912,32]{1,0:T(8,128)}), f32[1728,32]{1,0:T(8,128)}) %reduce-scatter.15.cloned.1.call-update) | async-done | bytes 221200
  626.7 1.4 copy.301
  628.8 40.9 %reduce-scatter.13.cloned.1.call-done = f32[1728,32]{1,0:T(8,128)} async-done(((f32[6912,32]{1,0:T(8,128)}), f32[1728,32]{1,0:T(8,128)}) %reduce-scatter.13.cloned.1.call-update) | async-done | bytes 221200
  669.8 1.4 copy.299
  (947 shorter events, 233.9 us)
Async XLA Ops:
  7.2 83.6 %all-gather.5.cloned.1.call-start = ((), (), s32[]{:S(2)}) async-start(), calls=%async_computation.4 | async-start | bytes 3981312 | tf_op jit(solution)/shard_map/all_gather | solution.py:81
  17.3 268.8 %all-gather.7.cloned.1.call-start = ((), (), s32[]{:S(2)}) async-start(), calls=%async_computation.5 | async-start | bytes 3981312 | tf_op jit(solution)/shard_map/all_gather | solution.py:80
  18.4 7.1 %copy-start.156 = (bf16[1728,32]{0,1:T(8,128)(2,1)S(1)}, bf16[1728,32]{0,1:T(8,128)(2,1)}, u32[]{:S(2)}) copy-start(bf16[1728,32]{0,1:T(8,128)(2,1)} %param.13) | copy-start | bytes 331780
  21.1 18.0 %copy-start.157 = (s32[2,2,1]{1,2,0:T(1,128)S(1)}, s32[2,2,1]{1,2,0:T(1,128)}, u32[]{:S(2)}) copy-start(s32[2,2,1]{1,2,0:T(1,128)} %param.15) | copy-start | bytes 52
  21.9 20.8 %collective-permute-start = (bf16[3,1,16,8,256]{4,3,2,1,0:T(8,128)(2,1)}, bf16[3,1,16,8,256]{4,3,2,1,0:T(8,128)(2,1)S(1)}, u32[]{:S(2)}, u32[]{:S(2)}) collective-permute-start(bf16[3,1,16,8,256]{4,3,2,1,0:T(8,128)(2,1)} %get-tuple-element.1189), channel_id=1, source_target_pairs={{0,8},{8,16},{16,24},{1,9},{9,17},{17,25},{2,10},{10,18},{18,26},{... | collective-permute-start | bytes 589832 | tf_op jit(solution)/shard_map/ppermute | solution.py:25
  24.1 18.5 %collective-permute-start.1 = (bf16[3,1,16,8,256]{4,3,2,1,0:T(8,128)(2,1)}, bf16[3,1,16,8,256]{4,3,2,1,0:T(8,128)(2,1)S(1)}, u32[]{:S(2)}, u32[]{:S(2)}) collective-permute-start(bf16[3,1,16,8,256]{4,3,2,1,0:T(8,128)(2,1)} %get-tuple-element.1190), channel_id=1, source_target_pairs={{8,0},{16,8},{24,16},{9,1},{17,9},{25,17},{10,2},{18,10},{26,18},{... | collective-permute-start | bytes 589832 | tf_op jit(solution)/shard_map/ppermute | solution.py:26
  39.0 413.7 %reduce-scatter.11.cloned.1.call-start = ((), (), s32[]{:S(2)}) async-start(), calls=%async_computation.7 | async-start | bytes 7962624 | tf_op jit(solution)/shard_map/reduce_scatter | solution.py:88
  42.7 12.3 %collective-permute-start.2 = (bf16[3,18,1,8,256]{4,3,2,1,0:T(8,128)(2,1)S(1)}, bf16[3,18,1,8,256]{4,3,2,1,0:T(8,128)(2,1)S(1)}, u32[]{:S(2)}, u32[]{:S(2)}) collective-permute-start(bf16[3,18,1,8,256]{4,3,2,1,0:T(8,128)(2,1)S(1)} %get-tuple-element.1187), channel_id=1, source_target_pairs={{0,1},{1,2},{2,3},{3,4},{4,5},{5,6},{6,7},{8,9},{9,10},{10,11},{11... | collective-permute-start | bytes 663560 | tf_op jit(solution)/shard_map/ppermute | solution.py:25
  46.2 14.0 %collective-permute-start.3 = (bf16[3,18,1,8,256]{4,3,2,1,0:T(8,128)(2,1)S(1)}, bf16[3,18,1,8,256]{4,3,2,1,0:T(8,128)(2,1)S(1)}, u32[]{:S(2)}, u32[]{:S(2)}) collective-permute-start(bf16[3,18,1,8,256]{4,3,2,1,0:T(8,128)(2,1)S(1)} %get-tuple-element.1188), channel_id=1, source_target_pairs={{1,0},{2,1},{3,2},{4,3},{5,4},{6,5},{7,6},{9,8},{10,9},{11,10},{12... | collective-permute-start | bytes 663560 | tf_op jit(solution)/shard_map/ppermute | solution.py:26
  120.1 3.5 copy-start.105
  222.5 13.1 %copy-start.149 = (f32[256,256]{1,0:T(8,128)S(1)}, f32[256,256]{1,0:T(8,128)}, u32[]{:S(2)}) copy-start(f32[256,256]{1,0:T(8,128)} %get-tuple-element.602) | copy-start | bytes 786436
  222.5 13.9 %copy-start.152 = (f32[256,256]{1,0:T(8,128)S(1)}, f32[256,256]{1,0:T(8,128)}, u32[]{:S(2)}) copy-start(f32[256,256]{1,0:T(8,128)} %get-tuple-element.603) | copy-start | bytes 786436
  222.5 14.7 %copy-start.155 = (f32[256,256]{1,0:T(8,128)S(1)}, f32[256,256]{1,0:T(8,128)}, u32[]{:S(2)}) copy-start(f32[256,256]{1,0:T(8,128)} %get-tuple-element.604) | copy-start | bytes 786436
  222.5 15.6 %copy-start.97 = (f32[256,256]{1,0:T(8,128)S(1)}, f32[256,256]{1,0:T(8,128)}, u32[]{:S(2)}) copy-start(f32[256,256]{1,0:T(8,128)} %get-tuple-element.605) | copy-start | bytes 786436
  222.5 16.5 %copy-start.100 = (f32[256,256]{1,0:T(8,128)S(1)}, f32[256,256]{1,0:T(8,128)}, u32[]{:S(2)}) copy-start(f32[256,256]{1,0:T(8,128)} %get-tuple-element.606) | copy-start | bytes 786436
  222.5 17.3 %copy-start.103 = (f32[256,256]{1,0:T(8,128)S(1)}, f32[256,256]{1,0:T(8,128)}, u32[]{:S(2)}) copy-start(f32[256,256]{1,0:T(8,128)} %get-tuple-element.607) | copy-start | bytes 786436
  222.5 18.2 %copy-start.104 = (f32[256,256]{1,0:T(8,128)S(1)}, f32[256,256]{1,0:T(8,128)}, u32[]{:S(2)}) copy-start(f32[256,256]{1,0:T(8,128)} %get-tuple-element.608) | copy-start | bytes 786436
  224.5 17.1 %copy-start.107 = (f32[256,256]{1,0:T(8,128)S(1)}, f32[256,256]{1,0:T(8,128)}, u32[]{:S(2)}) copy-start(f32[256,256]{1,0:T(8,128)} %get-tuple-element.609) | copy-start | bytes 786436
  226.3 16.1 %copy-start.110 = (f32[256,256]{1,0:T(8,128)S(1)}, f32[256,256]{1,0:T(8,128)}, u32[]{:S(2)}) copy-start(f32[256,256]{1,0:T(8,128)} %get-tuple-element.610) | copy-start | bytes 786436
  228.1 15.1 %copy-start.113 = (f32[256,256]{1,0:T(8,128)S(1)}, f32[256,256]{1,0:T(8,128)}, u32[]{:S(2)}) copy-start(f32[256,256]{1,0:T(8,128)} %get-tuple-element.611) | copy-start | bytes 786436
  230.0 14.1 %copy-start.116 = (f32[256,256]{1,0:T(8,128)S(1)}, f32[256,256]{1,0:T(8,128)}, u32[]{:S(2)}) copy-start(f32[256,256]{1,0:T(8,128)} %get-tuple-element.612) | copy-start | bytes 786436
  231.8 13.1 %copy-start.119 = (f32[256,256]{1,0:T(8,128)S(1)}, f32[256,256]{1,0:T(8,128)}, u32[]{:S(2)}) copy-start(f32[256,256]{1,0:T(8,128)} %get-tuple-element.613) | copy-start | bytes 786436
  233.7 11.3 %copy-start.122 = (f32[256,256]{1,0:T(8,128)S(1)}, f32[256,256]{1,0:T(8,128)}, u32[]{:S(2)}) copy-start(f32[256,256]{1,0:T(8,128)} %get-tuple-element.614) | copy-start | bytes 786436
  241.5 11.3 %copy-start.4 = (bf16[16,16,8,256]{3,2,1,0:T(8,128)(2,1)S(1)}, bf16[16,16,8,256]{3,2,1,0:T(8,128)(2,1)}, u32[]{:S(2)}) copy-start(bf16[16,16,8,256]{3,2,1,0:T(8,128)(2,1)} %get-tuple-element.566) | copy-start | bytes 3145732
  252.8 13.3 %copy-start.19 = (f32[256,256]{0,1:T(8,128)S(1)}, f32[256,256]{0,1:T(8,128)}, u32[]{:S(2)}) copy-start(f32[256,256]{0,1:T(8,128)} %copy.222) | copy-start | bytes 786436
  252.8 14.0 %copy-start.18 = (f32[256,256]{0,1:T(8,128)S(1)}, f32[256,256]{0,1:T(8,128)}, u32[]{:S(2)}) copy-start(f32[256,256]{0,1:T(8,128)} %copy.223) | copy-start | bytes 786436
  252.8 14.8 %copy-start.17 = (f32[256,256]{0,1:T(8,128)S(1)}, f32[256,256]{0,1:T(8,128)}, u32[]{:S(2)}) copy-start(f32[256,256]{0,1:T(8,128)} %copy.224) | copy-start | bytes 786436
  252.8 15.5 %copy-start.16 = (f32[256,256]{0,1:T(8,128)S(1)}, f32[256,256]{0,1:T(8,128)}, u32[]{:S(2)}) copy-start(f32[256,256]{0,1:T(8,128)} %copy.225) | copy-start | bytes 786436
  252.8 16.2 %copy-start.15 = (f32[256,256]{0,1:T(8,128)S(1)}, f32[256,256]{0,1:T(8,128)}, u32[]{:S(2)}) copy-start(f32[256,256]{0,1:T(8,128)} %copy.226) | copy-start | bytes 786436
  252.8 17.0 %copy-start.14 = (f32[256,256]{0,1:T(8,128)S(1)}, f32[256,256]{0,1:T(8,128)}, u32[]{:S(2)}) copy-start(f32[256,256]{0,1:T(8,128)} %copy.227) | copy-start | bytes 786436
  252.8 17.7 %copy-start.13 = (f32[256,256]{0,1:T(8,128)S(1)}, f32[256,256]{0,1:T(8,128)}, u32[]{:S(2)}) copy-start(f32[256,256]{0,1:T(8,128)} %copy.228) | copy-start | bytes 786436
  252.9 18.5 %copy-start.12 = (f32[256,256]{0,1:T(8,128)S(1)}, f32[256,256]{0,1:T(8,128)}, u32[]{:S(2)}) copy-start(f32[256,256]{0,1:T(8,128)} %copy.229) | copy-start | bytes 786436
  252.9 28.2 %collective-permute-start.4 = (bf16[1,16,8,256]{3,2,1,0:T(8,128)(2,1)S(1)}, bf16[1,16,8,256]{3,2,1,0:T(8,128)(2,1)S(1)}, u32[]{:S(2)}, u32[]{:S(2)}) collective-permute-start(bf16[1,16,8,256]{3,2,1,0:T(8,128)(2,1)S(1)} %get-tuple-element.1194), channel_id=1, source_target_pairs={{0,8},{8,16},{16,24},{1,9},{9,17},{17,25},{2,10},{10,18},{18,26},{... | collective-permute-start | bytes 196616 | tf_op jit(solution)/shard_map/ppermute | solution.py:25
  254.3 17.8 %copy-start.11 = (f32[256,256]{0,1:T(8,128)S(1)}, f32[256,256]{0,1:T(8,128)}, u32[]{:S(2)}) copy-start(f32[256,256]{0,1:T(8,128)} %copy.230) | copy-start | bytes 786436
  254.3 26.9 %collective-permute-start.5 = (bf16[1,16,8,256]{3,2,1,0:T(8,128)(2,1)S(1)}, bf16[1,16,8,256]{3,2,1,0:T(8,128)(2,1)S(1)}, u32[]{:S(2)}, u32[]{:S(2)}) collective-permute-start(bf16[1,16,8,256]{3,2,1,0:T(8,128)(2,1)S(1)} %get-tuple-element.1193), channel_id=1, source_target_pairs={{8,0},{16,8},{24,16},{9,1},{17,9},{25,17},{10,2},{18,10},{26,18},{... | collective-permute-start | bytes 196616 | tf_op jit(solution)/shard_map/ppermute | solution.py:26
  257.4 15.4 %copy-start.10 = (f32[256,256]{0,1:T(8,128)S(1)}, f32[256,256]{0,1:T(8,128)}, u32[]{:S(2)}) copy-start(f32[256,256]{0,1:T(8,128)} %copy.231) | copy-start | bytes 786436
  259.2 14.4 %copy-start.9 = (f32[256,256]{0,1:T(8,128)S(1)}, f32[256,256]{0,1:T(8,128)}, u32[]{:S(2)}) copy-start(f32[256,256]{0,1:T(8,128)} %copy.232) | copy-start | bytes 786436
  260.9 13.4 %copy-start.8 = (f32[256,256]{0,1:T(8,128)S(1)}, f32[256,256]{0,1:T(8,128)}, u32[]{:S(2)}) copy-start(f32[256,256]{0,1:T(8,128)} %copy.233) | copy-start | bytes 786436
  282.2 9.8 %collective-permute-start.6 = (bf16[18,1,8,256]{3,2,1,0:T(8,128)(2,1)S(1)}, bf16[18,1,8,256]{3,2,1,0:T(8,128)(2,1)S(1)}, u32[]{:S(2)}, u32[]{:S(2)}) collective-permute-start(bf16[18,1,8,256]{3,2,1,0:T(8,128)(2,1)S(1)} %get-tuple-element.1191), channel_id=1, source_target_pairs={{0,1},{1,2},{2,3},{3,4},{4,5},{5,6},{6,7},{8,9},{9,10},{10,11},{11... | collective-permute-start | bytes 221192 | tf_op jit(solution)/shard_map/ppermute | solution.py:25
  283.9 8.1 %collective-permute-start.7 = (bf16[18,1,8,256]{3,2,1,0:T(8,128)(2,1)S(1)}, bf16[18,1,8,256]{3,2,1,0:T(8,128)(2,1)S(1)}, u32[]{:S(2)}, u32[]{:S(2)}) collective-permute-start(bf16[18,1,8,256]{3,2,1,0:T(8,128)(2,1)S(1)} %get-tuple-element.1192), channel_id=1, source_target_pairs={{1,0},{2,1},{3,2},{4,3},{5,4},{6,5},{7,6},{9,8},{10,9},{11,10},{12... | collective-permute-start | bytes 221192 | tf_op jit(solution)/shard_map/ppermute | solution.py:26
  286.0 298.8 %reduce-scatter.9.cloned.1.call-start = ((), (), s32[]{:S(2)}) async-start(), calls=%async_computation.6 | async-start | bytes 7962624 | tf_op jit(solution)/shard_map/reduce_scatter | solution.py:87
  292.0 3.5 copy-start.27
  399.5 11.8 %copy-start.42 = (f32[256,256]{1,0:T(8,128)S(1)}, f32[256,256]{1,0:T(8,128)}, u32[]{:S(2)}) copy-start(f32[256,256]{1,0:T(8,128)} %get-tuple-element.575) | copy-start | bytes 786436
  399.5 12.6 %copy-start.45 = (f32[256,256]{1,0:T(8,128)S(1)}, f32[256,256]{1,0:T(8,128)}, u32[]{:S(2)}) copy-start(f32[256,256]{1,0:T(8,128)} %get-tuple-element.576) | copy-start | bytes 786436
  399.5 13.5 %copy-start.48 = (f32[256,256]{1,0:T(8,128)S(1)}, f32[256,256]{1,0:T(8,128)}, u32[]{:S(2)}) copy-start(f32[256,256]{1,0:T(8,128)} %get-tuple-element.577) | copy-start | bytes 786436
  399.5 14.3 %copy-start.51 = (f32[256,256]{1,0:T(8,128)S(1)}, f32[256,256]{1,0:T(8,128)}, u32[]{:S(2)}) copy-start(f32[256,256]{1,0:T(8,128)} %get-tuple-element.578) | copy-start | bytes 786436
  399.5 15.1 %copy-start.54 = (f32[256,256]{1,0:T(8,128)S(1)}, f32[256,256]{1,0:T(8,128)}, u32[]{:S(2)}) copy-start(f32[256,256]{1,0:T(8,128)} %get-tuple-element.579) | copy-start | bytes 786436
  399.5 16.0 %copy-start.57 = (f32[256,256]{1,0:T(8,128)S(1)}, f32[256,256]{1,0:T(8,128)}, u32[]{:S(2)}) copy-start(f32[256,256]{1,0:T(8,128)} %get-tuple-element.580) | copy-start | bytes 786436
  399.6 16.8 %copy-start.58 = (f32[256,256]{1,0:T(8,128)S(1)}, f32[256,256]{1,0:T(8,128)}, u32[]{:S(2)}) copy-start(f32[256,256]{1,0:T(8,128)} %get-tuple-element.581) | copy-start | bytes 786436
  400.4 16.8 %copy-start.61 = (f32[256,256]{1,0:T(8,128)S(1)}, f32[256,256]{1,0:T(8,128)}, u32[]{:S(2)}) copy-start(f32[256,256]{1,0:T(8,128)} %get-tuple-element.582) | copy-start | bytes 786436
  402.3 15.1 %copy-start.64 = (f32[256,256]{1,0:T(8,128)S(1)}, f32[256,256]{1,0:T(8,128)}, u32[]{:S(2)}) copy-start(f32[256,256]{1,0:T(8,128)} %get-tuple-element.583) | copy-start | bytes 786436
  404.1 13.4 %copy-start.67 = (f32[256,256]{1,0:T(8,128)S(1)}, f32[256,256]{1,0:T(8,128)}, u32[]{:S(2)}) copy-start(f32[256,256]{1,0:T(8,128)} %get-tuple-element.584) | copy-start | bytes 786436
  412.1 9.8 %copy-start.78 = (f32[256,256]{1,0:T(8,128)S(1)}, f32[256,256]{1,0:T(8,128)}, u32[]{:S(2)}) copy-start(f32[256,256]{1,0:T(8,128)} %get-tuple-element.589) | copy-start | bytes 786436
  413.0 9.1 %copy-start.81 = (f32[256,256]{1,0:T(8,128)S(1)}, f32[256,256]{1,0:T(8,128)}, u32[]{:S(2)}) copy-start(f32[256,256]{1,0:T(8,128)} %get-tuple-element.590) | copy-start | bytes 786436
  413.8 8.4 %copy-start.84 = (f32[256,256]{1,0:T(8,128)S(1)}, f32[256,256]{1,0:T(8,128)}, u32[]{:S(2)}) copy-start(f32[256,256]{1,0:T(8,128)} %get-tuple-element.591) | copy-start | bytes 786436
  425.7 12.1 %copy-start.26 = (f32[256,256]{0,1:T(8,128)S(1)}, f32[256,256]{0,1:T(8,128)}, u32[]{:S(2)}) copy-start(f32[256,256]{0,1:T(8,128)} %copy.196) | copy-start | bytes 786436
  425.7 12.8 %copy-start.25 = (f32[256,256]{0,1:T(8,128)S(1)}, f32[256,256]{0,1:T(8,128)}, u32[]{:S(2)}) copy-start(f32[256,256]{0,1:T(8,128)} %copy.197) | copy-start | bytes 786436
  425.7 13.5 %copy-start.24 = (f32[256,256]{0,1:T(8,128)S(1)}, f32[256,256]{0,1:T(8,128)}, u32[]{:S(2)}) copy-start(f32[256,256]{0,1:T(8,128)} %copy.198) | copy-start | bytes 786436
  425.7 14.2 %copy-start.23 = (f32[256,256]{0,1:T(8,128)S(1)}, f32[256,256]{0,1:T(8,128)}, u32[]{:S(2)}) copy-start(f32[256,256]{0,1:T(8,128)} %copy.199) | copy-start | bytes 786436
  425.7 15.0 %copy-start.22 = (f32[256,256]{0,1:T(8,128)S(1)}, f32[256,256]{0,1:T(8,128)}, u32[]{:S(2)}) copy-start(f32[256,256]{0,1:T(8,128)} %copy.200) | copy-start | bytes 786436
  425.7 15.7 %copy-start.21 = (f32[256,256]{0,1:T(8,128)S(1)}, f32[256,256]{0,1:T(8,128)}, u32[]{:S(2)}) copy-start(f32[256,256]{0,1:T(8,128)} %copy.201) | copy-start | bytes 786436
  425.7 16.4 %copy-start.20 = (f32[256,256]{0,1:T(8,128)S(1)}, f32[256,256]{0,1:T(8,128)}, u32[]{:S(2)}) copy-start(f32[256,256]{0,1:T(8,128)} %copy.202) | copy-start | bytes 786436
  452.6 174.0 %reduce-scatter.15.cloned.1.call-start = ((), (), s32[]{:S(2)}) async-start(), calls=%async_computation.9 | async-start | bytes 4423680
  456.2 213.6 %reduce-scatter.13.cloned.1.call-start = ((), (), s32[]{:S(2)}) async-start(), calls=%async_computation.8 | async-start | bytes 4423680
  (216 other events, 263.6 us)
Sparse Core Ops, SparseCore 0:
  17.4 73.2 all-gather.4
  92.9 62.6 all-gather.6
  286.1 131.8 reduce-scatter.10
  452.8 131.9 reduce-scatter.8
  587.1 39.4 reduce-scatter.14
  629.3 40.4 reduce-scatter.12
where the time goes:
time: 682 us; the launch traced here: 679 us
  waiting for transfers between devices  238 us (35%)
  local copies, waits for them, and re-layouts  162 us (24%)
  matrix products  153 us (22%)
  loops' own time  44 us (6%)
  other arithmetic  33.7 us (5%)
  blocking collectives  18.7 us (3%)
  between operations  15.5 us (2%)
  starting transfers between devices  14.3 us (2%)
    reduce_scatter x1, waiting for transfers between devices, reduce_kernels(): lax.psum_scatter(sum_one, 'gy', scatter_dimension=1, tiled=True)  129 us
    dot_general x108, matrix products, block_work(): lax.dot_general(piece_in, center, (((0,), (0,)), ((), ())), preferred_ele...  122 us
    unnamed x8, waiting for transfers between devices  79.6 us
    unnamed x162, local copies, waits for them, and re-layouts  77.6 us
    dot_general x108, matrix products, block_work(): lax.dot_general(piece_grad, tap_rows, (((1,), (1,)), ((), ())), preferred...  30.1 us
    while x27, local copies, waits for them, and re-layouts, body(): lax.scan(first_pass, start, (corner_x, corner_y, corner_z, valid))  30.1 us
    another operation x1, loops' own time, body(): lax.scan(first_pass, start, (corner_x, corner_y, corner_z, valid))  28.6 us
    while x27, local copies, waits for them, and re-layouts, body(): lax.scan(second_pass, start, (corner_x, corner_y, corner_z, valid))  25.9 us
  transfers between devices with their start and end apart: 14, of which 6 were waited for; matrix products, arithmetic and copies ran while one was open for 50% of the time, Pallas kernels for 0%

commit v1 on v0

v1 whole, which is shorter than its diff:
```python
import functools

import jax
import jax.numpy as jnp
from jax import lax
from jax.experimental import pallas as pl
from jax.experimental.pallas import tpu as pltpu
from jax.sharding import PartitionSpec as P

B = 8
AMAX = 2
LANES = 128
BOTH = ("gx", "gy")

stencil_columns = [(shift_x, shift_y) for shift_x in (-1, 0, 1) for shift_y in (-1, 0, 1)]


class Plan:
    def __init__(self, n_gx, n_gy, rows, chans):
        self.n_gx = n_gx
        self.n_gy = n_gy
        self.rows = rows
        self.chans = chans
        self.cols = chans // n_gy
        self.pair = 2 if n_gx % 2 == 0 else 1
        self.inner = 2 if n_gy % 2 == 0 else 1
        self.n_y = n_gx // self.pair
        self.n_z = n_gy // self.inner
        self.n_plane = self.n_y * self.inner
        self.tiles = 27 * chans // LANES
        self.first = [rows * i // LANES for i in range(n_gx)]
        self.offset = [rows * i % LANES for i in range(n_gx)]
        self.depth = max(-(-(self.offset[i] + rows) // LANES) for i in range(n_gx))

    def owners(self, tile):
        return [
            (i, tile - self.first[i])
            for i in range(self.n_gx)
            if tile * LANES < (i + 1) * self.rows and (tile + 1) * LANES > i * self.rows
        ]


def swap(x, plan, flip_gx, flip_gy):
    n_gy = plan.n_gy
    pairs = [
        (i * n_gy + j, (i ^ flip_gx) * n_gy + (j ^ flip_gy))
        for i in range(plan.n_gx)
        for j in range(n_gy)
    ]
    return lax.ppermute(x, BOTH, pairs)


def swap_plane(x, plan, slot):
    return swap(x, plan, slot // plan.inner * plan.pair, slot % plan.inner)


def swap_z(x, plan, slot):
    return swap(x, plan, 0, slot * plan.inner)


def pick_blocks(occ_ref, n_bx, n_by):
    count = jnp.int32(0)
    first = jnp.int32(0)
    second = jnp.int32(0)
    for i in range(n_bx * n_by):
        on = occ_ref[i] > 0
        first = jnp.where(jnp.logical_and(on, count == 0), i, first)
        second = jnp.where(jnp.logical_and(on, count == 1), i, second)
        count = count + on.astype(jnp.int32)
    blocks = []
    for slot, index in enumerate((first, second)):
        blocks.append((index // n_by, index % n_by, (count > slot).astype(jnp.int32)))
    return blocks


def block_mask(occ_ref, block, step_x, step_y, n_bx, n_by):
    bx = block[0] + step_x
    by = block[1] + step_y
    inside = (bx >= 0) & (bx < n_bx) & (by >= 0) & (by < n_by)
    at = jnp.clip(bx, 0, n_bx - 1) * n_by + jnp.clip(by, 0, n_by - 1)
    return jnp.where(inside, occ_ref[at], 1) * block[2]


def load_extended(tile_ref, low_x, high_x, low_y, high_y, ext_ref, sems):
    size_x, size_y = tile_ref.shape[:2]
    copies = [
        pltpu.make_async_copy(
            tile_ref, ext_ref.at[pl.ds(1, size_x), pl.ds(1, size_y)], sems.at[0]
        ),
        pltpu.make_async_copy(low_x, ext_ref.at[0, pl.ds(1, size_y)], sems.at[1]),
        pltpu.make_async_copy(high_x, ext_ref.at[size_x + 1, pl.ds(1, size_y)], sems.at[2]),
        pltpu.make_async_copy(low_y, ext_ref.at[:, 0], sems.at[3]),
        pltpu.make_async_copy(high_y, ext_ref.at[:, size_y + 1], sems.at[4]),
    ]
    for copy in copies:
        copy.start()
    for copy in copies:
        copy.wait()


def spread_patches(occ_ref, blocks, ext_ref, shifted_ref, n_bx, n_by, rectify):
    edge = B
    row = lax.broadcasted_iota(jnp.int32, (edge, ext_ref.shape[-1]), 0)

    def at_x(x, carry):
        step_x = jnp.where(x == 0, -1, jnp.where(x == edge + 1, 1, 0))
        masks = [
            [block_mask(occ_ref, block, step_x, step_y, n_bx, n_by) > 0 for step_y in (-1, 0, 1)]
            for block in blocks
        ]
        for y in range(edge + 2):
            side = 0 if y == 0 else (2 if y == edge + 1 else 1)
            planes = [[], [], []]
            for index, block in enumerate(blocks):
                value = ext_ref[block[0] * edge + x, block[1] * edge + y].astype(jnp.float32)
                if rectify:
                    value = jnp.maximum(value, 0.0)
                value = jnp.where(masks[index][side], value, 0.0)
                below = jnp.where(row == 0, 0.0, pltpu.roll(value, 1, 0))
                above = jnp.where(row == edge - 1, 0.0, pltpu.roll(value, edge - 1, 0))
                for plane, part in zip(planes, (below, value, above)):
                    plane.append(part)
            for j in range(3):
                shifted_ref[j, x, y] = jnp.concatenate(planes[j], axis=0).astype(jnp.bfloat16)
        return carry

    lax.fori_loop(0, edge + 2, at_x, 0)


def gather_blocks(blocks, tile_ref, center_ref):
    edge = B

    def at_x(x, carry):
        for y in range(edge):
            parts = []
            for block in blocks:
                value = tile_ref[block[0] * edge + x, block[1] * edge + y].astype(jnp.float32)
                parts.append(jnp.where(block[2] > 0, value, 0.0))
            center_ref[x, y] = jnp.concatenate(parts, axis=0).astype(jnp.bfloat16)
        return carry

    lax.fori_loop(0, edge, at_x, 0)


def window(shifted_ref, plane, start_x, start_y):
    edge = B
    piece = shifted_ref[plane, start_x : start_x + edge, start_y : start_y + edge]
    return piece.reshape(edge * edge * AMAX * edge, piece.shape[-1])


def weight_kernel(
    plan, n_bx, n_by, rectify, compact,
    occ_ref, pos_ref, tile_ref, low_x, high_x, low_y, high_y, grad_ref,
    out_ref,
    ext_ref, shifted_ref, center_ref, turned_ref, sems,
):
    blocks = pick_blocks(occ_ref, n_bx, n_by)
    load_extended(tile_ref, low_x, high_x, low_y, high_y, ext_ref, sems)
    spread_patches(occ_ref, blocks, ext_ref, shifted_ref, n_bx, n_by, rectify)
    if compact:
        center = grad_ref[...]
    else:
        gather_blocks(blocks, grad_ref, center_ref)
        center = center_ref[...]
    voxels = B * B * AMAX * B
    turned_ref[...] = center.reshape(voxels, plan.chans).astype(jnp.float32).T.astype(jnp.bfloat16)
    my_gx = pos_ref[0]
    my_gy = pos_ref[1]
    my_core = my_gx % plan.pair
    my_y = my_gx // plan.pair
    my_x = my_gy % plan.inner
    my_z = my_gy // plan.inner
    per_column = 3 * plan.chans // LANES
    for column, (shift_x, shift_y) in enumerate(stencil_columns):
        pieces = [window(shifted_ref, j, 1 + shift_x, 1 + shift_y) for j in range(3)]
        product = jnp.dot(
            turned_ref[...],
            jnp.concatenate(pieces, axis=1),
            preferred_element_type=jnp.float32,
        ).astype(jnp.bfloat16)
        for part in range(per_column):
            lanes = product[:, part * LANES : (part + 1) * LANES]
            for shard, place in plan.owners(column * per_column + part):
                core = (shard % plan.pair) ^ my_core
                y = (shard // plan.pair) ^ my_y
                for j in range(plan.n_gy):
                    slot = y * plan.inner + ((j % plan.inner) ^ my_x)
                    z = (j // plan.inner) ^ my_z
                    out_ref[core, slot, z, place] = lanes[j * plan.cols : (j + 1) * plan.cols]


def weight_sums(plan, occ, pos, tile, rim, grad, n_bx, n_by, rectify, compact):
    size_x, size_y, edge, chans = tile.shape
    smem = pl.BlockSpec(memory_space=pltpu.SMEM)
    anywhere = pl.BlockSpec(memory_space=pl.ANY)
    vmem = pl.BlockSpec(memory_space=pltpu.VMEM)
    voxels = B * B * AMAX * B
    shape = (plan.pair, plan.n_plane, plan.n_z, plan.depth, plan.cols, LANES)
    return pl.pallas_call(
        functools.partial(weight_kernel, plan, n_bx, n_by, rectify, compact),
        out_shape=jax.ShapeDtypeStruct(shape, jnp.bfloat16),
        in_specs=[smem, smem] + [anywhere] * 5 + [vmem],
        out_specs=vmem,
        scratch_shapes=[
            pltpu.VMEM((size_x + 2, size_y + 2, edge, chans), jnp.bfloat16),
            pltpu.VMEM((3, B + 2, B + 2, AMAX * B, chans), jnp.bfloat16),
            pltpu.VMEM((B, B, AMAX * B, chans), jnp.bfloat16),
            pltpu.VMEM((chans, voxels), jnp.bfloat16),
            pltpu.SemaphoreType.DMA((5,)),
        ],
        compiler_params=pltpu.CompilerParams(vmem_limit_bytes=40 * 1024 * 1024),
        cost_estimate=pl.CostEstimate(
            flops=2 * 27 * voxels * chans * chans, bytes_accessed=8 << 20, transcendentals=0
        ),
    )(occ, pos, tile, *rim, grad)


def data_kernel(
    plan, n_bx, n_by, gated, n_pieces,
    occ_ref, pos_ref, tile_ref, low_x, high_x, low_y, high_y, *rest,
):
    piece_refs = rest[:n_pieces]
    rest = rest[n_pieces:]
    if gated:
        gate_ref, out_ref, center_ref = rest[:3]
        rest = rest[3:]
    else:
        out_ref = rest[0]
        rest = rest[1:]
    ext_ref, shifted_ref, weight_ref, total_ref, sems, weight_sems = rest
    edge = B
    blocks = pick_blocks(occ_ref, n_bx, n_by)
    my_gx = pos_ref[0]
    my_gy = pos_ref[1]
    copies = []
    for piece in range(n_pieces):
        core = piece // plan.n_plane
        slot = piece % plan.n_plane
        shard = my_gx ^ (slot // plan.inner * plan.pair + core)
        for z in range(plan.n_z):
            column = my_gy ^ (z * plan.inner + slot % plan.inner)
            start = pl.multiple_of(column * plan.cols, plan.cols)
            copies.append(
                pltpu.make_async_copy(
                    piece_refs[piece].at[z],
                    weight_ref.at[shard, pl.ds(start, plan.cols)],
                    weight_sems.at[piece, z],
                )
            )
    for copy in copies:
        copy.start()
    load_extended(tile_ref, low_x, high_x, low_y, high_y, ext_ref, sems)
    spread_patches(occ_ref, blocks, ext_ref, shifted_ref, n_bx, n_by, False)
    out_ref[...] = jnp.zeros_like(out_ref)
    for copy in copies:
        copy.wait()

    def kernel_lanes(tile):
        total = None
        for shard, place in plan.owners(tile):
            part = weight_ref[shard, :, place * LANES : (place + 1) * LANES]
            total = part if total is None else total + part
        return total

    halves = plan.chans // LANES
    for column, (shift_x, shift_y) in enumerate(stencil_columns):
        pieces = [window(shifted_ref, 2 - j, 1 - shift_x, 1 - shift_y) for j in range(3)]
        taps = [
            jnp.concatenate(
                [kernel_lanes((3 * column + j) * halves + part) for part in range(halves)], axis=1
            )
            for j in range(3)
        ]
        product = jnp.dot(
            jnp.concatenate(pieces, axis=1),
            jnp.concatenate(taps, axis=0),
            preferred_element_type=jnp.float32,
        )
        if column == 0:
            total_ref[...] = product
        else:
            total_ref[...] += product

    def at_x(x, carry):
        for y in range(edge):
            kept = []
            for index, block in enumerate(blocks):
                start = pl.multiple_of((x * edge + y) * AMAX * edge, AMAX * edge) + index * edge
                value = total_ref[pl.ds(start, edge), :]
                at = (block[0] * edge + x, block[1] * edge + y)
                if gated:
                    value = jnp.where(gate_ref[at].astype(jnp.float32) > 0, value, 0.0)
                    value = jnp.where(block[2] > 0, value, 0.0)
                    kept.append(value)

                @pl.when(block[2] > 0)
                def _():
                    out_ref[at] = value.astype(jnp.bfloat16)

            if gated:
                center_ref[x, y] = jnp.concatenate(kept, axis=0).astype(jnp.bfloat16)
        return carry

    lax.fori_loop(0, edge, at_x, 0)


def data_grad(plan, occ, pos, tile, rim, pieces, n_bx, n_by, gate=None):
    size_x, size_y, edge, chans = tile.shape
    smem = pl.BlockSpec(memory_space=pltpu.SMEM)
    anywhere = pl.BlockSpec(memory_space=pl.ANY)
    vmem = pl.BlockSpec(memory_space=pltpu.VMEM)
    voxels = B * B * AMAX * B
    gated = gate is not None
    out_shape = [jax.ShapeDtypeStruct(tile.shape, jnp.bfloat16)]
    if gated:
        out_shape.append(jax.ShapeDtypeStruct((B, B, AMAX * B, chans), jnp.bfloat16))
    return pl.pallas_call(
        functools.partial(data_kernel, plan, n_bx, n_by, gated, len(pieces)),
        out_shape=out_shape,
        in_specs=[smem, smem] + [anywhere] * (5 + len(pieces)) + [vmem] * gated,
        out_specs=[vmem] * len(out_shape),
        scratch_shapes=[
            pltpu.VMEM((size_x + 2, size_y + 2, edge, chans), jnp.bfloat16),
            pltpu.VMEM((3, B + 2, B + 2, AMAX * B, chans), jnp.bfloat16),
            pltpu.VMEM((plan.n_gx, chans, plan.depth * LANES), jnp.bfloat16),
            pltpu.VMEM((voxels, chans), jnp.float32),
            pltpu.SemaphoreType.DMA((5,)),
            pltpu.SemaphoreType.DMA((len(pieces), plan.n_z)),
        ],
        compiler_params=pltpu.CompilerParams(vmem_limit_bytes=40 * 1024 * 1024),
        cost_estimate=pl.CostEstimate(
            flops=2 * 27 * voxels * chans * chans, bytes_accessed=8 << 20, transcendentals=0
        ),
    )(occ, pos, tile, *rim, *pieces, *([gate] if gated else []))


def offsets_of(plan):
    return jnp.asarray(plan.offset, jnp.int32)[lax.axis_index("gx")]


def gather_kernel(plan, weight):
    frame = jnp.zeros((plan.cols, plan.depth * LANES), weight.dtype)
    own = lax.dynamic_update_slice(frame, weight.T, (0, offsets_of(plan)))
    line = jnp.stack([own] + [swap_z(own, plan, slot) for slot in range(1, plan.n_z)])
    plane = [line] + [swap_plane(line, plan, slot) for slot in range(1, plan.n_plane)]
    other = [swap(part, plan, 1, 0) for part in plane] if plan.pair == 2 else []
    return plane + other


def reduce_kernel(plan, sums):
    total = [sums[0, slot].astype(jnp.float32) for slot in range(plan.n_plane)]
    if plan.pair == 2:
        got = swap(sums[1], plan, 1, 0)
        total = [total[slot] + got[slot].astype(jnp.float32) for slot in range(plan.n_plane)]
    got = [
        swap_plane(total[slot].astype(jnp.bfloat16), plan, slot)
        for slot in range(1, plan.n_plane)
    ]
    line = total[0]
    for part in got:
        line = line + part.astype(jnp.float32)
    got = [
        swap_z(line[slot].astype(jnp.bfloat16), plan, slot) for slot in range(1, plan.n_z)
    ]
    own = line[0]
    for part in got:
        own = own + part.astype(jnp.float32)
    scale = float(plan.n_gx * plan.n_gy * B**3) ** (-0.5)
    flat = (own * scale).transpose(0, 2, 1).reshape(plan.depth * LANES, plan.cols)
    return lax.dynamic_slice(flat, (offsets_of(plan), 0), (plan.rows, plan.cols))


def ring(axis):
    size = lax.axis_size(axis)
    up = [(i, i + 1) for i in range(size - 1)]
    return up, [(j, i) for i, j in up]


def rims(first_x, last_x, first_y, last_y):
    up, down = ring("gx")
    low_x = lax.ppermute(last_x, "gx", up)
    high_x = lax.ppermute(first_x, "gx", down)
    up, down = ring("gy")
    low_y = lax.ppermute(
        jnp.concatenate([low_x[:, -1:], last_y, high_x[:, -1:]], axis=1), "gy", up
    )
    high_y = lax.ppermute(
        jnp.concatenate([low_x[:, :1], first_y, high_x[:, :1]], axis=1), "gy", down
    )
    return low_x, high_x, low_y, high_y


def body(inputs, preact, out_grad, weight_one, weight_two, occupancy):
    n_bx, n_by = occupancy.shape[:2]
    plan = Plan(
        lax.axis_size("gx"), lax.axis_size("gy"), weight_one.shape[0], inputs.shape[-1]
    )
    occ = occupancy.reshape(-1)
    pos = jnp.stack([lax.axis_index("gx"), lax.axis_index("gy")]).astype(jnp.int32)
    on = occupancy[:, :, 0] > 0
    along_x = jnp.repeat(on, B, axis=0)[..., None, None]
    along_y = jnp.repeat(on, B, axis=1)[..., None, None]
    zero = jnp.zeros((), jnp.bfloat16)
    fields = (jnp.maximum(preact, zero), inputs, out_grad)
    edges = rims(
        jnp.stack([jnp.where(along_y[0], x[0], zero) for x in fields]),
        jnp.stack([jnp.where(along_y[-1], x[-1], zero) for x in fields]),
        jnp.stack([jnp.where(along_x[:, 0], x[:, 0], zero) for x in fields]),
        jnp.stack([jnp.where(along_x[:, -1], x[:, -1], zero) for x in fields]),
    )
    rim_second, rim_first, rim_grad = [tuple(edge[i] for edge in edges) for i in range(3)]
    pieces_two = gather_kernel(plan, weight_two)
    pieces_one = gather_kernel(plan, weight_one)
    sums_two = weight_sums(plan, occ, pos, preact, rim_second, out_grad, n_bx, n_by, True, False)
    grad_one, center = data_grad(
        plan, occ, pos, out_grad, rim_grad, pieces_two, n_bx, n_by, preact
    )
    sums_one = weight_sums(plan, occ, pos, inputs, rim_first, center, n_bx, n_by, False, True)
    edges = rims(
        grad_one[None, 0], grad_one[None, -1], grad_one[None, :, 0], grad_one[None, :, -1]
    )
    rim_one = tuple(edge[0] for edge in edges)
    (input_grad,) = data_grad(plan, occ, pos, grad_one, rim_one, pieces_one, n_bx, n_by)
    return (input_grad, reduce_kernel(plan, sums_one), reduce_kernel(plan, sums_two))


def solution(mesh):
    return jax.shard_map(
        body,
        mesh=mesh,
        in_specs=(
            P("gx", "gy", None, None),
            P("gx", "gy", None, None),
            P("gx", "gy", None, None),
            P("gx", "gy"),
            P("gx", "gy"),
            P("gx", "gy", None),
        ),
        out_specs=(P("gx", "gy", None, None), P("gx", "gy"), P("gx", "gy")),
        check_vma=False,
    )
```

time: 682 us -> 180 us (0.26)
  waiting for transfers between devices: 238 us -> 60.5 us
  local copies, waits for them, and re-layouts: 162 us -> 8.15 us
  matrix products: 153 us -> 0 us
  starting transfers between devices: 14.3 us -> 63 us
  loops' own time: 44 us -> 0 us
  Pallas kernels: 0 us -> 34.4 us
  other arithmetic: 33.7 us -> 10.6 us
  blocking collectives: 18.7 us -> 0 us
  between operations: 15.5 us -> 3.04 us
    dot_general x216 -> x0, matrix products: 153 us -> none  [the longest x108 122 us: block_work(): lax.dot_general(piece_in, center, (((0,), (0,)), ((), ())), preferred_ele...]
    reduce_scatter x2 -> x0, waiting for transfers between devices: 129 us -> none  [the longest x1 129 us: reduce_kernels(): lax.psum_scatter(sum_one, 'gy', scatter_dimension=1, tiled=True)]
    unnamed x8 -> x0, waiting for transfers between devices: 79.6 us -> none
    unnamed x162 -> x9, local copies, waits for them, and re-layouts: 77.6 us -> 0.6 us
    while x486 -> x0, local copies, waits for them, and re-layouts: 61 us -> none  [the longest x27 30.1 us: body(): lax.scan(first_pass, start, (corner_x, corner_y, corner_z, valid))]
    ppermute x8 -> x42, starting transfers between devices: 14.1 us -> 63 us  [the longest x34 49.9 us: swap(): return lax.ppermute(x, BOTH, pairs)]
    ppermute x8 -> x42, waiting for transfers between devices: 12.7 us -> 60.5 us  [the longest x34 29.5 us: swap(): return lax.ppermute(x, BOTH, pairs)]
    another operation x2 -> x0, loops' own time: 44 us -> none  [the longest x1 28.6 us: body(): lax.scan(first_pass, start, (corner_x, corner_y, corner_z, valid))]
  transfers between devices with their start and end apart: 14 -> 42, of which waited for: 6 -> 12; matrix products, arithmetic and copies ran while one was open for 50% -> 8% of each run, Pallas kernels for 0% -> 19%
where the time goes in v1:
time: 180 us
  starting transfers between devices  63 us (35%)
  waiting for transfers between devices  60.5 us (34%)
  Pallas kernels  34.4 us (19%)
  other arithmetic  10.6 us (6%)
  local copies, waits for them, and re-layouts  8.15 us (5%)
  between operations  3.04 us (2%)
    ppermute x34, starting transfers between devices, swap(): return lax.ppermute(x, BOTH, pairs)  49.9 us
    ppermute x34, waiting for transfers between devices, swap(): return lax.ppermute(x, BOTH, pairs)  29.5 us
    pallas_call x2, Pallas kernels, data_grad(): pl.pallas_call(functools.partial(data_kernel, plan, n_bx, n_by, gated, le...  23.5 us
    ppermute x2, waiting for transfers between devices, rims(): lax.ppermute(jnp.concatenate([low_x[:, -1:], last_y, high_x[:, -1:]], axi...  21.2 us
    pallas_call x2, Pallas kernels, weight_sums(): pl.pallas_call(functools.partial(weight_kernel, plan, n_bx, n_by, rectify...  10.9 us
    ppermute x2, waiting for transfers between devices, rims(): lax.ppermute(jnp.concatenate([low_x[:, :1], first_y, high_x[:, :1]], axis...  9.18 us
    ppermute x2, starting transfers between devices, rims(): lax.ppermute(jnp.concatenate([low_x[:, -1:], last_y, high_x[:, -1:]], axi...  4.82 us
  transfers between devices with their start and end apart: 42, of which 12 were waited for; matrix products, arithmetic and copies ran while one was open for 8% of the time, Pallas kernels for 19%

profile of v1, /device:TPU:0, one launch (start us, length us, event | category | flops | bytes accessed | tf_op | source)
XLA Modules:
  0.0 179.6 jit_solution(17638956112083559595)
XLA Ops:
  0.7 1.4 dynamic_slice.18
  4.0 1.5 dynamic_update_slice.6
  5.5 3.1 %collective-permute-start.4 = (bf16[32,1792]{1,0:T(8,128)(2,1)S(1)}, bf16[32,1792]{1,0:T(8,128)(2,1)}, u32[]{:S(2)}, u32[]{:S(2)}) collective-permute-start(bf16[32,1792]{1,0:T(8,128)(2,1)S(1)} %dynamic_update_slice.6), channel_id=1, source_target_pairs={{0,2},{1,3},{2,0},{3,1},{4,6},{5,7},{6,4},{7,5},{8,10},{9,11},{10,... | collective-permute-start | bytes 344072 | tf_op jit(solution)/shard_map/ppermute | solution.py:50
  8.6 2.6 %collective-permute-start.5 = (bf16[32,1792]{1,0:T(8,128)(2,1)S(1)}, bf16[32,1792]{1,0:T(8,128)(2,1)}, u32[]{:S(2)}, u32[]{:S(2)}) collective-permute-start(bf16[32,1792]{1,0:T(8,128)(2,1)S(1)} %dynamic_update_slice.6), channel_id=1, source_target_pairs={{0,4},{1,5},{2,6},{3,7},{4,0},{5,1},{6,2},{7,3},{8,12},{9,13},{10,... | collective-permute-start | bytes 344072 | tf_op jit(solution)/shard_map/ppermute | solution.py:50
  11.2 1.5 dynamic_update_slice.7
  12.7 1.0 collective-permute-start.18
  13.6 3.5 %collective-permute-start.19 = (bf16[32,1792]{1,0:T(8,128)(2,1)S(1)}, bf16[32,1792]{1,0:T(8,128)(2,1)}, u32[]{:S(2)}, u32[]{:S(2)}) collective-permute-start(bf16[32,1792]{1,0:T(8,128)(2,1)S(1)} %dynamic_update_slice.7), channel_id=1, source_target_pairs={{0,4},{1,5},{2,6},{3,7},{4,0},{5,1},{6,2},{7,3},{8,12},{9,13},{10,... | collective-permute-start | bytes 344072 | tf_op jit(solution)/shard_map/ppermute | solution.py:50
  17.1 0.7 broadcast_compare_fusion
  18.4 1.3 copy_maximum_fusion
  19.8 0.8 bitcast_select_fusion.3
  20.6 0.7 pad_maximum_fusion.4
  21.3 0.7 pad_maximum_fusion.5
  22.0 0.6 broadcast.122
  22.6 0.7 reduce.3
  23.5 1.3 collective-permute-start
  24.8 1.3 collective-permute-start.1
  26.1 1.1 pad_maximum_fusion.rest_0_
  27.2 1.6 collective-permute-start.7
  28.8 4.5 %collective-permute-start.8 = (bf16[4,32,1792]{2,1,0:T(8,128)(2,1)S(1)}, bf16[4,32,1792]{2,1,0:T(8,128)(2,1)S(1)}, u32[]{:S(2)}, u32[]{:S(2)}) collective-permute-start(bf16[4,32,1792]{2,1,0:T(8,128)(2,1)S(1)} %pad_maximum_fusion.rest_0_), channel_id=1, source_target_pairs={{0,16},{1,17},{2,18},{3,19},{4,20},{5,21},{6,22},{7,23},{8,24},{9,... | collective-permute-start | bytes 1376264 | tf_op jit(solution)/shard_map/ppermute | solution.py:50
  33.3 0.9 pad_maximum_fusion.3
  34.2 1.3 collective-permute-start.3
  35.5 0.9 pad_maximum_fusion.2
  36.4 8.0 %collective-permute-done.3 = bf16[3,18,8,256]{3,2,1,0:T(8,128)(2,1)S(1)} collective-permute-done((bf16[3,18,8,256]{3,2,1,0:T(8,128)(2,1)S(1)}, bf16[3,18,8,256]{3,2,1,0:T(8,128)(2,1)S(1)}, u32[]{:S(2)}, u32[]{:S(2)}) %collective-permute-start.3) | collective-permute-done | bytes 221216 | tf_op jit(solution)/shard_map/ppermute | solution.py:387
  44.5 1.6 collective-permute-start.2
  46.1 4.4 %collective-permute-done.2 = bf16[3,18,8,256]{3,2,1,0:T(8,128)(2,1)S(1)} collective-permute-done((bf16[3,18,8,256]{3,2,1,0:T(8,128)(2,1)S(1)}, bf16[3,18,8,256]{3,2,1,0:T(8,128)(2,1)S(1)}, u32[]{:S(2)}, u32[]{:S(2)}) %collective-permute-start.2) | collective-permute-done | bytes 221216 | tf_op jit(solution)/shard_map/ppermute | solution.py:384
  50.6 3.9 %collective-permute-start.9 = (bf16[4,32,1792]{2,1,0:T(8,128)(2,1)S(1)}, bf16[4,32,1792]{2,1,0:T(8,128)(2,1)S(1)}, u32[]{:S(2)}, u32[]{:S(2)}) collective-permute-start(bf16[4,32,1792]{2,1,0:T(8,128)(2,1)S(1)} %pad_maximum_fusion.rest_0_), channel_id=1, source_target_pairs={{0,17},{1,16},{2,19},{3,18},{4,21},{5,20},{6,23},{7,22},{8,25},{9,... | collective-permute-start | bytes 1376264 | tf_op jit(solution)/shard_map/ppermute | solution.py:50
  54.5 5.5 %shard_map.124 = bf16[2,4,4,14,32,128]{5,4,3,2,1,0:T(8,128)(2,1)S(1)} custom-call(s32[4]{0:T(128)S(1)} %reshape.131.occ_ref, s32[2]{0:T(128)S(1)} %pad_add_fusion.pos_ref, bf16[16,16,8,256]{3,2,1,0:T(8,128)(2,1)S(1)} %copy-done, bf16[16,8,256]{2,1,0:T(8,128)(2,1)S(1)} %get-tuple-element.46.low_x, bf16[16,8,256]{2,1,0:T(8,128)(2,1)S(1)} %get-tuple-element.43.high_x, ...), custom_call_target="tpu_custom_call" | custom-call | flops 3623878656 | bytes 8388608 | tf_op jit(solution)/shard_map/pallas_call | solution.py:199
  60.1 0.9 collective-permute-start.20
  61.0 0.5 collective-permute-start.11
  61.6 3.6 %collective-permute-done.9.rest_3_ = bf16[4,32,1792]{2,1,0:T(8,128)(2,1)S(1)} collective-permute-done((bf16[4,32,1792]{2,1,0:T(8,128)(2,1)S(1)}, bf16[4,32,1792]{2,1,0:T(8,128)(2,1)S(1)}, u32[]{:S(2)}, u32[]{:S(2)}) %collective-permute-start.9) | collective-permute-done | bytes 458784 | tf_op jit(solution)/shard_map/ppermute | solution.py:50
  65.5 1.3 collective-permute-done.20
  66.8 1.0 pad_maximum_fusion.1.rest_0_
  67.8 1.6 collective-permute-start.21
  69.4 2.0 %collective-permute-start.23 = (bf16[4,32,1792]{2,1,0:T(8,128)(2,1)S(1)}, bf16[4,32,1792]{2,1,0:T(8,128)(2,1)S(1)}, u32[]{:S(2)}, u32[]{:S(2)}) collective-permute-start(bf16[4,32,1792]{2,1,0:T(8,128)(2,1)S(1)} %pad_maximum_fusion.1.rest_0_), channel_id=1, source_target_pairs={{0,17},{1,16},{2,19},{3,18},{4,21},{5,20},{6,23},{7,22},{8,25},{9,... | collective-permute-start | bytes 1376264 | tf_op jit(solution)/shard_map/ppermute | solution.py:50
  71.4 11.3 %shard_map.121 = (bf16[16,16,8,256]{3,2,1,0:T(8,128)(2,1)S(1)}, bf16[8,8,16,256]{3,2,1,0:T(8,128)(2,1)S(1)}) custom-call(s32[4]{0:T(128)S(1)} %reshape.131.occ_ref, s32[2]{0:T(128)S(1)} %pad_add_fusion.pos_ref, bf16[16,16,8,256]{3,2,1,0:T(8,128)(2,1)S(1)} %copy-done.1, bf16[16,8,256]{2,1,0:T(8,128)(2,1)S(1)} %get-tuple-element.48.low_x, ...), custom_call_target="tpu_custom_call" | custom-call | flops 3623878656 | bytes 8388608 | tf_op jit(solution)/shard_map/pallas_call | solution.py:317
  82.7 5.3 %shard_map.123 = bf16[2,4,4,14,32,128]{5,4,3,2,1,0:T(8,128)(2,1)S(1)} custom-call(s32[4]{0:T(128)S(1)} %reshape.131.occ_ref, s32[2]{0:T(128)S(1)} %pad_add_fusion.pos_ref, bf16[16,16,8,256]{3,2,1,0:T(8,128)(2,1)S(1)} %copy-done.2, bf16[16,8,256]{2,1,0:T(8,128)(2,1)S(1)} %get-tuple-element.47.low_x, bf16[16,8,256]{2,1,0:T(8,128)(2,1)S(1)} %get-tuple-element.44.high_x, ...), custom_call_target="tpu_custom_call" | custom-call | flops 3623878656 | bytes 8388608 | tf_op jit(solution)/shard_map/pallas_call | solution.py:199
  88.4 1.6 collective-permute-start.14
  90.0 1.5 collective-permute-start.28
  91.6 1.3 collective-permute-start.15
  92.9 1.9 %collective-permute-start.24 = (bf16[4,32,1792]{2,1,0:T(8,128)(2,1)S(1)}, bf16[4,32,1792]{2,1,0:T(8,128)(2,1)S(1)}, u32[]{:S(2)}, u32[]{:S(2)}) collective-permute-start(bf16[4,32,1792]{2,1,0:T(8,128)(2,1)S(1)} %pad_maximum_fusion.1.rest_0_), channel_id=1, source_target_pairs={{0,8},{1,9},{2,10},{3,11},{4,12},{5,13},{6,14},{7,15},{8,0},{9,1},... | collective-permute-start | bytes 1376264 | tf_op jit(solution)/shard_map/ppermute | solution.py:50
  94.9 0.5 collective-permute-done.15
  95.4 3.6 %collective-permute-start.26 = (bf16[4,32,1792]{2,1,0:T(8,128)(2,1)S(1)}, bf16[4,32,1792]{2,1,0:T(8,128)(2,1)S(1)}, u32[]{:S(2)}, u32[]{:S(2)}) collective-permute-start(bf16[4,32,1792]{2,1,0:T(8,128)(2,1)S(1)} %collective-permute-done.22.rest_2_), channel_id=1, source_target_pairs={{0,8},{1,9},{2,10},{3,11},{4,12},{5,13},{6,14},{7,15},{8,0},{9,1},... | collective-permute-start | bytes 1376264 | tf_op jit(solution)/shard_map/ppermute | solution.py:50
  99.5 1.5 collective-permute-start.17
  101.0 2.7 %collective-permute-start.36 = (bf16[4,14,32,128]{3,2,1,0:T(8,128)(2,1)S(1)}, bf16[4,14,32,128]{3,2,1,0:T(8,128)(2,1)S(1)}, u32[]{:S(2)}, u32[]{:S(2)}) collective-permute-start(bf16[4,14,32,128]{3,2,1,0:T(8,128)(2,1)S(1)} %get-tuple-element.11), channel_id=1, source_target_pairs={{0,1},{1,0},{2,3},{3,2},{4,5},{5,4},{6,7},{7,6},{8,9},{9,8},{10,11... | collective-permute-start | bytes 1376264 | tf_op jit(solution)/shard_map/ppermute | solution.py:50
  104.1 1.2 collective-permute-start.38
  105.3 1.1 collective-permute-done.17
  106.4 3.2 %collective-permute-start.16 = (bf16[1,18,8,256]{3,2,1,0:T(8,128)(2,1)S(1)}, bf16[1,18,8,256]{3,2,1,0:T(8,128)(2,1)S(1)}, u32[]{:S(2)}, u32[]{:S(2)}) collective-permute-start(bf16[1,18,8,256]{3,2,1,0:T(8,128)(2,1)S(1)} %pad_maximum_fusion.6), channel_id=1, source_target_pairs={{0,1},{1,2},{2,3},{3,4},{4,5},{5,6},{6,7},{8,9},{9,10},{10,11},{11... | collective-permute-start | bytes 221192 | tf_op jit(solution)/shard_map/ppermute | solution.py:384
  109.6 16.8 %collective-permute-done.16 = bf16[1,18,8,256]{3,2,1,0:T(8,128)(2,1)S(1)} collective-permute-done((bf16[1,18,8,256]{3,2,1,0:T(8,128)(2,1)S(1)}, bf16[1,18,8,256]{3,2,1,0:T(8,128)(2,1)S(1)}, u32[]{:S(2)}, u32[]{:S(2)}) %collective-permute-start.16) | collective-permute-done | bytes 73760 | tf_op jit(solution)/shard_map/ppermute | solution.py:384
  126.4 12.2 %shard_map.122 = bf16[16,16,8,256]{3,2,1,0:T(8,128)(2,1)} custom-call(s32[4]{0:T(128)S(1)} %reshape.131.occ_ref, s32[2]{0:T(128)S(1)} %pad_add_fusion.pos_ref, bf16[16,16,8,256]{3,2,1,0:T(8,128)(2,1)S(1)} %get-tuple-element.5.tile_ref, bf16[16,8,256]{2,1,0:T(8,128)(2,1)S(1)} %bitcast.238, bf16[16,8,256]{2,1,0:T(8,128)(2,1)S(1)} %bitcast.239, ...), custom_call_target="tpu_custom_call" | custom-call | flops 3623878656 | bytes 8388608 | tf_op jit(solution)/shard_map/pallas_call | solution.py:317
  139.0 2.1 %collective-permute-start.39 = (bf16[14,32,128]{2,1,0:T(8,128)(2,1)S(1)}, bf16[14,32,128]{2,1,0:T(8,128)(2,1)S(1)}, u32[]{:S(2)}, u32[]{:S(2)}) collective-permute-start(bf16[14,32,128]{2,1,0:T(8,128)(2,1)S(1)} %get-tuple-element.31), channel_id=1, source_target_pairs={{0,2},{1,3},{2,0},{3,1},{4,6},{5,7},{6,4},{7,5},{8,10},{9,11},{10,... | collective-permute-start | bytes 344072 | tf_op jit(solution)/shard_map/ppermute | solution.py:50
  141.0 1.4 collective-permute-start.40
  142.5 1.4 collective-permute-start.41
  144.3 2.6 %collective-permute-start.29 = (bf16[4,14,32,128]{3,2,1,0:T(8,128)(2,1)S(1)}, bf16[4,14,32,128]{3,2,1,0:T(8,128)(2,1)S(1)}, u32[]{:S(2)}, u32[]{:S(2)}) collective-permute-start(bf16[4,14,32,128]{3,2,1,0:T(8,128)(2,1)S(1)} %get-tuple-element.14), channel_id=1, source_target_pairs={{0,1},{1,0},{2,3},{3,2},{4,5},{5,4},{6,7},{7,6},{8,9},{9,8},{10,11... | collective-permute-start | bytes 1376264 | tf_op jit(solution)/shard_map/ppermute | solution.py:50
  146.8 1.5 collective-permute-start.31
  148.4 4.3 %collective-permute-done.40 = bf16[14,32,128]{2,1,0:T(8,128)(2,1)S(1)} collective-permute-done((bf16[14,32,128]{2,1,0:T(8,128)(2,1)S(1)}, bf16[14,32,128]{2,1,0:T(8,128)(2,1)S(1)}, u32[]{:S(2)}, u32[]{:S(2)}) %collective-permute-start.40) | collective-permute-done | bytes 114720 | tf_op jit(solution)/shard_map/ppermute | solution.py:50
  152.8 5.5 %collective-permute-done.29 = bf16[4,14,32,128]{3,2,1,0:T(8,128)(2,1)S(1)} collective-permute-done((bf16[4,14,32,128]{3,2,1,0:T(8,128)(2,1)S(1)}, bf16[4,14,32,128]{3,2,1,0:T(8,128)(2,1)S(1)}, u32[]{:S(2)}, u32[]{:S(2)}) %collective-permute-start.29) | collective-permute-done | bytes 458784 | tf_op jit(solution)/shard_map/ppermute | solution.py:50
  158.3 9.7 %collective-permute-done.30 = bf16[4,14,32,128]{3,2,1,0:T(8,128)(2,1)S(1)} collective-permute-done((bf16[4,14,32,128]{3,2,1,0:T(8,128)(2,1)S(1)}, bf16[4,14,32,128]{3,2,1,0:T(8,128)(2,1)S(1)}, u32[]{:S(2)}, u32[]{:S(2)}) %collective-permute-start.30) | collective-permute-done | bytes 458784 | tf_op jit(solution)/shard_map/ppermute | solution.py:50
  168.3 0.8 collective-permute-start.32
  169.1 2.1 %collective-permute-start.33 = (bf16[14,32,128]{2,1,0:T(8,128)(2,1)S(1)}, bf16[14,32,128]{2,1,0:T(8,128)(2,1)S(1)}, u32[]{:S(2)}, u32[]{:S(2)}) collective-permute-start(bf16[14,32,128]{2,1,0:T(8,128)(2,1)S(1)} %get-tuple-element.36), channel_id=1, source_target_pairs={{0,4},{1,5},{2,6},{3,7},{4,0},{5,1},{6,2},{7,3},{8,12},{9,13},{10,... | collective-permute-start | bytes 344072 | tf_op jit(solution)/shard_map/ppermute | solution.py:50
  171.3 1.5 collective-permute-start.34
  172.8 0.8 constant_dynamic-slice_fusion.1
  173.6 1.9 %collective-permute-done.32 = bf16[14,32,128]{2,1,0:T(8,128)(2,1)S(1)} collective-permute-done((bf16[14,32,128]{2,1,0:T(8,128)(2,1)S(1)}, bf16[14,32,128]{2,1,0:T(8,128)(2,1)S(1)}, u32[]{:S(2)}, u32[]{:S(2)}) %collective-permute-start.32) | collective-permute-done | bytes 114720 | tf_op jit(solution)/shard_map/ppermute | solution.py:50
  175.4 3.3 %collective-permute-done.33 = bf16[14,32,128]{2,1,0:T(8,128)(2,1)S(1)} collective-permute-done((bf16[14,32,128]{2,1,0:T(8,128)(2,1)S(1)}, bf16[14,32,128]{2,1,0:T(8,128)(2,1)S(1)}, u32[]{:S(2)}, u32[]{:S(2)}) %collective-permute-start.33) | collective-permute-done | bytes 114720 | tf_op jit(solution)/shard_map/ppermute | solution.py:50
  178.8 0.8 constant_dynamic-slice_fusion
  (84 shorter events, 4.0 us)
Async XLA Ops:
  0.6 19.1 %copy-start.2 = (bf16[16,16,8,256]{3,2,1,0:T(8,128)(2,1)S(1)}, bf16[16,16,8,256]{3,2,1,0:T(8,128)(2,1)}, u32[]{:S(2)}) copy-start(bf16[16,16,8,256]{3,2,1,0:T(8,128)(2,1)} %tile_ref.4) | copy-start | bytes 3145732
  0.6 19.2 %copy-start.1 = (bf16[16,16,8,256]{3,2,1,0:T(8,128)(2,1)S(1)}, bf16[16,16,8,256]{3,2,1,0:T(8,128)(2,1)}, u32[]{:S(2)}) copy-start(bf16[16,16,8,256]{3,2,1,0:T(8,128)(2,1)} %grad_ref.1) | copy-start | bytes 3145732
  5.5 18.0 %collective-permute-start.4 = (bf16[32,1792]{1,0:T(8,128)(2,1)S(1)}, bf16[32,1792]{1,0:T(8,128)(2,1)}, u32[]{:S(2)}, u32[]{:S(2)}) collective-permute-start(bf16[32,1792]{1,0:T(8,128)(2,1)S(1)} %dynamic_update_slice.6), channel_id=1, source_target_pairs={{0,2},{1,3},{2,0},{3,1},{4,6},{5,7},{6,4},{7,5},{8,10},{9,11},{10,... | collective-permute-start | bytes 344072 | tf_op jit(solution)/shard_map/ppermute | solution.py:50
  8.6 16.2 %collective-permute-start.5 = (bf16[32,1792]{1,0:T(8,128)(2,1)S(1)}, bf16[32,1792]{1,0:T(8,128)(2,1)}, u32[]{:S(2)}, u32[]{:S(2)}) collective-permute-start(bf16[32,1792]{1,0:T(8,128)(2,1)S(1)} %dynamic_update_slice.6), channel_id=1, source_target_pairs={{0,4},{1,5},{2,6},{3,7},{4,0},{5,1},{6,2},{7,3},{8,12},{9,13},{10,... | collective-permute-start | bytes 344072 | tf_op jit(solution)/shard_map/ppermute | solution.py:50
  11.2 15.0 %collective-permute-start.6 = (bf16[32,1792]{1,0:T(8,128)(2,1)S(1)}, bf16[32,1792]{1,0:T(8,128)(2,1)}, u32[]{:S(2)}, u32[]{:S(2)}) collective-permute-start(bf16[32,1792]{1,0:T(8,128)(2,1)S(1)} %dynamic_update_slice.6), channel_id=1, source_target_pairs={{0,6},{1,7},{2,4},{3,5},{4,2},{5,3},{6,0},{7,1},{8,14},{9,15},{10,... | collective-permute-start | bytes 344072 | tf_op jit(solution)/shard_map/ppermute | solution.py:50
  12.7 47.4 %collective-permute-start.18 = (bf16[32,1792]{1,0:T(8,128)(2,1)S(1)}, bf16[32,1792]{1,0:T(8,128)(2,1)}, u32[]{:S(2)}, u32[]{:S(2)}) collective-permute-start(bf16[32,1792]{1,0:T(8,128)(2,1)S(1)} %dynamic_update_slice.7), channel_id=1, source_target_pairs={{0,2},{1,3},{2,0},{3,1},{4,6},{5,7},{6,4},{7,5},{8,10},{9,11},{10,... | collective-permute-start | bytes 344072 | tf_op jit(solution)/shard_map/ppermute | solution.py:50
  13.6 47.4 %collective-permute-start.19 = (bf16[32,1792]{1,0:T(8,128)(2,1)S(1)}, bf16[32,1792]{1,0:T(8,128)(2,1)}, u32[]{:S(2)}, u32[]{:S(2)}) collective-permute-start(bf16[32,1792]{1,0:T(8,128)(2,1)S(1)} %dynamic_update_slice.7), channel_id=1, source_target_pairs={{0,4},{1,5},{2,6},{3,7},{4,0},{5,1},{6,2},{7,3},{8,12},{9,13},{10,... | collective-permute-start | bytes 344072 | tf_op jit(solution)/shard_map/ppermute | solution.py:50
  18.4 4.2 %copy-start.3 = (s32[2,2,1]{1,2,0:T(1,128)S(1)}, s32[2,2,1]{1,2,0:T(1,128)}, u32[]{:S(2)}) copy-start(s32[2,2,1]{1,2,0:T(1,128)} %param.15) | copy-start | bytes 52
  22.0 32.5 %copy-start = (bf16[16,16,8,256]{3,2,1,0:T(8,128)(2,1)S(1)}, bf16[16,16,8,256]{3,2,1,0:T(8,128)(2,1)}, u32[]{:S(2)}) copy-start(bf16[16,16,8,256]{3,2,1,0:T(8,128)(2,1)} %tile_ref.5) | copy-start | bytes 3145732
  23.5 5.3 %collective-permute-start = (bf16[3,16,8,256]{3,2,1,0:T(8,128)(2,1)}, bf16[3,16,8,256]{3,2,1,0:T(8,128)(2,1)S(1)}, u32[]{:S(2)}, u32[]{:S(2)}) collective-permute-start(bf16[3,16,8,256]{3,2,1,0:T(8,128)(2,1)} %pad_maximum_fusion.4), channel_id=1, source_target_pairs={{0,8},{8,16},{16,24},{1,9},{9,17},{17,25},{2,10},{10,18},{18,26},{... | collective-permute-start | bytes 589832 | tf_op jit(solution)/shard_map/ppermute | solution.py:381
  24.8 8.4 %collective-permute-start.1 = (bf16[3,16,8,256]{3,2,1,0:T(8,128)(2,1)}, bf16[3,16,8,256]{3,2,1,0:T(8,128)(2,1)S(1)}, u32[]{:S(2)}, u32[]{:S(2)}) collective-permute-start(bf16[3,16,8,256]{3,2,1,0:T(8,128)(2,1)} %pad_maximum_fusion.5), channel_id=1, source_target_pairs={{8,0},{16,8},{24,16},{9,1},{17,9},{25,17},{10,2},{18,10},{26,18},{... | collective-permute-start | bytes 589832 | tf_op jit(solution)/shard_map/ppermute | solution.py:382
  27.2 33.8 %collective-permute-start.7 = (bf16[4,32,1792]{2,1,0:T(8,128)(2,1)S(1)}, bf16[4,32,1792]{2,1,0:T(8,128)(2,1)S(1)}, u32[]{:S(2)}, u32[]{:S(2)}) collective-permute-start(bf16[4,32,1792]{2,1,0:T(8,128)(2,1)S(1)} %pad_maximum_fusion.rest_0_), channel_id=1, source_target_pairs={{0,1},{1,0},{2,3},{3,2},{4,5},{5,4},{6,7},{7,6},{8,9},{9,8},{10,11... | collective-permute-start | bytes 1376264 | tf_op jit(solution)/shard_map/ppermute | solution.py:50
  28.8 32.7 %collective-permute-start.8 = (bf16[4,32,1792]{2,1,0:T(8,128)(2,1)S(1)}, bf16[4,32,1792]{2,1,0:T(8,128)(2,1)S(1)}, u32[]{:S(2)}, u32[]{:S(2)}) collective-permute-start(bf16[4,32,1792]{2,1,0:T(8,128)(2,1)S(1)} %pad_maximum_fusion.rest_0_), channel_id=1, source_target_pairs={{0,16},{1,17},{2,18},{3,19},{4,20},{5,21},{6,22},{7,23},{8,24},{9,... | collective-permute-start | bytes 1376264 | tf_op jit(solution)/shard_map/ppermute | solution.py:50
  34.2 10.3 %collective-permute-start.3 = (bf16[3,18,8,256]{3,2,1,0:T(8,128)(2,1)S(1)}, bf16[3,18,8,256]{3,2,1,0:T(8,128)(2,1)S(1)}, u32[]{:S(2)}, u32[]{:S(2)}) collective-permute-start(bf16[3,18,8,256]{3,2,1,0:T(8,128)(2,1)S(1)} %pad_maximum_fusion.3), channel_id=1, source_target_pairs={{1,0},{2,1},{3,2},{4,3},{5,4},{6,5},{7,6},{9,8},{10,9},{11,10},{12... | collective-permute-start | bytes 663560 | tf_op jit(solution)/shard_map/ppermute | solution.py:387
  44.5 6.1 %collective-permute-start.2 = (bf16[3,18,8,256]{3,2,1,0:T(8,128)(2,1)S(1)}, bf16[3,18,8,256]{3,2,1,0:T(8,128)(2,1)S(1)}, u32[]{:S(2)}, u32[]{:S(2)}) collective-permute-start(bf16[3,18,8,256]{3,2,1,0:T(8,128)(2,1)S(1)} %pad_maximum_fusion.2), channel_id=1, source_target_pairs={{0,1},{1,2},{2,3},{3,4},{4,5},{5,6},{6,7},{8,9},{9,10},{10,11},{11... | collective-permute-start | bytes 663560 | tf_op jit(solution)/shard_map/ppermute | solution.py:384
  50.6 14.6 %collective-permute-start.9 = (bf16[4,32,1792]{2,1,0:T(8,128)(2,1)S(1)}, bf16[4,32,1792]{2,1,0:T(8,128)(2,1)S(1)}, u32[]{:S(2)}, u32[]{:S(2)}) collective-permute-start(bf16[4,32,1792]{2,1,0:T(8,128)(2,1)S(1)} %pad_maximum_fusion.rest_0_), channel_id=1, source_target_pairs={{0,17},{1,16},{2,19},{3,18},{4,21},{5,20},{6,23},{7,22},{8,25},{9,... | collective-permute-start | bytes 1376264 | tf_op jit(solution)/shard_map/ppermute | solution.py:50
  60.1 6.7 %collective-permute-start.20 = (bf16[32,1792]{1,0:T(8,128)(2,1)S(1)}, bf16[32,1792]{1,0:T(8,128)(2,1)S(1)}, u32[]{:S(2)}, u32[]{:S(2)}) collective-permute-start(bf16[32,1792]{1,0:T(8,128)(2,1)S(1)} %dynamic_update_slice.7), channel_id=1, source_target_pairs={{0,6},{1,7},{2,4},{3,5},{4,2},{5,3},{6,0},{7,1},{8,14},{9,15},{10,... | collective-permute-start | bytes 344072 | tf_op jit(solution)/shard_map/ppermute | solution.py:50
  61.0 6.8 %collective-permute-start.10 = (bf16[4,32,1792]{2,1,0:T(8,128)(2,1)S(1)}, bf16[4,32,1792]{2,1,0:T(8,128)(2,1)S(1)}, u32[]{:S(2)}, u32[]{:S(2)}) collective-permute-start(bf16[4,32,1792]{2,1,0:T(8,128)(2,1)S(1)} %pad_maximum_fusion.rest_0_), channel_id=1, source_target_pairs={{0,8},{1,9},{2,10},{3,11},{4,12},{5,13},{6,14},{7,15},{8,0},{9,1},... | collective-permute-start | bytes 1376264 | tf_op jit(solution)/shard_map/ppermute | solution.py:50
  61.0 8.4 %collective-permute-start.11 = (bf16[4,32,1792]{2,1,0:T(8,128)(2,1)S(1)}, bf16[4,32,1792]{2,1,0:T(8,128)(2,1)S(1)}, u32[]{:S(2)}, u32[]{:S(2)}) collective-permute-start(bf16[4,32,1792]{2,1,0:T(8,128)(2,1)S(1)} %collective-permute-done.7.rest_1_), channel_id=1, source_target_pairs={{0,8},{1,9},{2,10},{3,11},{4,12},{5,13},{6,14},{7,15},{8,0},{9,1},... | collective-permute-start | bytes 1376264 | tf_op jit(solution)/shard_map/ppermute | solution.py:50
  61.5 7.9 %collective-permute-start.12 = (bf16[4,32,1792]{2,1,0:T(8,128)(2,1)S(1)}, bf16[4,32,1792]{2,1,0:T(8,128)(2,1)S(1)}, u32[]{:S(2)}, u32[]{:S(2)}) collective-permute-start(bf16[4,32,1792]{2,1,0:T(8,128)(2,1)S(1)} %collective-permute-done.8.rest_2_), channel_id=1, source_target_pairs={{0,8},{1,9},{2,10},{3,11},{4,12},{5,13},{6,14},{7,15},{8,0},{9,1},... | collective-permute-start | bytes 1376264 | tf_op jit(solution)/shard_map/ppermute | solution.py:50
  65.2 6.2 %collective-permute-start.13 = (bf16[4,32,1792]{2,1,0:T(8,128)(2,1)S(1)}, bf16[4,32,1792]{2,1,0:T(8,128)(2,1)S(1)}, u32[]{:S(2)}, u32[]{:S(2)}) collective-permute-start(bf16[4,32,1792]{2,1,0:T(8,128)(2,1)S(1)} %collective-permute-done.9.rest_3_), channel_id=1, source_target_pairs={{0,8},{1,9},{2,10},{3,11},{4,12},{5,13},{6,14},{7,15},{8,0},{9,1},... | collective-permute-start | bytes 1376264 | tf_op jit(solution)/shard_map/ppermute | solution.py:50
  66.8 32.2 %collective-permute-start.35 = (bf16[4,4,14,32,128]{4,3,2,1,0:T(8,128)(2,1)S(1)}, bf16[4,4,14,32,128]{4,3,2,1,0:T(8,128)(2,1)S(1)}, u32[]{:S(2)}, u32[]{:S(2)}) collective-permute-start(bf16[4,4,14,32,128]{4,3,2,1,0:T(8,128)(2,1)S(1)} %slice_bitcast_fusion), channel_id=1, source_target_pairs={{0,8},{1,9},{2,10},{3,11},{4,12},{5,13},{6,14},{7,15},{8,0},{9,1},... | collective-permute-start | bytes 5505032 | tf_op jit(solution)/shard_map/ppermute | solution.py:50
  67.8 22.2 %collective-permute-start.21 = (bf16[4,32,1792]{2,1,0:T(8,128)(2,1)S(1)}, bf16[4,32,1792]{2,1,0:T(8,128)(2,1)S(1)}, u32[]{:S(2)}, u32[]{:S(2)}) collective-permute-start(bf16[4,32,1792]{2,1,0:T(8,128)(2,1)S(1)} %pad_maximum_fusion.1.rest_0_), channel_id=1, source_target_pairs={{0,1},{1,0},{2,3},{3,2},{4,5},{5,4},{6,7},{7,6},{8,9},{9,8},{10,11... | collective-permute-start | bytes 1376264 | tf_op jit(solution)/shard_map/ppermute | solution.py:50
  69.4 23.5 %collective-permute-start.22 = (bf16[4,32,1792]{2,1,0:T(8,128)(2,1)S(1)}, bf16[4,32,1792]{2,1,0:T(8,128)(2,1)S(1)}, u32[]{:S(2)}, u32[]{:S(2)}) collective-permute-start(bf16[4,32,1792]{2,1,0:T(8,128)(2,1)S(1)} %pad_maximum_fusion.1.rest_0_), channel_id=1, source_target_pairs={{0,16},{1,17},{2,18},{3,19},{4,20},{5,21},{6,22},{7,23},{8,24},{9,... | collective-permute-start | bytes 1376264 | tf_op jit(solution)/shard_map/ppermute | solution.py:50
  69.4 25.4 %collective-permute-start.23 = (bf16[4,32,1792]{2,1,0:T(8,128)(2,1)S(1)}, bf16[4,32,1792]{2,1,0:T(8,128)(2,1)S(1)}, u32[]{:S(2)}, u32[]{:S(2)}) collective-permute-start(bf16[4,32,1792]{2,1,0:T(8,128)(2,1)S(1)} %pad_maximum_fusion.1.rest_0_), channel_id=1, source_target_pairs={{0,17},{1,16},{2,19},{3,18},{4,21},{5,20},{6,23},{7,22},{8,25},{9,... | collective-permute-start | bytes 1376264 | tf_op jit(solution)/shard_map/ppermute | solution.py:50
  88.4 3.1 %collective-permute-start.14 = (bf16[1,16,8,256]{3,2,1,0:T(8,128)(2,1)S(1)}, bf16[1,16,8,256]{3,2,1,0:T(8,128)(2,1)S(1)}, u32[]{:S(2)}, u32[]{:S(2)}) collective-permute-start(bf16[1,16,8,256]{3,2,1,0:T(8,128)(2,1)S(1)} %get-tuple-element.20), channel_id=1, source_target_pairs={{0,8},{8,16},{16,24},{1,9},{9,17},{17,25},{2,10},{10,18},{18,26},{... | collective-permute-start | bytes 196616 | tf_op jit(solution)/shard_map/ppermute | solution.py:381
  90.0 53.8 %collective-permute-start.28 = (bf16[4,4,14,32,128]{4,3,2,1,0:T(8,128)(2,1)S(1)}, bf16[4,4,14,32,128]{4,3,2,1,0:T(8,128)(2,1)S(1)}, u32[]{:S(2)}, u32[]{:S(2)}) collective-permute-start(bf16[4,4,14,32,128]{4,3,2,1,0:T(8,128)(2,1)S(1)} %slice_bitcast_fusion.1), channel_id=1, source_target_pairs={{0,8},{1,9},{2,10},{3,11},{4,12},{5,13},{6,14},{7,15},{8,0},{9,1},... | collective-permute-start | bytes 5505032 | tf_op jit(solution)/shard_map/ppermute | solution.py:50
  91.6 3.9 %collective-permute-start.15 = (bf16[1,16,8,256]{3,2,1,0:T(8,128)(2,1)S(1)}, bf16[1,16,8,256]{3,2,1,0:T(8,128)(2,1)S(1)}, u32[]{:S(2)}, u32[]{:S(2)}) collective-permute-start(bf16[1,16,8,256]{3,2,1,0:T(8,128)(2,1)S(1)} %get-tuple-element.19), channel_id=1, source_target_pairs={{8,0},{16,8},{24,16},{9,1},{17,9},{25,17},{10,2},{18,10},{26,18},{... | collective-permute-start | bytes 196616 | tf_op jit(solution)/shard_map/ppermute | solution.py:382
  92.9 6.6 %collective-permute-start.24 = (bf16[4,32,1792]{2,1,0:T(8,128)(2,1)S(1)}, bf16[4,32,1792]{2,1,0:T(8,128)(2,1)S(1)}, u32[]{:S(2)}, u32[]{:S(2)}) collective-permute-start(bf16[4,32,1792]{2,1,0:T(8,128)(2,1)S(1)} %pad_maximum_fusion.1.rest_0_), channel_id=1, source_target_pairs={{0,8},{1,9},{2,10},{3,11},{4,12},{5,13},{6,14},{7,15},{8,0},{9,1},... | collective-permute-start | bytes 1376264 | tf_op jit(solution)/shard_map/ppermute | solution.py:50
  94.8 6.2 %collective-permute-start.25 = (bf16[4,32,1792]{2,1,0:T(8,128)(2,1)S(1)}, bf16[4,32,1792]{2,1,0:T(8,128)(2,1)S(1)}, u32[]{:S(2)}, u32[]{:S(2)}) collective-permute-start(bf16[4,32,1792]{2,1,0:T(8,128)(2,1)S(1)} %collective-permute-done.21.rest_1_), channel_id=1, source_target_pairs={{0,8},{1,9},{2,10},{3,11},{4,12},{5,13},{6,14},{7,15},{8,0},{9,1},... | collective-permute-start | bytes 1376264 | tf_op jit(solution)/shard_map/ppermute | solution.py:50
  95.4 8.3 %collective-permute-start.26 = (bf16[4,32,1792]{2,1,0:T(8,128)(2,1)S(1)}, bf16[4,32,1792]{2,1,0:T(8,128)(2,1)S(1)}, u32[]{:S(2)}, u32[]{:S(2)}) collective-permute-start(bf16[4,32,1792]{2,1,0:T(8,128)(2,1)S(1)} %collective-permute-done.22.rest_2_), channel_id=1, source_target_pairs={{0,8},{1,9},{2,10},{3,11},{4,12},{5,13},{6,14},{7,15},{8,0},{9,1},... | collective-permute-start | bytes 1376264 | tf_op jit(solution)/shard_map/ppermute | solution.py:50
  99.0 5.1 %collective-permute-start.27 = (bf16[4,32,1792]{2,1,0:T(8,128)(2,1)S(1)}, bf16[4,32,1792]{2,1,0:T(8,128)(2,1)S(1)}, u32[]{:S(2)}, u32[]{:S(2)}) collective-permute-start(bf16[4,32,1792]{2,1,0:T(8,128)(2,1)S(1)} %collective-permute-done.23.rest_3_), channel_id=1, source_target_pairs={{0,8},{1,9},{2,10},{3,11},{4,12},{5,13},{6,14},{7,15},{8,0},{9,1},... | collective-permute-start | bytes 1376264 | tf_op jit(solution)/shard_map/ppermute | solution.py:50
  99.5 7.0 %collective-permute-start.17 = (bf16[1,18,8,256]{3,2,1,0:T(8,128)(2,1)S(1)}, bf16[1,18,8,256]{3,2,1,0:T(8,128)(2,1)S(1)}, u32[]{:S(2)}, u32[]{:S(2)}) collective-permute-start(bf16[1,18,8,256]{3,2,1,0:T(8,128)(2,1)S(1)} %pad_maximum_fusion.7), channel_id=1, source_target_pairs={{1,0},{2,1},{3,2},{4,3},{5,4},{6,5},{7,6},{9,8},{10,9},{11,10},{12... | collective-permute-start | bytes 221192 | tf_op jit(solution)/shard_map/ppermute | solution.py:387
  101.0 37.6 %collective-permute-start.36 = (bf16[4,14,32,128]{3,2,1,0:T(8,128)(2,1)S(1)}, bf16[4,14,32,128]{3,2,1,0:T(8,128)(2,1)S(1)}, u32[]{:S(2)}, u32[]{:S(2)}) collective-permute-start(bf16[4,14,32,128]{3,2,1,0:T(8,128)(2,1)S(1)} %get-tuple-element.11), channel_id=1, source_target_pairs={{0,1},{1,0},{2,3},{3,2},{4,5},{5,4},{6,7},{7,6},{8,9},{9,8},{10,11... | collective-permute-start | bytes 1376264 | tf_op jit(solution)/shard_map/ppermute | solution.py:50
  103.7 34.9 %collective-permute-start.37 = (bf16[4,14,32,128]{3,2,1,0:T(8,128)(2,1)S(1)}, bf16[4,14,32,128]{3,2,1,0:T(8,128)(2,1)S(1)}, u32[]{:S(2)}, u32[]{:S(2)}) collective-permute-start(bf16[4,14,32,128]{3,2,1,0:T(8,128)(2,1)S(1)} %get-tuple-element.13), channel_id=1, source_target_pairs={{0,16},{1,17},{2,18},{3,19},{4,20},{5,21},{6,22},{7,23},{8,24},{9,... | collective-permute-start | bytes 1376264 | tf_op jit(solution)/shard_map/ppermute | solution.py:50
  104.1 34.5 %collective-permute-start.38 = (bf16[4,14,32,128]{3,2,1,0:T(8,128)(2,1)S(1)}, bf16[4,14,32,128]{3,2,1,0:T(8,128)(2,1)S(1)}, u32[]{:S(2)}, u32[]{:S(2)}) collective-permute-start(bf16[4,14,32,128]{3,2,1,0:T(8,128)(2,1)S(1)} %get-tuple-element.12), channel_id=1, source_target_pairs={{0,17},{1,16},{2,19},{3,18},{4,21},{5,20},{6,23},{7,22},{8,25},{9,... | collective-permute-start | bytes 1376264 | tf_op jit(solution)/shard_map/ppermute | solution.py:50
  106.4 19.9 %collective-permute-start.16 = (bf16[1,18,8,256]{3,2,1,0:T(8,128)(2,1)S(1)}, bf16[1,18,8,256]{3,2,1,0:T(8,128)(2,1)S(1)}, u32[]{:S(2)}, u32[]{:S(2)}) collective-permute-start(bf16[1,18,8,256]{3,2,1,0:T(8,128)(2,1)S(1)} %pad_maximum_fusion.6), channel_id=1, source_target_pairs={{0,1},{1,2},{2,3},{3,4},{4,5},{5,6},{6,7},{8,9},{9,10},{10,11},{11... | collective-permute-start | bytes 221192 | tf_op jit(solution)/shard_map/ppermute | solution.py:384
  139.0 7.9 %collective-permute-start.39 = (bf16[14,32,128]{2,1,0:T(8,128)(2,1)S(1)}, bf16[14,32,128]{2,1,0:T(8,128)(2,1)S(1)}, u32[]{:S(2)}, u32[]{:S(2)}) collective-permute-start(bf16[14,32,128]{2,1,0:T(8,128)(2,1)S(1)} %get-tuple-element.31), channel_id=1, source_target_pairs={{0,2},{1,3},{2,0},{3,1},{4,6},{5,7},{6,4},{7,5},{8,10},{9,11},{10,... | collective-permute-start | bytes 344072 | tf_op jit(solution)/shard_map/ppermute | solution.py:50
  141.0 11.7 %collective-permute-start.40 = (bf16[14,32,128]{2,1,0:T(8,128)(2,1)S(1)}, bf16[14,32,128]{2,1,0:T(8,128)(2,1)S(1)}, u32[]{:S(2)}, u32[]{:S(2)}) collective-permute-start(bf16[14,32,128]{2,1,0:T(8,128)(2,1)S(1)} %get-tuple-element.33), channel_id=1, source_target_pairs={{0,4},{1,5},{2,6},{3,7},{4,0},{5,1},{6,2},{7,3},{8,12},{9,13},{10,... | collective-permute-start | bytes 344072 | tf_op jit(solution)/shard_map/ppermute | solution.py:50
  142.5 10.3 %collective-permute-start.41 = (bf16[14,32,128]{2,1,0:T(8,128)(2,1)S(1)}, bf16[14,32,128]{2,1,0:T(8,128)(2,1)S(1)}, u32[]{:S(2)}, u32[]{:S(2)}) collective-permute-start(bf16[14,32,128]{2,1,0:T(8,128)(2,1)S(1)} %get-tuple-element.32), channel_id=1, source_target_pairs={{0,6},{1,7},{2,4},{3,5},{4,2},{5,3},{6,0},{7,1},{8,14},{9,15},{10,... | collective-permute-start | bytes 344072 | tf_op jit(solution)/shard_map/ppermute | solution.py:50
  144.3 14.0 %collective-permute-start.29 = (bf16[4,14,32,128]{3,2,1,0:T(8,128)(2,1)S(1)}, bf16[4,14,32,128]{3,2,1,0:T(8,128)(2,1)S(1)}, u32[]{:S(2)}, u32[]{:S(2)}) collective-permute-start(bf16[4,14,32,128]{3,2,1,0:T(8,128)(2,1)S(1)} %get-tuple-element.14), channel_id=1, source_target_pairs={{0,1},{1,0},{2,3},{3,2},{4,5},{5,4},{6,7},{7,6},{8,9},{9,8},{10,11... | collective-permute-start | bytes 1376264 | tf_op jit(solution)/shard_map/ppermute | solution.py:50
  146.8 21.1 %collective-permute-start.30 = (bf16[4,14,32,128]{3,2,1,0:T(8,128)(2,1)S(1)}, bf16[4,14,32,128]{3,2,1,0:T(8,128)(2,1)S(1)}, u32[]{:S(2)}, u32[]{:S(2)}) collective-permute-start(bf16[4,14,32,128]{3,2,1,0:T(8,128)(2,1)S(1)} %get-tuple-element.16), channel_id=1, source_target_pairs={{0,16},{1,17},{2,18},{3,19},{4,20},{5,21},{6,22},{7,23},{8,24},{9,... | collective-permute-start | bytes 1376264 | tf_op jit(solution)/shard_map/ppermute | solution.py:50
  146.8 21.1 %collective-permute-start.31 = (bf16[4,14,32,128]{3,2,1,0:T(8,128)(2,1)S(1)}, bf16[4,14,32,128]{3,2,1,0:T(8,128)(2,1)S(1)}, u32[]{:S(2)}, u32[]{:S(2)}) collective-permute-start(bf16[4,14,32,128]{3,2,1,0:T(8,128)(2,1)S(1)} %get-tuple-element.15), channel_id=1, source_target_pairs={{0,17},{1,16},{2,19},{3,18},{4,21},{5,20},{6,23},{7,22},{8,25},{9,... | collective-permute-start | bytes 1376264 | tf_op jit(solution)/shard_map/ppermute | solution.py:50
  168.3 7.1 %collective-permute-start.32 = (bf16[14,32,128]{2,1,0:T(8,128)(2,1)S(1)}, bf16[14,32,128]{2,1,0:T(8,128)(2,1)S(1)}, u32[]{:S(2)}, u32[]{:S(2)}) collective-permute-start(bf16[14,32,128]{2,1,0:T(8,128)(2,1)S(1)} %get-tuple-element.34), channel_id=1, source_target_pairs={{0,2},{1,3},{2,0},{3,1},{4,6},{5,7},{6,4},{7,5},{8,10},{9,11},{10,... | collective-permute-start | bytes 344072 | tf_op jit(solution)/shard_map/ppermute | solution.py:50
  169.1 9.6 %collective-permute-start.33 = (bf16[14,32,128]{2,1,0:T(8,128)(2,1)S(1)}, bf16[14,32,128]{2,1,0:T(8,128)(2,1)S(1)}, u32[]{:S(2)}, u32[]{:S(2)}) collective-permute-start(bf16[14,32,128]{2,1,0:T(8,128)(2,1)S(1)} %get-tuple-element.36), channel_id=1, source_target_pairs={{0,4},{1,5},{2,6},{3,7},{4,0},{5,1},{6,2},{7,3},{8,12},{9,13},{10,... | collective-permute-start | bytes 344072 | tf_op jit(solution)/shard_map/ppermute | solution.py:50
  171.3 7.5 %collective-permute-start.34 = (bf16[14,32,128]{2,1,0:T(8,128)(2,1)S(1)}, bf16[14,32,128]{2,1,0:T(8,128)(2,1)S(1)}, u32[]{:S(2)}, u32[]{:S(2)}) collective-permute-start(bf16[14,32,128]{2,1,0:T(8,128)(2,1)S(1)} %get-tuple-element.35), channel_id=1, source_target_pairs={{0,6},{1,7},{2,4},{3,5},{4,2},{5,3},{6,0},{7,1},{8,14},{9,15},{10,... | collective-permute-start | bytes 344072 | tf_op jit(solution)/shard_map/ppermute | solution.py:50

commit v2 on v1

v2 whole, which is shorter than its diff:
```python
import functools

import jax
import jax.numpy as jnp
from jax import lax
from jax.experimental import pallas as pl
from jax.experimental.pallas import tpu as pltpu
from jax.sharding import PartitionSpec as P

B = 8
AMAX = 2
LANES = 128
BOTH = ("gx", "gy")
SMALL = pl.CostEstimate(flops=1, bytes_accessed=1, transcendentals=0)

stencil_columns = [(shift_x, shift_y) for shift_x in (-1, 0, 1) for shift_y in (-1, 0, 1)]


class Plan:
    def __init__(self, n_gx, n_gy, rows, chans):
        self.n_gx = n_gx
        self.n_gy = n_gy
        self.rows = rows
        self.chans = chans
        self.cols = chans // n_gy
        self.pair = 2 if n_gx % 2 == 0 else 1
        self.inner = 2 if n_gy % 2 == 0 else 1
        self.n_y = n_gx // self.pair
        self.n_z = n_gy // self.inner
        self.n_plane = self.n_y * self.inner
        self.tiles = 27 * chans // LANES
        self.first = [rows * i // LANES for i in range(n_gx)]
        self.offset = [rows * i % LANES for i in range(n_gx)]
        self.depth = max(-(-(self.offset[i] + rows) // LANES) for i in range(n_gx))

    def owners(self, tile):
        return [
            (i, tile - self.first[i])
            for i in range(self.n_gx)
            if tile * LANES < (i + 1) * self.rows and (tile + 1) * LANES > i * self.rows
        ]


def swap(x, plan, flip_gx, flip_gy):
    n_gy = plan.n_gy
    pairs = [
        (i * n_gy + j, (i ^ flip_gx) * n_gy + (j ^ flip_gy))
        for i in range(plan.n_gx)
        for j in range(n_gy)
    ]
    return lax.ppermute(x, BOTH, pairs)


def swap_plane(x, plan, slot):
    return swap(x, plan, slot // plan.inner * plan.pair, slot % plan.inner)


def swap_z(x, plan, slot):
    return swap(x, plan, 0, slot * plan.inner)


def pick_blocks(occ_ref, n_bx, n_by):
    count = jnp.int32(0)
    first = jnp.int32(0)
    second = jnp.int32(0)
    for i in range(n_bx * n_by):
        on = occ_ref[i // n_by, i % n_by, 0] > 0
        first = jnp.where(jnp.logical_and(on, count == 0), i, first)
        second = jnp.where(jnp.logical_and(on, count == 1), i, second)
        count = count + on.astype(jnp.int32)
    blocks = []
    for slot, index in enumerate((first, second)):
        blocks.append((index // n_by, index % n_by, (count > slot).astype(jnp.int32)))
    return blocks


def block_mask(occ_ref, block, step_x, step_y, n_bx, n_by):
    bx = block[0] + step_x
    by = block[1] + step_y
    inside = (bx >= 0) & (bx < n_bx) & (by >= 0) & (by < n_by)
    near = occ_ref[jnp.clip(bx, 0, n_bx - 1), jnp.clip(by, 0, n_by - 1), 0]
    return jnp.where(inside, near, 1) * block[2]


def load_extended(index, tile_ref, low_x, high_x, low_y, high_y, ext_ref, sems):
    size_x, size_y = tile_ref.shape[:2]
    copies = [
        pltpu.make_async_copy(
            tile_ref, ext_ref.at[pl.ds(1, size_x), pl.ds(1, size_y)], sems.at[0]
        ),
        pltpu.make_async_copy(low_x.at[index], ext_ref.at[0, pl.ds(1, size_y)], sems.at[1]),
        pltpu.make_async_copy(
            high_x.at[index], ext_ref.at[size_x + 1, pl.ds(1, size_y)], sems.at[2]
        ),
        pltpu.make_async_copy(low_y.at[index], ext_ref.at[:, 0], sems.at[3]),
        pltpu.make_async_copy(high_y.at[index], ext_ref.at[:, size_y + 1], sems.at[4]),
    ]
    for copy in copies:
        copy.start()
    for copy in copies:
        copy.wait()


def spread_patches(occ_ref, blocks, ext_ref, shifted_ref, n_bx, n_by, rectify):
    edge = B
    row = lax.broadcasted_iota(jnp.int32, (edge, ext_ref.shape[-1]), 0)

    def at_x(x, carry):
        step_x = jnp.where(x == 0, -1, jnp.where(x == edge + 1, 1, 0))
        masks = [
            [block_mask(occ_ref, block, step_x, step_y, n_bx, n_by) > 0 for step_y in (-1, 0, 1)]
            for block in blocks
        ]
        for y in range(edge + 2):
            side = 0 if y == 0 else (2 if y == edge + 1 else 1)
            planes = [[], [], []]
            for index, block in enumerate(blocks):
                value = ext_ref[block[0] * edge + x, block[1] * edge + y].astype(jnp.float32)
                if rectify:
                    value = jnp.maximum(value, 0.0)
                value = jnp.where(masks[index][side], value, 0.0)
                below = jnp.where(row == 0, 0.0, pltpu.roll(value, 1, 0))
                above = jnp.where(row == edge - 1, 0.0, pltpu.roll(value, edge - 1, 0))
                for plane, part in zip(planes, (below, value, above)):
                    plane.append(part)
            for j in range(3):
                shifted_ref[j, x, y] = jnp.concatenate(planes[j], axis=0).astype(jnp.bfloat16)
        return carry

    lax.fori_loop(0, edge + 2, at_x, 0)


def gather_blocks(blocks, tile_ref, center_ref):
    edge = B

    def at_x(x, carry):
        for y in range(edge):
            parts = []
            for block in blocks:
                value = tile_ref[block[0] * edge + x, block[1] * edge + y].astype(jnp.float32)
                parts.append(jnp.where(block[2] > 0, value, 0.0))
            center_ref[x, y] = jnp.concatenate(parts, axis=0).astype(jnp.bfloat16)
        return carry

    lax.fori_loop(0, edge, at_x, 0)


def window(shifted_ref, plane, start_x, start_y):
    edge = B
    piece = shifted_ref[plane, start_x : start_x + edge, start_y : start_y + edge]
    return piece.reshape(edge * edge * AMAX * edge, piece.shape[-1])


def weight_kernel(
    plan, n_bx, n_by, index, rectify, compact,
    occ_ref, tile_ref, low_x, high_x, low_y, high_y, grad_ref,
    *rest,
):
    *out_refs, ext_ref, shifted_ref, center_ref, turned_ref, sems = rest
    blocks = pick_blocks(occ_ref, n_bx, n_by)
    load_extended(index, tile_ref, low_x, high_x, low_y, high_y, ext_ref, sems)
    spread_patches(occ_ref, blocks, ext_ref, shifted_ref, n_bx, n_by, rectify)
    if compact:
        center = grad_ref[...]
    else:
        gather_blocks(blocks, grad_ref, center_ref)
        center = center_ref[...]
    voxels = B * B * AMAX * B
    turned_ref[...] = center.reshape(voxels, plan.chans).astype(jnp.float32).T.astype(jnp.bfloat16)
    my_gx = lax.axis_index("gx")
    my_gy = lax.axis_index("gy")
    my_core = my_gx % plan.pair
    my_y = my_gx // plan.pair
    my_x = my_gy % plan.inner
    my_z = my_gy // plan.inner
    per_column = 3 * plan.chans // LANES

    def products(core_here):
        for column, (shift_x, shift_y) in enumerate(stencil_columns):
            pieces = [window(shifted_ref, j, 1 + shift_x, 1 + shift_y) for j in range(3)]
            product = jnp.dot(
                turned_ref[...],
                jnp.concatenate(pieces, axis=1),
                preferred_element_type=jnp.float32,
            ).astype(jnp.bfloat16)
            for part in range(per_column):
                lanes = product[:, part * LANES : (part + 1) * LANES]
                for shard, place in plan.owners(column * per_column + part):
                    out_ref = out_refs[(shard % plan.pair) ^ core_here]
                    y = (shard // plan.pair) ^ my_y
                    for j in range(plan.n_gy):
                        slot = y * plan.inner + ((j % plan.inner) ^ my_x)
                        z = (j // plan.inner) ^ my_z
                        out_ref[slot, z, place] = lanes[j * plan.cols : (j + 1) * plan.cols]

    for core_here in range(plan.pair):
        pl.when(my_core == core_here)(functools.partial(products, core_here))


def weight_sums(plan, occ, tile, rim, index, grad, n_bx, n_by, rectify, compact):
    size_x, size_y, edge, chans = tile.shape
    smem = pl.BlockSpec(memory_space=pltpu.SMEM)
    anywhere = pl.BlockSpec(memory_space=pl.ANY)
    vmem = pl.BlockSpec(memory_space=pltpu.VMEM)
    voxels = B * B * AMAX * B
    shape = (plan.n_plane, plan.n_z, plan.depth, plan.cols, LANES)
    return pl.pallas_call(
        functools.partial(weight_kernel, plan, n_bx, n_by, index, rectify, compact),
        out_shape=[jax.ShapeDtypeStruct(shape, jnp.bfloat16)] * plan.pair,
        in_specs=[smem] + [anywhere] * 5 + [vmem],
        out_specs=[vmem] * plan.pair,
        scratch_shapes=[
            pltpu.VMEM((size_x + 2, size_y + 2, edge, chans), jnp.bfloat16),
            pltpu.VMEM((3, B + 2, B + 2, AMAX * B, chans), jnp.bfloat16),
            pltpu.VMEM((B, B, AMAX * B, chans), jnp.bfloat16),
            pltpu.VMEM((chans, voxels), jnp.bfloat16),
            pltpu.SemaphoreType.DMA((5,)),
        ],
        compiler_params=pltpu.CompilerParams(vmem_limit_bytes=40 * 1024 * 1024),
        cost_estimate=SMALL,
    )(occ, tile, *rim, grad)


def data_kernel(
    plan, n_bx, n_by, index, gated, n_pieces,
    occ_ref, tile_ref, low_x, high_x, low_y, high_y, *rest,
):
    piece_refs = rest[:n_pieces]
    rest = rest[n_pieces:]
    if gated:
        gate_ref, out_ref, center_ref = rest[:3]
        rest = rest[3:]
    else:
        out_ref = rest[0]
        rest = rest[1:]
    ext_ref, shifted_ref, weight_ref, total_ref, sems = rest
    edge = B
    blocks = pick_blocks(occ_ref, n_bx, n_by)
    my_gx = lax.axis_index("gx")
    my_gy = lax.axis_index("gy")
    if n_pieces == 1:
        for shard in range(plan.n_gx):
            for column in range(plan.n_gy):
                weight_ref[shard, column * plan.cols : (column + 1) * plan.cols] = piece_refs[0][
                    shard * plan.n_gy + column
                ]
    else:
        for piece in range(n_pieces):
            core = piece // plan.n_plane
            slot = piece % plan.n_plane
            shard = my_gx ^ (slot // plan.inner * plan.pair + core)
            for z in range(plan.n_z):
                column = my_gy ^ (z * plan.inner + slot % plan.inner)
                start = pl.multiple_of(column * plan.cols, plan.cols)
                weight_ref[shard, pl.ds(start, plan.cols)] = piece_refs[piece][z]
    load_extended(index, tile_ref, low_x, high_x, low_y, high_y, ext_ref, sems)
    spread_patches(occ_ref, blocks, ext_ref, shifted_ref, n_bx, n_by, False)
    out_ref[...] = jnp.zeros_like(out_ref)

    def kernel_lanes(tile):
        total = None
        for shard, place in plan.owners(tile):
            part = weight_ref[shard, :, place * LANES : (place + 1) * LANES]
            total = part if total is None else total + part
        return total

    halves = plan.chans // LANES
    for column, (shift_x, shift_y) in enumerate(stencil_columns):
        pieces = [window(shifted_ref, 2 - j, 1 - shift_x, 1 - shift_y) for j in range(3)]
        taps = [
            jnp.concatenate(
                [kernel_lanes((3 * column + j) * halves + part) for part in range(halves)], axis=1
            )
            for j in range(3)
        ]
        product = jnp.dot(
            jnp.concatenate(pieces, axis=1),
            jnp.concatenate(taps, axis=0),
            preferred_element_type=jnp.float32,
        )
        if column == 0:
            total_ref[...] = product
        else:
            total_ref[...] += product

    def at_x(x, carry):
        for y in range(edge):
            kept = []
            for index, block in enumerate(blocks):
                start = pl.multiple_of((x * edge + y) * AMAX * edge, AMAX * edge) + index * edge
                value = total_ref[pl.ds(start, edge), :]
                at = (block[0] * edge + x, block[1] * edge + y)
                if gated:
                    value = jnp.where(gate_ref[at].astype(jnp.float32) > 0, value, 0.0)
                    value = jnp.where(block[2] > 0, value, 0.0)
                    kept.append(value)

                @pl.when(block[2] > 0)
                def _():
                    out_ref[at] = value.astype(jnp.bfloat16)

            if gated:
                center_ref[x, y] = jnp.concatenate(kept, axis=0).astype(jnp.bfloat16)
        return carry

    lax.fori_loop(0, edge, at_x, 0)


def data_grad(plan, occ, tile, rim, index, pieces, n_bx, n_by, gate=None):
    size_x, size_y, edge, chans = tile.shape
    smem = pl.BlockSpec(memory_space=pltpu.SMEM)
    anywhere = pl.BlockSpec(memory_space=pl.ANY)
    vmem = pl.BlockSpec(memory_space=pltpu.VMEM)
    voxels = B * B * AMAX * B
    gated = gate is not None
    out_shape = [jax.ShapeDtypeStruct(tile.shape, jnp.bfloat16)]
    if gated:
        out_shape.append(jax.ShapeDtypeStruct((B, B, AMAX * B, chans), jnp.bfloat16))
    return pl.pallas_call(
        functools.partial(data_kernel, plan, n_bx, n_by, index, gated, len(pieces)),
        out_shape=out_shape,
        in_specs=[smem] + [anywhere] * 5 + [vmem] * (len(pieces) + gated),
        out_specs=[vmem] * len(out_shape),
        scratch_shapes=[
            pltpu.VMEM((size_x + 2, size_y + 2, edge, chans), jnp.bfloat16),
            pltpu.VMEM((3, B + 2, B + 2, AMAX * B, chans), jnp.bfloat16),
            pltpu.VMEM((plan.n_gx, chans, plan.depth * LANES), jnp.bfloat16),
            pltpu.VMEM((voxels, chans), jnp.float32),
            pltpu.SemaphoreType.DMA((5,)),
        ],
        compiler_params=pltpu.CompilerParams(vmem_limit_bytes=40 * 1024 * 1024),
        cost_estimate=SMALL,
    )(occ, tile, *rim, *pieces, *([gate] if gated else []))


def after(x, *others):
    return lax.optimization_barrier((x, others))[0]


def first_kernel(
    plan, n_bx, n_by,
    occ_ref, two_ref, one_ref, *rest,
):
    field_refs = rest[:3]
    own_two, own_one, first_x, last_x, first_y, last_y, raw_ref, sems = rest[3:]
    size_x, size_y = field_refs[0].shape[:2]
    copies = []
    for index, ref in enumerate(field_refs):
        for side, strip in enumerate((ref.at[0], ref.at[size_x - 1], ref.at[:, 0], ref.at[:, size_y - 1])):
            size = size_y if side < 2 else size_x
            copies.append(
                pltpu.make_async_copy(
                    strip, raw_ref.at[side, index, pl.ds(0, size)], sems.at[side, index]
                )
            )
    for copy in copies:
        copy.start()
    offset = lax.axis_index("gx") * plan.rows % LANES
    for share_ref, weight_ref in ((own_two, two_ref), (own_one, one_ref)):
        wide = jnp.concatenate(
            [
                weight_ref[...].astype(jnp.float32),
                jnp.zeros((plan.cols, plan.depth * LANES - plan.rows), jnp.float32),
            ],
            axis=1,
        )
        share_ref[...] = pltpu.roll(wide, offset, 1).astype(jnp.bfloat16)
    for copy in copies:
        copy.wait()
    for side, strip_ref in enumerate((first_x, last_x, first_y, last_y)):
        for part in range(n_by if side < 2 else n_bx):
            at = ((0, part), (n_bx - 1, part), (part, 0), (part, n_by - 1))[side]
            rows = slice(part * B, (part + 1) * B)
            for index in range(3):
                value = raw_ref[side, index, rows].astype(jnp.float32)
                if index == 0:
                    value = jnp.maximum(value, 0.0)
                value = jnp.where(occ_ref[at[0], at[1], 0] > 0, value, 0.0)
                strip_ref[index, rows] = value.astype(jnp.bfloat16)


def first_steps(plan, occ, weight_two, weight_one, fields, n_bx, n_by):
    size_x, size_y, edge, chans = fields[0].shape
    smem = pl.BlockSpec(memory_space=pltpu.SMEM)
    anywhere = pl.BlockSpec(memory_space=pl.ANY)
    vmem = pl.BlockSpec(memory_space=pltpu.VMEM)
    share = jax.ShapeDtypeStruct((plan.cols, plan.depth * LANES), jnp.bfloat16)
    along_y = jax.ShapeDtypeStruct((3, size_y, edge, chans), jnp.bfloat16)
    along_x = jax.ShapeDtypeStruct((3, size_x, edge, chans), jnp.bfloat16)
    return pl.pallas_call(
        functools.partial(first_kernel, plan, n_bx, n_by),
        out_shape=[share, share, along_y, along_y, along_x, along_x],
        in_specs=[smem, vmem, vmem] + [anywhere] * 3,
        out_specs=[vmem] * 6,
        scratch_shapes=[
            pltpu.VMEM((4, 3, max(size_x, size_y), edge, chans), jnp.bfloat16),
            pltpu.SemaphoreType.DMA((4, 3)),
        ],
        cost_estimate=SMALL,
    )(occ, weight_two.T, weight_one.T, *fields)


def gather_line(plan, own):
    return jnp.stack([own] + [swap_z(own, plan, slot) for slot in range(1, plan.n_z)])


def gather_plane(plan, line):
    return [line] + [swap_plane(line, plan, slot) for slot in range(1, plan.n_plane)]


def gather_pair(plan, plane):
    return [swap(part, plan, 1, 0) for part in plane] if plan.pair == 2 else []


def reduce_pair(plan, sums):
    total = [sums[0][slot].astype(jnp.float32) for slot in range(plan.n_plane)]
    if plan.pair == 2:
        got = swap(sums[1], plan, 1, 0)
        total = [total[slot] + got[slot].astype(jnp.float32) for slot in range(plan.n_plane)]
    return [total[0]] + [part.astype(jnp.bfloat16) for part in total[1:]]


def swap_parts(plan, parts, swap_one):
    return [swap_one(parts[slot], plan, slot) for slot in range(1, len(parts))]


def reduce_plane(plan, own, got):
    line = own
    for part in got:
        line = line + part.astype(jnp.float32)
    return [line[0]] + [line[slot].astype(jnp.bfloat16) for slot in range(1, plan.n_z)]


def reduce_z(plan, own, got):
    for part in got:
        own = own + part.astype(jnp.float32)
    scale = float(plan.n_gx * plan.n_gy * B**3) ** (-0.5)
    flat = (own * scale).transpose(1, 0, 2).reshape(plan.cols, plan.depth * LANES)
    offset = lax.axis_index("gx") * plan.rows % LANES
    return lax.dynamic_slice(flat, (0, offset), (plan.cols, plan.rows)).T


def ring(axis):
    size = lax.axis_size(axis)
    up = [(i, i + 1) for i in range(size - 1)]
    return up, [(j, i) for i, j in up]


def rims_x(first_x, last_x):
    up, down = ring("gx")
    return lax.ppermute(last_x, "gx", up), lax.ppermute(first_x, "gx", down)


def strips_y(low_x, high_x, first_y, last_y):
    return (
        jnp.concatenate([low_x[:, :1], first_y, high_x[:, :1]], axis=1),
        jnp.concatenate([low_x[:, -1:], last_y, high_x[:, -1:]], axis=1),
    )


def rims_y(first_y, last_y):
    up, down = ring("gy")
    return lax.ppermute(last_y, "gy", up), lax.ppermute(first_y, "gy", down)


def body(inputs, preact, out_grad, weight_one, weight_two, occupancy):
    n_bx, n_by = occupancy.shape[:2]
    plan = Plan(
        lax.axis_size("gx"), lax.axis_size("gy"), weight_one.shape[0], inputs.shape[-1]
    )
    occ = occupancy

    own_two, own_one, first_x, last_x, first_y, last_y = first_steps(
        plan, occ, weight_two, weight_one, (preact, inputs, out_grad), n_bx, n_by
    )
    pieces_one = [lax.all_gather(own_one, BOTH, axis=0)]
    low_x, high_x = rims_x(first_x, last_x)
    sent_y = strips_y(low_x, high_x, first_y, last_y)
    edges = (low_x, high_x) + rims_y(*sent_y)
    line = after(gather_line(plan, own_two), edges)
    sums_two = weight_sums(plan, occ, preact, edges, 0, out_grad, n_bx, n_by, True, False)
    plane = gather_plane(plan, line)
    sums_two = [sums_two[0]] + list(after(sums_two[1:], plane))
    plane_two = reduce_pair(plan, sums_two)
    pieces_two = after(plane + gather_pair(plan, plane), plane_two)
    grad_one, center = data_grad(
        plan, occ, out_grad, edges, 2, pieces_two, n_bx, n_by, preact
    )

    strips = (grad_one[None, 0], grad_one[None, -1], grad_one[None, :, 0], grad_one[None, :, -1])
    center, strips = lax.optimization_barrier((center, strips))
    sums_one = weight_sums(plan, occ, inputs, edges, 1, center, n_bx, n_by, False, True)
    got_two = after(swap_parts(plan, plane_two, swap_plane), sums_one)
    low_x, high_x = after(rims_x(*strips[:2]), sums_one)
    sums_one = [sums_one[0]] + list(after(sums_one[1:], got_two, low_x, high_x))
    edges_one = (low_x, high_x) + rims_y(*strips_y(low_x, high_x, *strips[2:]))
    line_two = reduce_plane(plan, plane_two[0], got_two)
    sums_one = after(sums_one[:1], edges_one, line_two) + sums_one[1:]
    plane_one = reduce_pair(plan, sums_one)
    got = swap_parts(plan, line_two, swap_z)
    grad_one = after(grad_one, plane_one, got)
    (input_grad,) = data_grad(plan, occ, grad_one, edges_one, 0, pieces_one, n_bx, n_by)
    own_two = reduce_z(plan, line_two[0], after(got, input_grad))
    got_one = after(swap_parts(plan, plane_one, swap_plane), input_grad)
    line_one = reduce_plane(plan, plane_one[0], got_one)
    own_one = reduce_z(plan, line_one[0], swap_parts(plan, line_one, swap_z))
    return (input_grad, own_one, own_two)


def solution(mesh):
    return jax.shard_map(
        body,
        mesh=mesh,
        in_specs=(
            P("gx", "gy", None, None),
            P("gx", "gy", None, None),
            P("gx", "gy", None, None),
            P("gx", "gy"),
            P("gx", "gy"),
            P("gx", "gy", None),
        ),
        out_specs=(P("gx", "gy", None, None), P("gx", "gy"), P("gx", "gy")),
        check_vma=False,
    )
```

time: 180 us -> 156 us (0.87)
  waiting for transfers between devices: 60.5 us -> 45.2 us
  between operations: 3.04 us -> 14.4 us
  starting transfers between devices: 63 us -> 52.1 us
  Pallas kernels: 34.4 us -> 28.1 us
  local copies, waits for them, and re-layouts: 8.15 us -> 5.9 us
    ppermute x8, waiting for transfers between devices: 30.9 us -> 8.53 us  [the longest x4 5.57 us: rims_y(): return (lax.ppermute(last_y, 'gy', up), lax.ppermute(first_y, 'gy', down))]
    ppermute x34 -> x24, starting transfers between devices: 49.9 us -> 33.5 us  [swap(): return lax.ppermute(x, BOTH, pairs)]
    ppermute x34 -> x24, waiting for transfers between devices: 29.5 us -> 36.6 us  [swap(): return lax.ppermute(x, BOTH, pairs)]
    pallas_call x4 -> x5, Pallas kernels: 34.4 us -> 28.1 us  [the longest x2 13.4 us: data_grad(): pl.pallas_call(functools.partial(data_kernel, plan, n_bx, n_by, index, ga...]
    ppermute x8, starting transfers between devices: 13.1 us -> 18.6 us  [the longest x4 11.9 us: rims_y(): return (lax.ppermute(last_y, 'gy', up), lax.ppermute(first_y, 'gy', down))]
    dynamic_slice x3 -> x0, local copies, waits for them, and re-layouts: 3.03 us -> none  [the longest x2 1.64 us: reduce_kernel(): lax.dynamic_slice(flat, (offsets_of(plan), 0), (plan.rows, plan.cols))]
    dynamic_update_slice x2 -> x0, local copies, waits for them, and re-layouts: 2.95 us -> none  [gather_kernel(): own = lax.dynamic_update_slice(frame, weight.T, (0, offsets_of(plan)))]
    unnamed x9 -> x13, local copies, waits for them, and re-layouts: 0.6 us -> 3.49 us
  transfers between devices with their start and end apart: 42 -> 33, of which waited for: 12 -> 11; matrix products, arithmetic and copies ran while one was open for 8% -> 6% of each run, Pallas kernels for 19% -> 16%
where the time goes in v2:
time: 156 us; the launch traced here: 155 us
  starting transfers between devices  52.1 us (33%)
  waiting for transfers between devices  45.2 us (29%)
  Pallas kernels  28.1 us (18%)
  between operations  14.4 us (9%)
  other arithmetic  9.1 us (6%)
  local copies, waits for them, and re-layouts  5.9 us (4%)
    ppermute x24, waiting for transfers between devices, swap(): return lax.ppermute(x, BOTH, pairs)  36.6 us
    ppermute x24, starting transfers between devices, swap(): return lax.ppermute(x, BOTH, pairs)  33.5 us
    pallas_call x2, Pallas kernels, data_grad(): pl.pallas_call(functools.partial(data_kernel, plan, n_bx, n_by, index, ga...  13.4 us
    ppermute x4, starting transfers between devices, rims_y(): return (lax.ppermute(last_y, 'gy', up), lax.ppermute(first_y, 'gy', down))  11.9 us
    pallas_call x2, Pallas kernels, weight_sums(): pl.pallas_call(functools.partial(weight_kernel, plan, n_bx, n_by, index,...  11.4 us
    ppermute x4, starting transfers between devices, rims_x(): return (lax.ppermute(last_x, 'gx', up), lax.ppermute(first_x, 'gx', down))  6.68 us
    ppermute x4, waiting for transfers between devices, rims_y(): return (lax.ppermute(last_y, 'gy', up), lax.ppermute(first_y, 'gy', down))  5.57 us
    unnamed x13, local copies, waits for them, and re-layouts  3.49 us
  transfers between devices with their start and end apart: 33, of which 11 were waited for; matrix products, arithmetic and copies ran while one was open for 6% of the time, Pallas kernels for 16%

profile of v2, /device:TPU:0, one launch (start us, length us, event | category | flops | bytes accessed | tf_op | source)
XLA Modules:
  0.0 154.7 jit_solution(10930739910951995113)
XLA Ops:
  7.2 0.0 all-gather.3.cloned.1.call-start
  7.2 1.4 copy.22.occ_ref
  8.6 3.3 %shard_map.85 = (bf16[32,1792]{1,0:T(8,128)(2,1)}, bf16[32,1792]{1,0:T(8,128)(2,1)}, bf16[3,16,8,256]{3,2,1,0:T(8,128)(2,1)}, bf16[3,16,8,256]{3,2,1,0:T(8,128)(...) custom-call(s32[2,2,1]{2,1,0:T(2,128)} %copy.22.occ_ref, bf16[32,1728]{1,0:T(8,128)(2,1)} %bitcast.84, ...), custom_call_target="tpu_custom_call" | custom-call | flops 1 | bytes 1 | tf_op jit(solution)/shard_map/pallas_call | solution.py:390
  11.9 0.0 copy-start
  11.9 0.0 all-gather.3.cloned.1.call-update
  11.9 2.5 %collective-permute-start = (bf16[3,16,8,256]{3,2,1,0:T(8,128)(2,1)}, bf16[3,16,8,256]{3,2,1,0:T(8,128)(2,1)S(1)}, u32[]{:S(2)}, u32[]{:S(2)}) collective-permute-start(bf16[3,16,8,256]{3,2,1,0:T(8,128)(2,1)} %get-tuple-element.44), channel_id=1, source_target_pairs={{0,8},{8,16},{16,24},{1,9},{9,17},{17,25},{2,10},{10,18},{18,26},{... | collective-permute-start | bytes 589832 | tf_op jit(solution)/shard_map/ppermute | solution.py:451
  14.4 2.5 %collective-permute-start.4 = (bf16[32,1792]{1,0:T(8,128)(2,1)}, bf16[32,1792]{1,0:T(8,128)(2,1)S(1)}, u32[]{:S(2)}, u32[]{:S(2)}) collective-permute-start(bf16[32,1792]{1,0:T(8,128)(2,1)} %get-tuple-element.48), channel_id=1, source_target_pairs={{0,2},{1,3},{2,0},{3,1},{4,6},{5,7},{6,4},{7,5},{8,10},{9,11},{10,... | collective-permute-start | bytes 344072 | tf_op jit(solution)/shard_map/ppermute | solution.py:51
  16.9 2.6 %collective-permute-start.5 = (bf16[32,1792]{1,0:T(8,128)(2,1)}, bf16[32,1792]{1,0:T(8,128)(2,1)S(1)}, u32[]{:S(2)}, u32[]{:S(2)}) collective-permute-start(bf16[32,1792]{1,0:T(8,128)(2,1)} %get-tuple-element.48), channel_id=1, source_target_pairs={{0,4},{1,5},{2,6},{3,7},{4,0},{5,1},{6,2},{7,3},{8,12},{9,13},{10,... | collective-permute-start | bytes 344072 | tf_op jit(solution)/shard_map/ppermute | solution.py:51
  19.5 1.3 collective-permute-start.1
  20.8 3.0 %collective-permute-done.1.high_x = bf16[3,16,8,256]{3,2,1,0:T(8,128)(2,1)S(1)} collective-permute-done((bf16[3,16,8,256]{3,2,1,0:T(8,128)(2,1)}, bf16[3,16,8,256]{3,2,1,0:T(8,128)(2,1)S(1)}, u32[]{:S(2)}, u32[]{:S(2)}) %collective-permute-start.1) | collective-permute-done | bytes 196640 | tf_op jit(solution)/shard_map/ppermute | solution.py:451
  23.8 1.0 pad_maximum_fusion.2
  24.7 1.3 collective-permute-start.3
  26.0 1.0 pad_maximum_fusion.1
  27.0 4.6 %collective-permute-start.2 = (bf16[3,18,8,256]{3,2,1,0:T(8,128)(2,1)S(1)}, bf16[3,18,8,256]{3,2,1,0:T(8,128)(2,1)S(1)}, u32[]{:S(2)}, u32[]{:S(2)}) collective-permute-start(bf16[3,18,8,256]{3,2,1,0:T(8,128)(2,1)S(1)} %pad_maximum_fusion.1), channel_id=1, source_target_pairs={{0,1},{1,2},{2,3},{3,4},{4,5},{5,6},{6,7},{8,9},{9,10},{10,11},{11... | collective-permute-start | bytes 663560 | tf_op jit(solution)/shard_map/ppermute | solution.py:463
  31.6 1.0 pad_maximum_fusion.rest_0_
  32.6 5.6 %collective-permute-done.2.low_y = bf16[3,18,8,256]{3,2,1,0:T(8,128)(2,1)S(1)} collective-permute-done((bf16[3,18,8,256]{3,2,1,0:T(8,128)(2,1)S(1)}, bf16[3,18,8,256]{3,2,1,0:T(8,128)(2,1)S(1)}, u32[]{:S(2)}, u32[]{:S(2)}) %collective-permute-start.2) | collective-permute-done | bytes 221216 | tf_op jit(solution)/shard_map/ppermute | solution.py:463
  38.1 2.5 %collective-permute-start.7 = (bf16[4,32,1792]{2,1,0:T(8,128)(2,1)S(1)}, bf16[4,32,1792]{2,1,0:T(8,128)(2,1)S(1)}, u32[]{:S(2)}, u32[]{:S(2)}) collective-permute-start(bf16[4,32,1792]{2,1,0:T(8,128)(2,1)S(1)} %pad_maximum_fusion.rest_0_), channel_id=1, source_target_pairs={{0,1},{1,0},{2,3},{3,2},{4,5},{5,4},{6,7},{7,6},{8,9},{9,8},{10,11... | collective-permute-start | bytes 1376264 | tf_op jit(solution)/shard_map/ppermute | solution.py:51
  40.6 2.5 %collective-permute-start.8 = (bf16[4,32,1792]{2,1,0:T(8,128)(2,1)S(1)}, bf16[4,32,1792]{2,1,0:T(8,128)(2,1)S(1)}, u32[]{:S(2)}, u32[]{:S(2)}) collective-permute-start(bf16[4,32,1792]{2,1,0:T(8,128)(2,1)S(1)} %pad_maximum_fusion.rest_0_), channel_id=1, source_target_pairs={{0,16},{1,17},{2,18},{3,19},{4,20},{5,21},{6,22},{7,23},{8,24},{9,... | collective-permute-start | bytes 1376264 | tf_op jit(solution)/shard_map/ppermute | solution.py:51
  43.1 5.9 %shard_map.86 = (bf16[4,4,14,32,128]{4,3,2,1,0:T(8,128)(2,1)S(1)}, bf16[4,4,14,32,128]{4,3,2,1,0:T(8,128)(2,1)S(1)}) custom-call(s32[2,2,1]{2,1,0:T(2,128)S(1)} %copy-done.4, bf16[16,16,8,256]{3,2,1,0:T(8,128)(2,1)S(1)} %copy-done.1, bf16[3,16,8,256]{3,2,1,0:T(8,128)(2,1)S(1)} %collective-permute-done.low_x, ...), custom_call_target="tpu_custom_call" | custom-call | flops 1 | bytes 1 | tf_op jit(solution)/shard_map/pallas_call | solution.py:207
  49.0 5.4 %collective-permute-done.7.rest_1_ = bf16[4,32,1792]{2,1,0:T(8,128)(2,1)S(1)} collective-permute-done((bf16[4,32,1792]{2,1,0:T(8,128)(2,1)S(1)}, bf16[4,32,1792]{2,1,0:T(8,128)(2,1)S(1)}, u32[]{:S(2)}, u32[]{:S(2)}) %collective-permute-start.7) | collective-permute-done | bytes 458784 | tf_op jit(solution)/shard_map/ppermute | solution.py:51
  54.5 1.8 %collective-permute-done.8.rest_2_ = bf16[4,32,1792]{2,1,0:T(8,128)(2,1)S(1)} collective-permute-done((bf16[4,32,1792]{2,1,0:T(8,128)(2,1)S(1)}, bf16[4,32,1792]{2,1,0:T(8,128)(2,1)S(1)}, u32[]{:S(2)}, u32[]{:S(2)}) %collective-permute-start.8) | collective-permute-done | bytes 458784 | tf_op jit(solution)/shard_map/ppermute | solution.py:51
  56.2 10.9 %collective-permute-done.9.rest_3_ = bf16[4,32,1792]{2,1,0:T(8,128)(2,1)S(1)} collective-permute-done((bf16[4,32,1792]{2,1,0:T(8,128)(2,1)S(1)}, bf16[4,32,1792]{2,1,0:T(8,128)(2,1)S(1)}, u32[]{:S(2)}, u32[]{:S(2)}) %collective-permute-start.9) | collective-permute-done | bytes 458784 | tf_op jit(solution)/shard_map/ppermute | solution.py:51
  67.2 0.2 collective-permute-start.14
  67.4 0.3 collective-permute-start.10
  67.7 0.2 collective-permute-start.11
  67.9 0.3 collective-permute-start.12
  68.2 0.2 collective-permute-start.13
  68.4 2.5 %collective-permute-done.14 = bf16[4,4,14,32,128]{4,3,2,1,0:T(8,128)(2,1)S(1)} collective-permute-done((bf16[4,4,14,32,128]{4,3,2,1,0:T(8,128)(2,1)S(1)}, bf16[4,4,14,32,128]{4,3,2,1,0:T(8,128)(2,1)S(1)}, u32[]{:S(2)}, u32[]{:S(2)}) %collective-permute-start.14) | collective-permute-done | bytes 1835040 | tf_op jit(solution)/shard_map/ppermute | solution.py:51
  71.0 0.4 fusion.2
  71.4 3.1 %collective-permute-start.19 = (bf16[4,14,32,128]{3,2,1,0:T(8,128)(2,1)S(1)}, bf16[4,14,32,128]{3,2,1,0:T(8,128)(2,1)S(1)}, u32[]{:S(2)}, u32[]{:S(2)}) collective-permute-start(bf16[4,14,32,128]{3,2,1,0:T(8,128)(2,1)S(1)} %get-tuple-element.94), channel_id=1, source_target_pairs={{0,1},{1,0},{2,3},{3,2},{4,5},{5,4},{6,7},{7,6},{8,9},{9,8},{10,11... | collective-permute-start | bytes 1376264 | tf_op jit(solution)/shard_map/ppermute | solution.py:51
  74.5 0.9 collective-permute-start.20
  75.4 0.8 collective-permute-start.21
  76.2 6.3 %shard_map.87 = (bf16[16,16,8,256]{3,2,1,0:T(8,128)(2,1)S(1)}, bf16[8,8,16,256]{3,2,1,0:T(8,128)(2,1)S(1)}) custom-call(s32[2,2,1]{2,1,0:T(2,128)S(1)} %copy-done.4, bf16[16,16,8,256]{3,2,1,0:T(8,128)(2,1)S(1)} %copy-done, bf16[3,16,8,256]{3,2,1,0:T(8,128)(2,1)S(1)} %collective-permute-done.low_x, bf16[3,16,8,256]{3,2,1,0:T(8,128)(2,1)S(1)} %collective-permute-done.1.high_x, ...), custom_call_target="tpu_custom_call" | custom-call | flops 1 | bytes 1 | tf_op jit(solution)/shard_map/pallas_call | solution.py:319
  82.6 1.6 %collective-permute-start.15 = (bf16[1,16,8,256]{3,2,1,0:T(8,128)(2,1)S(1)}, bf16[1,16,8,256]{3,2,1,0:T(8,128)(2,1)S(1)}, u32[]{:S(2)}, u32[]{:S(2)}) collective-permute-start(bf16[1,16,8,256]{3,2,1,0:T(8,128)(2,1)S(1)} %get-tuple-element.65), channel_id=1, source_target_pairs={{0,8},{8,16},{16,24},{1,9},{9,17},{17,25},{2,10},{10,18},{18,26},{... | collective-permute-start | bytes 196616 | tf_op jit(solution)/shard_map/ppermute | solution.py:451
  84.2 1.3 collective-permute-start.16
  85.5 5.5 %shard_map.88 = (bf16[4,4,14,32,128]{4,3,2,1,0:T(8,128)(2,1)S(1)}, bf16[4,4,14,32,128]{4,3,2,1,0:T(8,128)(2,1)S(1)}) custom-call(s32[2,2,1]{2,1,0:T(2,128)S(1)} %copy-done.4, bf16[16,16,8,256]{3,2,1,0:T(8,128)(2,1)S(1)} %copy-done.2, bf16[3,16,8,256]{3,2,1,0:T(8,128)(2,1)S(1)} %collective-permute-done.low_x, ...), custom_call_target="tpu_custom_call" | custom-call | flops 1 | bytes 1 | tf_op jit(solution)/shard_map/pallas_call | solution.py:207
  91.1 5.5 %collective-permute-done.20 = bf16[4,14,32,128]{3,2,1,0:T(8,128)(2,1)S(1)} collective-permute-done((bf16[4,14,32,128]{3,2,1,0:T(8,128)(2,1)S(1)}, bf16[4,14,32,128]{3,2,1,0:T(8,128)(2,1)S(1)}, u32[]{:S(2)}, u32[]{:S(2)}) %collective-permute-start.20) | collective-permute-done | bytes 458784 | tf_op jit(solution)/shard_map/ppermute | solution.py:51
  96.6 0.6 collective-permute-start.22
  97.2 1.3 collective-permute-start.18
  98.5 4.8 %collective-permute-start.17 = (bf16[1,18,8,256]{3,2,1,0:T(8,128)(2,1)S(1)}, bf16[1,18,8,256]{3,2,1,0:T(8,128)(2,1)S(1)}, u32[]{:S(2)}, u32[]{:S(2)}) collective-permute-start(bf16[1,18,8,256]{3,2,1,0:T(8,128)(2,1)S(1)} %pad_maximum_fusion.3), channel_id=1, source_target_pairs={{0,1},{1,2},{2,3},{3,4},{4,5},{5,6},{6,7},{8,9},{9,10},{10,11},{11... | collective-permute-start | bytes 221192 | tf_op jit(solution)/shard_map/ppermute | solution.py:463
  103.3 1.3 fusion.12
  104.6 0.7 slice_bitcast_fusion.5
  105.3 1.7 %fusion.5 = (bf16[4,14,32,128]{3,2,1,0:T(8,128)(2,1)}, bf16[4,14,32,128]{3,2,1,0:T(8,128)(2,1)}, bf16[4,14,32,128]{3,2,1,0:T(8,128)(2,1)}) fusion(bf16[4,4,14,32,128]{4,3,2,1,0:T(8,128)(2,1)S(1)} %collective-permute-done.22, bf16[4,4,14,32,128]{4,3,2,1,0:T(8,128)(2,1)S(1)} %get-tuple-element.75), kind=kLoop, calls=%fused_computation.15 | loop fusion | flops 2752512 | bytes 4128768 | tf_op jit(solution)/shard_map/convert_element_type | solution.py:420
  107.0 0.1 copy-done.5
  107.0 2.1 %collective-permute-start.26 = (bf16[4,14,32,128]{3,2,1,0:T(8,128)(2,1)}, bf16[4,14,32,128]{3,2,1,0:T(8,128)(2,1)}, u32[]{:S(2)}, u32[]{:S(2)}) collective-permute-start(bf16[4,14,32,128]{3,2,1,0:T(8,128)(2,1)} %get-tuple-element.91), channel_id=1, source_target_pairs={{0,1},{1,0},{2,3},{3,2},{4,5},{5,4},{6,7},{7,6},{8,9},{9,8},{10,11... | collective-permute-start | bytes 1376264 | tf_op jit(solution)/shard_map/ppermute | solution.py:51
  109.2 1.3 collective-permute-start.27
  110.5 0.2 collective-permute-start.28
  110.6 3.2 %collective-permute-start.23 = (bf16[14,32,128]{2,1,0:T(8,128)(2,1)S(1)}, bf16[14,32,128]{2,1,0:T(8,128)(2,1)S(1)}, u32[]{:S(2)}, u32[]{:S(2)}) collective-permute-start(bf16[14,32,128]{2,1,0:T(8,128)(2,1)S(1)} %get-tuple-element.104), channel_id=1, source_target_pairs={{0,2},{1,3},{2,0},{3,1},{4,6},{5,7},{6,4},{7,5},{8,10},{9,11},{10,... | collective-permute-start | bytes 344072 | tf_op jit(solution)/shard_map/ppermute | solution.py:51
  113.9 2.3 %collective-permute-start.24 = (bf16[14,32,128]{2,1,0:T(8,128)(2,1)}, bf16[14,32,128]{2,1,0:T(8,128)(2,1)S(1)}, u32[]{:S(2)}, u32[]{:S(2)}) collective-permute-start(bf16[14,32,128]{2,1,0:T(8,128)(2,1)} %get-tuple-element.103), channel_id=1, source_target_pairs={{0,4},{1,5},{2,6},{3,7},{4,0},{5,1},{6,2},{7,3},{8,12},{9,13},{10,... | collective-permute-start | bytes 344072 | tf_op jit(solution)/shard_map/ppermute | solution.py:51
  116.2 1.6 %collective-permute-done.23 = bf16[14,32,128]{2,1,0:T(8,128)(2,1)S(1)} collective-permute-done((bf16[14,32,128]{2,1,0:T(8,128)(2,1)S(1)}, bf16[14,32,128]{2,1,0:T(8,128)(2,1)S(1)}, u32[]{:S(2)}, u32[]{:S(2)}) %collective-permute-start.23) | collective-permute-done | bytes 114720 | tf_op jit(solution)/shard_map/ppermute | solution.py:51
  117.8 3.1 %collective-permute-start.25 = (bf16[14,32,128]{2,1,0:T(8,128)(2,1)}, bf16[14,32,128]{2,1,0:T(8,128)(2,1)}, u32[]{:S(2)}, u32[]{:S(2)}) collective-permute-start(bf16[14,32,128]{2,1,0:T(8,128)(2,1)} %get-tuple-element.102), channel_id=1, source_target_pairs={{0,6},{1,7},{2,4},{3,5},{4,2},{5,3},{6,0},{7,1},{8,14},{9,15},{10,... | collective-permute-start | bytes 344072 | tf_op jit(solution)/shard_map/ppermute | solution.py:51
  120.9 2.5 %collective-permute-done.24 = bf16[14,32,128]{2,1,0:T(8,128)(2,1)S(1)} collective-permute-done((bf16[14,32,128]{2,1,0:T(8,128)(2,1)}, bf16[14,32,128]{2,1,0:T(8,128)(2,1)S(1)}, u32[]{:S(2)}, u32[]{:S(2)}) %collective-permute-start.24) | collective-permute-done | bytes 114720 | tf_op jit(solution)/shard_map/ppermute | solution.py:51
  123.4 1.4 collective-permute-done.25
  124.8 2.0 %copy-done.3 = bf16[1024,1792]{1,0:T(8,128)(2,1)S(1)} copy-done((bf16[1024,1792]{1,0:T(8,128)(2,1)S(1)}, bf16[1024,1792]{1,0:T(8,128)(2,1)}, u32[]{:S(2)}) %copy-start.3) | copy-done | bytes 3670040
  126.8 7.1 %shard_map.89 = bf16[16,16,8,256]{3,2,1,0:T(8,128)(2,1)} custom-call(s32[2,2,1]{2,1,0:T(2,128)S(1)} %copy-done.4, bf16[16,16,8,256]{3,2,1,0:T(8,128)(2,1)S(1)} %get-tuple-element.77.tile_ref, bf16[1,16,8,256]{3,2,1,0:T(8,128)(2,1)S(1)} %collective-permute-done.15.low_x, bf16[1,16,8,256]{3,2,1,0:T(8,128)(2,1)S(1)} %collective-permute-done.16.high_x, ...), custom_call_target="tpu_custom_call" | custom-call | flops 1 | bytes 1 | tf_op jit(solution)/shard_map/pallas_call | solution.py:319
  133.9 1.7 %fusion.11 = (bf16[4,14,32,128]{3,2,1,0:T(8,128)(2,1)S(1)}, f32[4,14,32,128]{3,2,1,0:T(8,128)S(1)}) fusion(bf16[4,14,32,128]{3,2,1,0:T(8,128)(2,1)} %collective-permute-done.28, bf16[4,14,32,128]{3,2,1,0:T(8,128)(2,1)} %collective-permute-done.27, bf16[4,14,32,128]{3,2,1,0:T(8,128)(2,1)} %collective-permute-done.26, ...), kind=kLoop, calls=%fused_computation.41 | loop fusion | flops 2293760 | bytes 3670016 | tf_op jit(solution)/shard_map/convert.2
  135.7 1.8 %collective-permute-start.29 = (bf16[14,32,128]{2,1,0:T(8,128)(2,1)S(1)}, bf16[14,32,128]{2,1,0:T(8,128)(2,1)S(1)}, u32[]{:S(2)}, u32[]{:S(2)}) collective-permute-start(bf16[14,32,128]{2,1,0:T(8,128)(2,1)S(1)} %get-tuple-element.99), channel_id=1, source_target_pairs={{0,2},{1,3},{2,0},{3,1},{4,6},{5,7},{6,4},{7,5},{8,10},{9,11},{10,... | collective-permute-start | bytes 344072 | tf_op jit(solution)/shard_map/ppermute | solution.py:51
  137.5 2.0 %collective-permute-start.30 = (bf16[14,32,128]{2,1,0:T(8,128)(2,1)S(1)}, bf16[14,32,128]{2,1,0:T(8,128)(2,1)S(1)}, u32[]{:S(2)}, u32[]{:S(2)}) collective-permute-start(bf16[14,32,128]{2,1,0:T(8,128)(2,1)S(1)} %get-tuple-element.101), channel_id=1, source_target_pairs={{0,4},{1,5},{2,6},{3,7},{4,0},{5,1},{6,2},{7,3},{8,12},{9,13},{10,... | collective-permute-start | bytes 344072 | tf_op jit(solution)/shard_map/ppermute | solution.py:51
  139.5 0.7 collective-permute-start.31
  140.2 1.1 copy_bitcast_fusion
  141.2 0.8 dynamic-slice_bitcast_fusion
  142.1 4.9 %collective-permute-done.30 = bf16[14,32,128]{2,1,0:T(8,128)(2,1)S(1)} collective-permute-done((bf16[14,32,128]{2,1,0:T(8,128)(2,1)S(1)}, bf16[14,32,128]{2,1,0:T(8,128)(2,1)S(1)}, u32[]{:S(2)}, u32[]{:S(2)}) %collective-permute-start.30) | collective-permute-done | bytes 114720 | tf_op jit(solution)/shard_map/ppermute | solution.py:51
  147.0 0.1 copy_bitcast_fusion.1
  147.1 0.8 dynamic-slice_bitcast_fusion.1
  (41 shorter events, 0.2 us)
Async XLA Ops:
  7.2 117.6 %all-gather.3.cloned.1.call-start = ((), (), s32[]{:S(2)}) async-start(), calls=%async_computation | async-start | bytes 3784704 | tf_op jit(solution)/shard_map/all_gather | solution.py:476
  8.6 34.5 %copy-start.1 = (bf16[16,16,8,256]{3,2,1,0:T(8,128)(2,1)S(1)}, bf16[16,16,8,256]{3,2,1,0:T(8,128)(2,1)}, u32[]{:S(2)}) copy-start(bf16[16,16,8,256]{3,2,1,0:T(8,128)(2,1)} %rest_8_.1) | copy-start | bytes 3145732
  11.9 31.2 %copy-start = (bf16[16,16,8,256]{3,2,1,0:T(8,128)(2,1)S(1)}, bf16[16,16,8,256]{3,2,1,0:T(8,128)(2,1)}, u32[]{:S(2)}) copy-start(bf16[16,16,8,256]{3,2,1,0:T(8,128)(2,1)} %tile_ref.4) | copy-start | bytes 3145732
  11.9 31.2 %copy-start.4 = (s32[2,2,1]{2,1,0:T(2,128)S(1)}, s32[2,2,1]{2,1,0:T(2,128)}, u32[]{:S(2)}) copy-start(s32[2,2,1]{2,1,0:T(2,128)} %copy.22.occ_ref) | copy-start | bytes 52
  11.9 8.9 %collective-permute-start = (bf16[3,16,8,256]{3,2,1,0:T(8,128)(2,1)}, bf16[3,16,8,256]{3,2,1,0:T(8,128)(2,1)S(1)}, u32[]{:S(2)}, u32[]{:S(2)}) collective-permute-start(bf16[3,16,8,256]{3,2,1,0:T(8,128)(2,1)} %get-tuple-element.44), channel_id=1, source_target_pairs={{0,8},{8,16},{16,24},{1,9},{9,17},{17,25},{2,10},{10,18},{18,26},{... | collective-permute-start | bytes 589832 | tf_op jit(solution)/shard_map/ppermute | solution.py:451
  14.4 17.1 %collective-permute-start.4 = (bf16[32,1792]{1,0:T(8,128)(2,1)}, bf16[32,1792]{1,0:T(8,128)(2,1)S(1)}, u32[]{:S(2)}, u32[]{:S(2)}) collective-permute-start(bf16[32,1792]{1,0:T(8,128)(2,1)} %get-tuple-element.48), channel_id=1, source_target_pairs={{0,2},{1,3},{2,0},{3,1},{4,6},{5,7},{6,4},{7,5},{8,10},{9,11},{10,... | collective-permute-start | bytes 344072 | tf_op jit(solution)/shard_map/ppermute | solution.py:51
  16.9 14.7 %collective-permute-start.5 = (bf16[32,1792]{1,0:T(8,128)(2,1)}, bf16[32,1792]{1,0:T(8,128)(2,1)S(1)}, u32[]{:S(2)}, u32[]{:S(2)}) collective-permute-start(bf16[32,1792]{1,0:T(8,128)(2,1)} %get-tuple-element.48), channel_id=1, source_target_pairs={{0,4},{1,5},{2,6},{3,7},{4,0},{5,1},{6,2},{7,3},{8,12},{9,13},{10,... | collective-permute-start | bytes 344072 | tf_op jit(solution)/shard_map/ppermute | solution.py:51
  19.5 12.1 %collective-permute-start.6 = (bf16[32,1792]{1,0:T(8,128)(2,1)}, bf16[32,1792]{1,0:T(8,128)(2,1)S(1)}, u32[]{:S(2)}, u32[]{:S(2)}) collective-permute-start(bf16[32,1792]{1,0:T(8,128)(2,1)} %get-tuple-element.48), channel_id=1, source_target_pairs={{0,6},{1,7},{2,4},{3,5},{4,2},{5,3},{6,0},{7,1},{8,14},{9,15},{10,... | collective-permute-start | bytes 344072 | tf_op jit(solution)/shard_map/ppermute | solution.py:51
  19.5 4.3 %collective-permute-start.1 = (bf16[3,16,8,256]{3,2,1,0:T(8,128)(2,1)}, bf16[3,16,8,256]{3,2,1,0:T(8,128)(2,1)S(1)}, u32[]{:S(2)}, u32[]{:S(2)}) collective-permute-start(bf16[3,16,8,256]{3,2,1,0:T(8,128)(2,1)} %get-tuple-element.45), channel_id=1, source_target_pairs={{8,0},{16,8},{24,16},{9,1},{17,9},{25,17},{10,2},{18,10},{26,18},{... | collective-permute-start | bytes 589832 | tf_op jit(solution)/shard_map/ppermute | solution.py:451
  24.7 7.8 %collective-permute-start.3 = (bf16[3,18,8,256]{3,2,1,0:T(8,128)(2,1)S(1)}, bf16[3,18,8,256]{3,2,1,0:T(8,128)(2,1)S(1)}, u32[]{:S(2)}, u32[]{:S(2)}) collective-permute-start(bf16[3,18,8,256]{3,2,1,0:T(8,128)(2,1)S(1)} %pad_maximum_fusion.2), channel_id=1, source_target_pairs={{1,0},{2,1},{3,2},{4,3},{5,4},{6,5},{7,6},{9,8},{10,9},{11,10},{12... | collective-permute-start | bytes 663560 | tf_op jit(solution)/shard_map/ppermute | solution.py:463
  27.0 11.1 %collective-permute-start.2 = (bf16[3,18,8,256]{3,2,1,0:T(8,128)(2,1)S(1)}, bf16[3,18,8,256]{3,2,1,0:T(8,128)(2,1)S(1)}, u32[]{:S(2)}, u32[]{:S(2)}) collective-permute-start(bf16[3,18,8,256]{3,2,1,0:T(8,128)(2,1)S(1)} %pad_maximum_fusion.1), channel_id=1, source_target_pairs={{0,1},{1,2},{2,3},{3,4},{4,5},{5,6},{6,7},{8,9},{9,10},{10,11},{11... | collective-permute-start | bytes 663560 | tf_op jit(solution)/shard_map/ppermute | solution.py:463
  38.1 16.3 %collective-permute-start.7 = (bf16[4,32,1792]{2,1,0:T(8,128)(2,1)S(1)}, bf16[4,32,1792]{2,1,0:T(8,128)(2,1)S(1)}, u32[]{:S(2)}, u32[]{:S(2)}) collective-permute-start(bf16[4,32,1792]{2,1,0:T(8,128)(2,1)S(1)} %pad_maximum_fusion.rest_0_), channel_id=1, source_target_pairs={{0,1},{1,0},{2,3},{3,2},{4,5},{5,4},{6,7},{7,6},{8,9},{9,8},{10,11... | collective-permute-start | bytes 1376264 | tf_op jit(solution)/shard_map/ppermute | solution.py:51
  40.6 15.6 %collective-permute-start.8 = (bf16[4,32,1792]{2,1,0:T(8,128)(2,1)S(1)}, bf16[4,32,1792]{2,1,0:T(8,128)(2,1)S(1)}, u32[]{:S(2)}, u32[]{:S(2)}) collective-permute-start(bf16[4,32,1792]{2,1,0:T(8,128)(2,1)S(1)} %pad_maximum_fusion.rest_0_), channel_id=1, source_target_pairs={{0,16},{1,17},{2,18},{3,19},{4,20},{5,21},{6,22},{7,23},{8,24},{9,... | collective-permute-start | bytes 1376264 | tf_op jit(solution)/shard_map/ppermute | solution.py:51
  43.1 24.1 %collective-permute-start.9 = (bf16[4,32,1792]{2,1,0:T(8,128)(2,1)S(1)}, bf16[4,32,1792]{2,1,0:T(8,128)(2,1)S(1)}, u32[]{:S(2)}, u32[]{:S(2)}) collective-permute-start(bf16[4,32,1792]{2,1,0:T(8,128)(2,1)S(1)} %pad_maximum_fusion.rest_0_), channel_id=1, source_target_pairs={{0,17},{1,16},{2,19},{3,18},{4,21},{5,20},{6,23},{7,22},{8,25},{9,... | collective-permute-start | bytes 1376264 | tf_op jit(solution)/shard_map/ppermute | solution.py:51
  67.2 3.8 %collective-permute-start.14 = (bf16[4,4,14,32,128]{4,3,2,1,0:T(8,128)(2,1)S(1)}, bf16[4,4,14,32,128]{4,3,2,1,0:T(8,128)(2,1)S(1)}, u32[]{:S(2)}, u32[]{:S(2)}) collective-permute-start(bf16[4,4,14,32,128]{4,3,2,1,0:T(8,128)(2,1)S(1)} %get-tuple-element.52), channel_id=1, source_target_pairs={{0,8},{1,9},{2,10},{3,11},{4,12},{5,13},{6,14},{7,15},{8,0},{9,1},... | collective-permute-start | bytes 5505032 | tf_op jit(solution)/shard_map/ppermute | solution.py:51
  67.4 7.0 %collective-permute-start.10 = (bf16[4,32,1792]{2,1,0:T(8,128)(2,1)S(1)}, bf16[4,32,1792]{2,1,0:T(8,128)(2,1)S(1)}, u32[]{:S(2)}, u32[]{:S(2)}) collective-permute-start(bf16[4,32,1792]{2,1,0:T(8,128)(2,1)S(1)} %pad_maximum_fusion.rest_0_), channel_id=1, source_target_pairs={{0,8},{1,9},{2,10},{3,11},{4,12},{5,13},{6,14},{7,15},{8,0},{9,1},... | collective-permute-start | bytes 1376264 | tf_op jit(solution)/shard_map/ppermute | solution.py:51
  67.7 7.7 %collective-permute-start.11 = (bf16[4,32,1792]{2,1,0:T(8,128)(2,1)S(1)}, bf16[4,32,1792]{2,1,0:T(8,128)(2,1)S(1)}, u32[]{:S(2)}, u32[]{:S(2)}) collective-permute-start(bf16[4,32,1792]{2,1,0:T(8,128)(2,1)S(1)} %collective-permute-done.7.rest_1_), channel_id=1, source_target_pairs={{0,8},{1,9},{2,10},{3,11},{4,12},{5,13},{6,14},{7,15},{8,0},{9,1},... | collective-permute-start | bytes 1376264 | tf_op jit(solution)/shard_map/ppermute | solution.py:51
  67.9 8.3 %collective-permute-start.12 = (bf16[4,32,1792]{2,1,0:T(8,128)(2,1)S(1)}, bf16[4,32,1792]{2,1,0:T(8,128)(2,1)S(1)}, u32[]{:S(2)}, u32[]{:S(2)}) collective-permute-start(bf16[4,32,1792]{2,1,0:T(8,128)(2,1)S(1)} %collective-permute-done.8.rest_2_), channel_id=1, source_target_pairs={{0,8},{1,9},{2,10},{3,11},{4,12},{5,13},{6,14},{7,15},{8,0},{9,1},... | collective-permute-start | bytes 1376264 | tf_op jit(solution)/shard_map/ppermute | solution.py:51
  68.2 8.0 %collective-permute-start.13 = (bf16[4,32,1792]{2,1,0:T(8,128)(2,1)S(1)}, bf16[4,32,1792]{2,1,0:T(8,128)(2,1)S(1)}, u32[]{:S(2)}, u32[]{:S(2)}) collective-permute-start(bf16[4,32,1792]{2,1,0:T(8,128)(2,1)S(1)} %collective-permute-done.9.rest_3_), channel_id=1, source_target_pairs={{0,8},{1,9},{2,10},{3,11},{4,12},{5,13},{6,14},{7,15},{8,0},{9,1},... | collective-permute-start | bytes 1376264 | tf_op jit(solution)/shard_map/ppermute | solution.py:51
  71.4 19.7 %collective-permute-start.19 = (bf16[4,14,32,128]{3,2,1,0:T(8,128)(2,1)S(1)}, bf16[4,14,32,128]{3,2,1,0:T(8,128)(2,1)S(1)}, u32[]{:S(2)}, u32[]{:S(2)}) collective-permute-start(bf16[4,14,32,128]{3,2,1,0:T(8,128)(2,1)S(1)} %get-tuple-element.94), channel_id=1, source_target_pairs={{0,1},{1,0},{2,3},{3,2},{4,5},{5,4},{6,7},{7,6},{8,9},{9,8},{10,11... | collective-permute-start | bytes 1376264 | tf_op jit(solution)/shard_map/ppermute | solution.py:51
  74.5 22.1 %collective-permute-start.20 = (bf16[4,14,32,128]{3,2,1,0:T(8,128)(2,1)S(1)}, bf16[4,14,32,128]{3,2,1,0:T(8,128)(2,1)S(1)}, u32[]{:S(2)}, u32[]{:S(2)}) collective-permute-start(bf16[4,14,32,128]{3,2,1,0:T(8,128)(2,1)S(1)} %get-tuple-element.93), channel_id=1, source_target_pairs={{0,16},{1,17},{2,18},{3,19},{4,20},{5,21},{6,22},{7,23},{8,24},{9,... | collective-permute-start | bytes 1376264 | tf_op jit(solution)/shard_map/ppermute | solution.py:51
  75.4 10.1 %copy-start.2 = (bf16[16,16,8,256]{3,2,1,0:T(8,128)(2,1)S(1)}, bf16[16,16,8,256]{3,2,1,0:T(8,128)(2,1)}, u32[]{:S(2)}) copy-start(bf16[16,16,8,256]{3,2,1,0:T(8,128)(2,1)} %tile_ref.5) | copy-start | bytes 3145732
  75.4 21.2 %collective-permute-start.21 = (bf16[4,14,32,128]{3,2,1,0:T(8,128)(2,1)S(1)}, bf16[4,14,32,128]{3,2,1,0:T(8,128)(2,1)S(1)}, u32[]{:S(2)}, u32[]{:S(2)}) collective-permute-start(bf16[4,14,32,128]{3,2,1,0:T(8,128)(2,1)S(1)} %get-tuple-element.92), channel_id=1, source_target_pairs={{0,17},{1,16},{2,19},{3,18},{4,21},{5,20},{6,23},{7,22},{8,25},{9,... | collective-permute-start | bytes 1376264 | tf_op jit(solution)/shard_map/ppermute | solution.py:51
  82.6 8.5 %collective-permute-start.15 = (bf16[1,16,8,256]{3,2,1,0:T(8,128)(2,1)S(1)}, bf16[1,16,8,256]{3,2,1,0:T(8,128)(2,1)S(1)}, u32[]{:S(2)}, u32[]{:S(2)}) collective-permute-start(bf16[1,16,8,256]{3,2,1,0:T(8,128)(2,1)S(1)} %get-tuple-element.65), channel_id=1, source_target_pairs={{0,8},{8,16},{16,24},{1,9},{9,17},{17,25},{2,10},{10,18},{18,26},{... | collective-permute-start | bytes 196616 | tf_op jit(solution)/shard_map/ppermute | solution.py:451
  84.2 6.9 %collective-permute-start.16 = (bf16[1,16,8,256]{3,2,1,0:T(8,128)(2,1)S(1)}, bf16[1,16,8,256]{3,2,1,0:T(8,128)(2,1)S(1)}, u32[]{:S(2)}, u32[]{:S(2)}) collective-permute-start(bf16[1,16,8,256]{3,2,1,0:T(8,128)(2,1)S(1)} %get-tuple-element.66), channel_id=1, source_target_pairs={{8,0},{16,8},{24,16},{9,1},{17,9},{25,17},{10,2},{18,10},{26,18},{... | collective-permute-start | bytes 196616 | tf_op jit(solution)/shard_map/ppermute | solution.py:451
  96.6 8.7 %collective-permute-start.22 = (bf16[4,4,14,32,128]{4,3,2,1,0:T(8,128)(2,1)S(1)}, bf16[4,4,14,32,128]{4,3,2,1,0:T(8,128)(2,1)S(1)}, u32[]{:S(2)}, u32[]{:S(2)}) collective-permute-start(bf16[4,4,14,32,128]{4,3,2,1,0:T(8,128)(2,1)S(1)} %get-tuple-element.76), channel_id=1, source_target_pairs={{0,8},{1,9},{2,10},{3,11},{4,12},{5,13},{6,14},{7,15},{8,0},{9,1},... | collective-permute-start | bytes 5505032 | tf_op jit(solution)/shard_map/ppermute | solution.py:51
  97.2 8.1 %collective-permute-start.18 = (bf16[1,18,8,256]{3,2,1,0:T(8,128)(2,1)S(1)}, bf16[1,18,8,256]{3,2,1,0:T(8,128)(2,1)S(1)}, u32[]{:S(2)}, u32[]{:S(2)}) collective-permute-start(bf16[1,18,8,256]{3,2,1,0:T(8,128)(2,1)S(1)} %pad_maximum_fusion.4), channel_id=1, source_target_pairs={{1,0},{2,1},{3,2},{4,3},{5,4},{6,5},{7,6},{9,8},{10,9},{11,10},{12... | collective-permute-start | bytes 221192 | tf_op jit(solution)/shard_map/ppermute | solution.py:463
  98.5 6.8 %collective-permute-start.17 = (bf16[1,18,8,256]{3,2,1,0:T(8,128)(2,1)S(1)}, bf16[1,18,8,256]{3,2,1,0:T(8,128)(2,1)S(1)}, u32[]{:S(2)}, u32[]{:S(2)}) collective-permute-start(bf16[1,18,8,256]{3,2,1,0:T(8,128)(2,1)S(1)} %pad_maximum_fusion.3), channel_id=1, source_target_pairs={{0,1},{1,2},{2,3},{3,4},{4,5},{5,6},{6,7},{8,9},{9,10},{10,11},{11... | collective-permute-start | bytes 221192 | tf_op jit(solution)/shard_map/ppermute | solution.py:463
  105.3 1.8 %copy-start.5 = (bf16[4,4,14,32,128]{4,3,2,1,0:T(8,128)(2,1)}, bf16[4,4,14,32,128]{4,3,2,1,0:T(8,128)(2,1)S(1)}, u32[]{:S(2)}) copy-start(bf16[4,4,14,32,128]{4,3,2,1,0:T(8,128)(2,1)S(1)} %collective-permute-done.22) | copy-start | bytes 5505028
  107.0 26.9 %collective-permute-start.26 = (bf16[4,14,32,128]{3,2,1,0:T(8,128)(2,1)}, bf16[4,14,32,128]{3,2,1,0:T(8,128)(2,1)}, u32[]{:S(2)}, u32[]{:S(2)}) collective-permute-start(bf16[4,14,32,128]{3,2,1,0:T(8,128)(2,1)} %get-tuple-element.91), channel_id=1, source_target_pairs={{0,1},{1,0},{2,3},{3,2},{4,5},{5,4},{6,7},{7,6},{8,9},{9,8},{10,11... | collective-permute-start | bytes 1376264 | tf_op jit(solution)/shard_map/ppermute | solution.py:51
  109.2 24.7 %collective-permute-start.27 = (bf16[4,14,32,128]{3,2,1,0:T(8,128)(2,1)}, bf16[4,14,32,128]{3,2,1,0:T(8,128)(2,1)}, u32[]{:S(2)}, u32[]{:S(2)}) collective-permute-start(bf16[4,14,32,128]{3,2,1,0:T(8,128)(2,1)} %get-tuple-element.90), channel_id=1, source_target_pairs={{0,16},{1,17},{2,18},{3,19},{4,20},{5,21},{6,22},{7,23},{8,24},{9,... | collective-permute-start | bytes 1376264 | tf_op jit(solution)/shard_map/ppermute | solution.py:51
  110.5 23.4 %collective-permute-start.28 = (bf16[4,14,32,128]{3,2,1,0:T(8,128)(2,1)}, bf16[4,14,32,128]{3,2,1,0:T(8,128)(2,1)}, u32[]{:S(2)}, u32[]{:S(2)}) collective-permute-start(bf16[4,14,32,128]{3,2,1,0:T(8,128)(2,1)} %get-tuple-element.89), channel_id=1, source_target_pairs={{0,17},{1,16},{2,19},{3,18},{4,21},{5,20},{6,23},{7,22},{8,25},{9,... | collective-permute-start | bytes 1376264 | tf_op jit(solution)/shard_map/ppermute | solution.py:51
  110.6 7.2 %collective-permute-start.23 = (bf16[14,32,128]{2,1,0:T(8,128)(2,1)S(1)}, bf16[14,32,128]{2,1,0:T(8,128)(2,1)S(1)}, u32[]{:S(2)}, u32[]{:S(2)}) collective-permute-start(bf16[14,32,128]{2,1,0:T(8,128)(2,1)S(1)} %get-tuple-element.104), channel_id=1, source_target_pairs={{0,2},{1,3},{2,0},{3,1},{4,6},{5,7},{6,4},{7,5},{8,10},{9,11},{10,... | collective-permute-start | bytes 344072 | tf_op jit(solution)/shard_map/ppermute | solution.py:51
  113.9 9.5 %collective-permute-start.24 = (bf16[14,32,128]{2,1,0:T(8,128)(2,1)}, bf16[14,32,128]{2,1,0:T(8,128)(2,1)S(1)}, u32[]{:S(2)}, u32[]{:S(2)}) collective-permute-start(bf16[14,32,128]{2,1,0:T(8,128)(2,1)} %get-tuple-element.103), channel_id=1, source_target_pairs={{0,4},{1,5},{2,6},{3,7},{4,0},{5,1},{6,2},{7,3},{8,12},{9,13},{10,... | collective-permute-start | bytes 344072 | tf_op jit(solution)/shard_map/ppermute | solution.py:51
  117.8 7.0 %collective-permute-start.25 = (bf16[14,32,128]{2,1,0:T(8,128)(2,1)}, bf16[14,32,128]{2,1,0:T(8,128)(2,1)}, u32[]{:S(2)}, u32[]{:S(2)}) collective-permute-start(bf16[14,32,128]{2,1,0:T(8,128)(2,1)} %get-tuple-element.102), channel_id=1, source_target_pairs={{0,6},{1,7},{2,4},{3,5},{4,2},{5,3},{6,0},{7,1},{8,14},{9,15},{10,... | collective-permute-start | bytes 344072 | tf_op jit(solution)/shard_map/ppermute | solution.py:51
  124.8 2.0 %copy-start.3 = (bf16[1024,1792]{1,0:T(8,128)(2,1)S(1)}, bf16[1024,1792]{1,0:T(8,128)(2,1)}, u32[]{:S(2)}) copy-start(bf16[1024,1792]{1,0:T(8,128)(2,1)} %all-gather.3.cloned.1.call-done) | copy-start | bytes 11010052
  135.7 6.3 %collective-permute-start.29 = (bf16[14,32,128]{2,1,0:T(8,128)(2,1)S(1)}, bf16[14,32,128]{2,1,0:T(8,128)(2,1)S(1)}, u32[]{:S(2)}, u32[]{:S(2)}) collective-permute-start(bf16[14,32,128]{2,1,0:T(8,128)(2,1)S(1)} %get-tuple-element.99), channel_id=1, source_target_pairs={{0,2},{1,3},{2,0},{3,1},{4,6},{5,7},{6,4},{7,5},{8,10},{9,11},{10,... | collective-permute-start | bytes 344072 | tf_op jit(solution)/shard_map/ppermute | solution.py:51
  137.5 9.5 %collective-permute-start.30 = (bf16[14,32,128]{2,1,0:T(8,128)(2,1)S(1)}, bf16[14,32,128]{2,1,0:T(8,128)(2,1)S(1)}, u32[]{:S(2)}, u32[]{:S(2)}) collective-permute-start(bf16[14,32,128]{2,1,0:T(8,128)(2,1)S(1)} %get-tuple-element.101), channel_id=1, source_target_pairs={{0,4},{1,5},{2,6},{3,7},{4,0},{5,1},{6,2},{7,3},{8,12},{9,13},{10,... | collective-permute-start | bytes 344072 | tf_op jit(solution)/shard_map/ppermute | solution.py:51
  139.5 7.5 %collective-permute-start.31 = (bf16[14,32,128]{2,1,0:T(8,128)(2,1)S(1)}, bf16[14,32,128]{2,1,0:T(8,128)(2,1)S(1)}, u32[]{:S(2)}, u32[]{:S(2)}) collective-permute-start(bf16[14,32,128]{2,1,0:T(8,128)(2,1)S(1)} %get-tuple-element.100), channel_id=1, source_target_pairs={{0,6},{1,7},{2,4},{3,5},{4,2},{5,3},{6,0},{7,1},{8,14},{9,15},{10,... | collective-permute-start | bytes 344072 | tf_op jit(solution)/shard_map/ppermute | solution.py:51
Sparse Core Ops, SparseCore 0:
  12.0 68.8 all-gather.2

commit v3 on v2

--- a/solution.py
+++ b/solution.py
@@ -23,8 +23,8 @@
         self.rows = rows
         self.chans = chans
         self.cols = chans // n_gy
-        self.pair = 2 if n_gx % 2 == 0 else 1
-        self.inner = 2 if n_gy % 2 == 0 else 1
+        self.pair = 2
+        self.inner = 2
         self.n_y = n_gx // self.pair
         self.n_z = n_gy // self.inner
         self.n_plane = self.n_y * self.inner
@@ -82,9 +82,9 @@
     return jnp.where(inside, near, 1) * block[2]
 
 
-def load_extended(index, tile_ref, low_x, high_x, low_y, high_y, ext_ref, sems):
+def extended_copies(index, tile_ref, low_x, high_x, low_y, high_y, ext_ref, sems):
     size_x, size_y = tile_ref.shape[:2]
-    copies = [
+    return [
         pltpu.make_async_copy(
             tile_ref, ext_ref.at[pl.ds(1, size_x), pl.ds(1, size_y)], sems.at[0]
         ),
@@ -95,13 +95,17 @@
         pltpu.make_async_copy(low_y.at[index], ext_ref.at[:, 0], sems.at[3]),
         pltpu.make_async_copy(high_y.at[index], ext_ref.at[:, size_y + 1], sems.at[4]),
     ]
+
+
+def load_extended(*refs):
+    copies = extended_copies(*refs)
     for copy in copies:
         copy.start()
     for copy in copies:
         copy.wait()
 
 
-def spread_patches(occ_ref, blocks, ext_ref, shifted_ref, n_bx, n_by, rectify):
+def spread_patches(occ_ref, blocks, ext_ref, shifted_ref, n_bx, n_by):
     edge = B
     row = lax.broadcasted_iota(jnp.int32, (edge, ext_ref.shape[-1]), 0)
 
@@ -116,8 +120,6 @@
             planes = [[], [], []]
             for index, block in enumerate(blocks):
                 value = ext_ref[block[0] * edge + x, block[1] * edge + y].astype(jnp.float32)
-                if rectify:
-                    value = jnp.maximum(value, 0.0)
                 value = jnp.where(masks[index][side], value, 0.0)
                 below = jnp.where(row == 0, 0.0, pltpu.roll(value, 1, 0))
                 above = jnp.where(row == edge - 1, 0.0, pltpu.roll(value, edge - 1, 0))
@@ -130,63 +132,146 @@
     lax.fori_loop(0, edge + 2, at_x, 0)
 
 
-def gather_blocks(blocks, tile_ref, center_ref):
+def spread_rows(patch_ref, put):
     edge = B
+    row = lax.broadcasted_iota(jnp.int32, (AMAX * edge, patch_ref.shape[-1]), 0) % edge
 
     def at_x(x, carry):
-        for y in range(edge):
-            parts = []
-            for block in blocks:
-                value = tile_ref[block[0] * edge + x, block[1] * edge + y].astype(jnp.float32)
-                parts.append(jnp.where(block[2] > 0, value, 0.0))
-            center_ref[x, y] = jnp.concatenate(parts, axis=0).astype(jnp.bfloat16)
+        for y in range(edge + 2):
+            kept = patch_ref[x, y]
+            value = kept.astype(jnp.float32)
+            below = jnp.where(row == 0, 0.0, pltpu.roll(value, 1, 0))
+            above = jnp.where(row == edge - 1, 0.0, pltpu.roll(value, AMAX * edge - 1, 0))
+            put(0, x, y, below.astype(jnp.bfloat16))
+            put(1, x, y, kept)
+            put(2, x, y, above.astype(jnp.bfloat16))
         return carry
 
-    lax.fori_loop(0, edge, at_x, 0)
-
-
-def window(shifted_ref, plane, start_x, start_y):
+    lax.fori_loop(0, edge + 2, at_x, 0)
+
+
+def patch_kernel(n_bx, n_by, occ_ref, *rest):
+    tile_refs = rest[:3]
+    low_x, high_x, low_y, high_y = rest[3:7]
+    patches_ref, ext_ref, sems = rest[7:]
     edge = B
-    piece = shifted_ref[plane, start_x : start_x + edge, start_y : start_y + edge]
+    blocks = pick_blocks(occ_ref, n_bx, n_by)
+    copies = []
+    for index, tile_ref in enumerate(tile_refs):
+        copies.append(
+            extended_copies(
+                index, tile_ref, low_x, high_x, low_y, high_y, ext_ref.at[index], sems.at[index]
+            )
+        )
+    for group in copies:
+        for copy in group:
+            copy.start()
+    for index in range(len(tile_refs)):
+        for copy in copies[index]:
+            copy.wait()
+
+        def at_x(x, carry, index=index):
+            step_x = jnp.where(x == 0, -1, jnp.where(x == edge + 1, 1, 0))
+            masks = [
+                [
+                    block_mask(occ_ref, block, step_x, step_y, n_bx, n_by) > 0
+                    for step_y in (-1, 0, 1)
+                ]
+                for block in blocks
+            ]
+            for y in range(edge + 2):
+                side = 0 if y == 0 else (2 if y == edge + 1 else 1)
+                parts = []
+                for slot, block in enumerate(blocks):
+                    value = ext_ref[index, block[0] * edge + x, block[1] * edge + y]
+                    value = value.astype(jnp.float32)
+                    if index == 0:
+                        value = jnp.maximum(value, 0.0)
+                    parts.append(jnp.where(masks[slot][side], value, 0.0))
+                patches_ref[index, x, y] = jnp.concatenate(parts, axis=0).astype(jnp.bfloat16)
+            return carry
+
+        lax.fori_loop(0, edge + 2, at_x, 0)
+
+
+def patches_of(occ, fields, edges, n_bx, n_by):
+    size_x, size_y, edge, chans = fields[0].shape
+    anywhere = pl.BlockSpec(memory_space=pl.ANY)
+    vmem = pl.BlockSpec(memory_space=pltpu.VMEM)
+    shape = (len(fields), B + 2, B + 2, AMAX * B, chans)
+    return pl.pallas_call(
+        functools.partial(patch_kernel, n_bx, n_by),
+        out_shape=jax.ShapeDtypeStruct(shape, jnp.bfloat16),
+        in_specs=[pl.BlockSpec(memory_space=pltpu.SMEM)] + [anywhere] * 7,
+        out_specs=vmem,
+        scratch_shapes=[
+            pltpu.VMEM((3, size_x + 2, size_y + 2, edge, chans), jnp.bfloat16),
+            pltpu.SemaphoreType.DMA((3, 5)),
+        ],
+        compiler_params=pltpu.CompilerParams(vmem_limit_bytes=40 * 1024 * 1024),
+        cost_estimate=SMALL,
+    )(occ, *fields, *edges)
+
+
+def window(shifted_ref, plane, start_x, start_y, lanes=slice(None)):
+    edge = B
+    piece = shifted_ref[plane, start_x : start_x + edge, start_y : start_y + edge, :, lanes]
     return piece.reshape(edge * edge * AMAX * edge, piece.shape[-1])
 
 
-def weight_kernel(
-    plan, n_bx, n_by, index, rectify, compact,
-    occ_ref, tile_ref, low_x, high_x, low_y, high_y, grad_ref,
-    *rest,
-):
-    *out_refs, ext_ref, shifted_ref, center_ref, turned_ref, sems = rest
-    blocks = pick_blocks(occ_ref, n_bx, n_by)
-    load_extended(index, tile_ref, low_x, high_x, low_y, high_y, ext_ref, sems)
-    spread_patches(occ_ref, blocks, ext_ref, shifted_ref, n_bx, n_by, rectify)
-    if compact:
-        center = grad_ref[...]
-    else:
-        gather_blocks(blocks, grad_ref, center_ref)
-        center = center_ref[...]
+def weight_kernel(plan, field, own_ref, other_ref, *rest):
+    *center_refs, out_ref, shifted_ref, turned_ref = rest
     voxels = B * B * AMAX * B
-    turned_ref[...] = center.reshape(voxels, plan.chans).astype(jnp.float32).T.astype(jnp.bfloat16)
+    pair = (own_ref, other_ref)
+    for index, patch_ref in enumerate(pair):
+
+        def put(j, x, y, rows, index=index):
+            shifted_ref[index, j, x, y] = rows
+
+        spread_rows(patch_ref.at[field], put)
+        if center_refs:
+            center = center_refs[index][...]
+        else:
+            center = patch_ref[2, 1 : B + 1, 1 : B + 1]
+        turned = center.reshape(voxels, plan.chans).astype(jnp.float32).T
+        turned_ref[:, index * voxels : (index + 1) * voxels] = turned.astype(jnp.bfloat16)
     my_gx = lax.axis_index("gx")
     my_gy = lax.axis_index("gy")
     my_core = my_gx % plan.pair
     my_y = my_gx // plan.pair
     my_x = my_gy % plan.inner
     my_z = my_gy // plan.inner
-    per_column = 3 * plan.chans // LANES
+    halves = plan.chans // LANES
+
+    def taps(tile):
+        column, j = divmod(tile // halves, 3)
+        shift_x, shift_y = stencil_columns[column]
+        lanes = slice(tile % halves * LANES, (tile % halves + 1) * LANES)
+        return jnp.concatenate(
+            [
+                window(shifted_ref.at[index], j, 1 + shift_x, 1 + shift_y, lanes)
+                for index in range(len(pair))
+            ],
+            axis=0,
+        )
 
     def products(core_here):
-        for column, (shift_x, shift_y) in enumerate(stencil_columns):
-            pieces = [window(shifted_ref, j, 1 + shift_x, 1 + shift_y) for j in range(3)]
+        places = []
+        for tile in range(plan.tiles):
+            mine = [owner for owner in plan.owners(tile) if owner[0] % plan.pair == core_here]
+            if mine:
+                places.append((tile, mine))
+        at_once = 6
+        for begin in range(0, len(places), at_once):
+            group = places[begin : begin + at_once]
             product = jnp.dot(
                 turned_ref[...],
-                jnp.concatenate(pieces, axis=1),
+                jnp.concatenate([taps(tile) for tile, _ in group], axis=1),
                 preferred_element_type=jnp.float32,
             ).astype(jnp.bfloat16)
-            for part in range(per_column):
+            for part, (_, mine) in enumerate(group):
                 lanes = product[:, part * LANES : (part + 1) * LANES]
-                for shard, place in plan.owners(column * per_column + part):
-                    out_ref = out_refs[(shard % plan.pair) ^ core_here]
+                for shard, place in mine:
                     y = (shard // plan.pair) ^ my_y
                     for j in range(plan.n_gy):
                         slot = y * plan.inner + ((j % plan.inner) ^ my_x)
@@ -197,36 +282,30 @@
         pl.when(my_core == core_here)(functools.partial(products, core_here))
 
 
-def weight_sums(plan, occ, tile, rim, index, grad, n_bx, n_by, rectify, compact):
-    size_x, size_y, edge, chans = tile.shape
-    smem = pl.BlockSpec(memory_space=pltpu.SMEM)
-    anywhere = pl.BlockSpec(memory_space=pl.ANY)
+def weight_sums(plan, field, own, other, centers=()):
+    chans = plan.chans
     vmem = pl.BlockSpec(memory_space=pltpu.VMEM)
     voxels = B * B * AMAX * B
     shape = (plan.n_plane, plan.n_z, plan.depth, plan.cols, LANES)
     return pl.pallas_call(
-        functools.partial(weight_kernel, plan, n_bx, n_by, index, rectify, compact),
-        out_shape=[jax.ShapeDtypeStruct(shape, jnp.bfloat16)] * plan.pair,
-        in_specs=[smem] + [anywhere] * 5 + [vmem],
-        out_specs=[vmem] * plan.pair,
+        functools.partial(weight_kernel, plan, field),
+        out_shape=jax.ShapeDtypeStruct(shape, jnp.bfloat16),
+        in_specs=[vmem] * (2 + len(centers)),
+        out_specs=vmem,
         scratch_shapes=[
-            pltpu.VMEM((size_x + 2, size_y + 2, edge, chans), jnp.bfloat16),
-            pltpu.VMEM((3, B + 2, B + 2, AMAX * B, chans), jnp.bfloat16),
-            pltpu.VMEM((B, B, AMAX * B, chans), jnp.bfloat16),
-            pltpu.VMEM((chans, voxels), jnp.bfloat16),
-            pltpu.SemaphoreType.DMA((5,)),
+            pltpu.VMEM((plan.pair, 3, B + 2, B + 2, AMAX * B, chans), jnp.bfloat16),
+            pltpu.VMEM((chans, plan.pair * voxels), jnp.bfloat16),
         ],
         compiler_params=pltpu.CompilerParams(vmem_limit_bytes=40 * 1024 * 1024),
         cost_estimate=SMALL,
-    )(occ, tile, *rim, grad)
-
-
-def data_kernel(
-    plan, n_bx, n_by, index, gated, n_pieces,
-    occ_ref, tile_ref, low_x, high_x, low_y, high_y, *rest,
-):
-    piece_refs = rest[:n_pieces]
-    rest = rest[n_pieces:]
+    )(own, other, *centers)
+
+
+def data_kernel(plan, n_bx, n_by, n_sources, gated, distances, occ_ref, *rest):
+    source_refs = rest[:n_sources]
+    rest = rest[n_sources:]
+    piece_refs = rest[: len(distances)]
+    rest = rest[len(distances) :]
     if gated:
         gate_ref, out_ref, center_ref = rest[:3]
         rest = rest[3:]
@@ -238,23 +317,19 @@
     blocks = pick_blocks(occ_ref, n_bx, n_by)
     my_gx = lax.axis_index("gx")
     my_gy = lax.axis_index("gy")
-    if n_pieces == 1:
-        for shard in range(plan.n_gx):
-            for column in range(plan.n_gy):
-                weight_ref[shard, column * plan.cols : (column + 1) * plan.cols] = piece_refs[0][
-                    shard * plan.n_gy + column
-                ]
+    for piece_ref, flips in zip(piece_refs, distances):
+        for place, (flip_gx, flip_gy) in enumerate(flips):
+            start = pl.multiple_of((my_gy ^ flip_gy) * plan.cols, plan.cols)
+            weight_ref[my_gx ^ flip_gx, pl.ds(start, plan.cols)] = piece_ref[place]
+    if n_sources == 1:
+
+        def put(j, x, y, rows):
+            shifted_ref[j, x, y] = rows
+
+        spread_rows(source_refs[0].at[2], put)
     else:
-        for piece in range(n_pieces):
-            core = piece // plan.n_plane
-            slot = piece % plan.n_plane
-            shard = my_gx ^ (slot // plan.inner * plan.pair + core)
-            for z in range(plan.n_z):
-                column = my_gy ^ (z * plan.inner + slot % plan.inner)
-                start = pl.multiple_of(column * plan.cols, plan.cols)
-                weight_ref[shard, pl.ds(start, plan.cols)] = piece_refs[piece][z]
-    load_extended(index, tile_ref, low_x, high_x, low_y, high_y, ext_ref, sems)
-    spread_patches(occ_ref, blocks, ext_ref, shifted_ref, n_bx, n_by, False)
+        load_extended(0, *source_refs, ext_ref, sems)
+        spread_patches(occ_ref, blocks, ext_ref, shifted_ref, n_bx, n_by)
     out_ref[...] = jnp.zeros_like(out_ref)
 
     def kernel_lanes(tile):
@@ -306,20 +381,20 @@
     lax.fori_loop(0, edge, at_x, 0)
 
 
-def data_grad(plan, occ, tile, rim, index, pieces, n_bx, n_by, gate=None):
-    size_x, size_y, edge, chans = tile.shape
+def data_grad(plan, occ, shape, sources, pieces, distances, n_bx, n_by, gate=None):
+    size_x, size_y, edge, chans = shape
     smem = pl.BlockSpec(memory_space=pltpu.SMEM)
-    anywhere = pl.BlockSpec(memory_space=pl.ANY)
     vmem = pl.BlockSpec(memory_space=pltpu.VMEM)
+    source = vmem if len(sources) == 1 else pl.BlockSpec(memory_space=pl.ANY)
     voxels = B * B * AMAX * B
     gated = gate is not None
-    out_shape = [jax.ShapeDtypeStruct(tile.shape, jnp.bfloat16)]
+    out_shape = [jax.ShapeDtypeStruct(shape, jnp.bfloat16)]
     if gated:
         out_shape.append(jax.ShapeDtypeStruct((B, B, AMAX * B, chans), jnp.bfloat16))
     return pl.pallas_call(
-        functools.partial(data_kernel, plan, n_bx, n_by, index, gated, len(pieces)),
+        functools.partial(data_kernel, plan, n_bx, n_by, len(sources), gated, distances),
         out_shape=out_shape,
-        in_specs=[smem] + [anywhere] * 5 + [vmem] * (len(pieces) + gated),
+        in_specs=[smem] + [source] * len(sources) + [vmem] * (len(pieces) + gated),
         out_specs=[vmem] * len(out_shape),
         scratch_shapes=[
             pltpu.VMEM((size_x + 2, size_y + 2, edge, chans), jnp.bfloat16),
@@ -330,7 +405,7 @@
         ],
         compiler_params=pltpu.CompilerParams(vmem_limit_bytes=40 * 1024 * 1024),
         cost_estimate=SMALL,
-    )(occ, tile, *rim, *pieces, *([gate] if gated else []))
+    )(occ, *sources, *pieces, *([gate] if gated else []))
 
 
 def after(x, *others):
@@ -400,40 +475,117 @@
     )(occ, weight_two.T, weight_one.T, *fields)
 
 
-def gather_line(plan, own):
-    return jnp.stack([own] + [swap_z(own, plan, slot) for slot in range(1, plan.n_z)])
-
-
-def gather_plane(plan, line):
-    return [line] + [swap_plane(line, plan, slot) for slot in range(1, plan.n_plane)]
-
-
-def gather_pair(plan, plane):
-    return [swap(part, plan, 1, 0) for part in plane] if plan.pair == 2 else []
-
-
-def reduce_pair(plan, sums):
-    total = [sums[0][slot].astype(jnp.float32) for slot in range(plan.n_plane)]
-    if plan.pair == 2:
-        got = swap(sums[1], plan, 1, 0)
-        total = [total[slot] + got[slot].astype(jnp.float32) for slot in range(plan.n_plane)]
-    return [total[0]] + [part.astype(jnp.bfloat16) for part in total[1:]]
-
-
-def swap_parts(plan, parts, swap_one):
-    return [swap_one(parts[slot], plan, slot) for slot in range(1, len(parts))]
-
-
-def reduce_plane(plan, own, got):
-    line = own
-    for part in got:
-        line = line + part.astype(jnp.float32)
-    return [line[0]] + [line[slot].astype(jnp.bfloat16) for slot in range(1, plan.n_z)]
-
-
-def reduce_z(plan, own, got):
-    for part in got:
+class Gathered:
+    def __init__(self, array, distances):
+        self.array = array
+        self.distances = distances
+
+    def from_others(self, plan, flips):
+        return [
+            Gathered(
+                swap(self.array, plan, flip_gx, flip_gy),
+                [(i ^ flip_gx, j ^ flip_gy) for i, j in self.distances],
+            )
+            for flip_gx, flip_gy in flips
+        ]
+
+    def joined(self, others):
+        parts = [self] + others
+        return Gathered(
+            jnp.concatenate([part.array for part in parts], axis=0),
+            [distance for part in parts for distance in part.distances],
+        )
+
+    def part(self, start, stop):
+        return Gathered(self.array[start:stop], self.distances[start:stop])
+
+    def after(self, *others):
+        return Gathered(after(self.array, *others), self.distances)
+
+
+def plane_flips(plan):
+    return [
+        (slot // plan.inner * plan.pair, slot % plan.inner) for slot in range(1, plan.n_plane)
+    ]
+
+
+def z_steps(plan):
+    step = plan.n_z // 2
+    while step > 0:
+        yield [(0, step * plan.inner)]
+        step //= 2
+
+
+def both_cores(plan, gathered):
+    return [gathered] + gathered.from_others(plan, [(1, 0)])
+
+
+class Halving:
+    def __init__(self, plan, sums):
+        self.plan = plan
+        bits = [1 << i for i in range(plan.n_plane.bit_length() - 1)]
+        self.orders = [bits, bits[1:] + bits[:1]]
+        half = plan.n_z // 2
+        self.slots = [list(range(plan.n_plane))] * 2
+        self.parts = [sums[:, :half], sums[:, half:]]
+        self.step = 0
+
+    def sends(self):
+        out = []
+        for half in range(2):
+            bit = self.orders[half][self.step]
+            away = [i for i, slot in enumerate(self.slots[half]) if slot & bit]
+            out.append(take(self.parts[half], away).astype(jnp.bfloat16))
+        return out
+
+    def swaps(self, sends):
+        out = []
+        for half in range(2):
+            slot = self.orders[half][self.step]
+            plan = self.plan
+            out.append(
+                swap(sends[half], plan, slot // plan.inner * plan.pair, slot % plan.inner)
+            )
+        return out
+
+    def add(self, got):
+        for half in range(2):
+            bit = self.orders[half][self.step]
+            stay = [i for i, slot in enumerate(self.slots[half]) if not slot & bit]
+            kept = take(self.parts[half], stay).astype(jnp.float32)
+            self.parts[half] = kept + got[half].astype(jnp.float32)
+            self.slots = list(self.slots)
+            self.slots[half] = [self.slots[half][i] for i in stay]
+        self.step += 1
+
+    def done(self):
+        return self.step == len(self.orders[0])
+
+    def line(self):
+        return jnp.concatenate([part[0] for part in self.parts], axis=0)
+
+
+def take(array, indices):
+    return jnp.concatenate([array[i : i + 1] for i in indices], axis=0)
+
+
+def halve_z_step(plan, line):
+    step = line.shape[0] // 2
+    got = swap_z(line[step:].astype(jnp.bfloat16), plan, step)
+    return line[:step].astype(jnp.float32) + got.astype(jnp.float32)
+
+
+def spread_z(plan, line, *before):
+    got = [
+        swap_z(line[slot].astype(jnp.bfloat16), plan, slot) for slot in range(1, plan.n_z)
+    ]
+    own = line[0]
+    for part in after(got, *before):
         own = own + part.astype(jnp.float32)
+    return own
+
+
+def finished(plan, own):
     scale = float(plan.n_gx * plan.n_gy * B**3) ** (-0.5)
     flat = (own * scale).transpose(1, 0, 2).reshape(plan.cols, plan.depth * LANES)
     offset = lax.axis_index("gx") * plan.rows % LANES
@@ -473,38 +625,74 @@
     own_two, own_one, first_x, last_x, first_y, last_y = first_steps(
         plan, occ, weight_two, weight_one, (preact, inputs, out_grad), n_bx, n_by
     )
-    pieces_one = [lax.all_gather(own_one, BOTH, axis=0)]
     low_x, high_x = rims_x(first_x, last_x)
-    sent_y = strips_y(low_x, high_x, first_y, last_y)
-    edges = (low_x, high_x) + rims_y(*sent_y)
-    line = after(gather_line(plan, own_two), edges)
-    sums_two = weight_sums(plan, occ, preact, edges, 0, out_grad, n_bx, n_by, True, False)
-    plane = gather_plane(plan, line)
-    sums_two = [sums_two[0]] + list(after(sums_two[1:], plane))
-    plane_two = reduce_pair(plan, sums_two)
-    pieces_two = after(plane + gather_pair(plan, plane), plane_two)
+    steps = list(z_steps(plan))
+    two = Gathered(own_two[None], [(0, 0)])
+    for flips in steps[:-1]:
+        two = two.joined(two.from_others(plan, flips))
+    sent_y = after(strips_y(low_x, high_x, first_y, last_y), two.array)
+    for flips in steps[-1:]:
+        two = two.joined(two.from_others(plan, flips))
+    one = Gathered(own_one[None], [(0, 0)]).after(low_x, high_x)
+    one = one.joined(one.from_others(plan, plane_flips(plan)))
+    edges = after((low_x, high_x) + rims_y(*sent_y), one.array, two.array)
+    two = two.after(edges)
+    patches = patches_of(occ, (preact, inputs, out_grad), edges, n_bx, n_by)
+    other = swap(patches, plan, 1, 0)
+    sums_two = weight_sums(plan, 0, patches, other)
+    for flips in steps[:-1]:
+        one = one.joined([part.after(sums_two) for part in one.from_others(plan, flips)])
+    others = two.from_others(plan, plane_flips(plan))
+    two = two.joined([part.after(sums_two) for part in others]).after(one.array)
+    halving_two = Halving(plan, sums_two)
+    sends = after(halving_two.sends(), two.array)
+    got_two = halving_two.swaps(sends)
+    pieces = both_cores(plan, two)
     grad_one, center = data_grad(
-        plan, occ, out_grad, edges, 2, pieces_two, n_bx, n_by, preact
+        plan, occ, inputs.shape, [patches], after([part.array for part in pieces], sends),
+        [part.distances for part in pieces], n_bx, n_by, preact,
     )
-
+    other_center = swap(center, plan, 1, 0)
+    halving_two.add(after(got_two, grad_one))
+    while not halving_two.done():
+        sends = halving_two.sends()
+        got_two = halving_two.swaps(sends)
+        if halving_two.step + 1 == len(halving_two.orders[0]):
+            sums_one = weight_sums(plan, 1, patches, other, (after(center, sends), other_center))
+            got_two = after(got_two, sums_one)
+        halving_two.add(got_two)
+    for flips in steps[-1:]:
+        others = one.after(two.array).from_others(plan, flips)
+        one = one.joined([part.after(sums_one) for part in others])
+    line_two = halving_two.line()
+
+    halving_one = Halving(plan, after(sums_one, got_two))
+    sends = halving_one.sends()
+    got_one = halving_one.swaps(sends)
+    line_two = halve_z_step(plan, after(line_two, sends))
     strips = (grad_one[None, 0], grad_one[None, -1], grad_one[None, :, 0], grad_one[None, :, -1])
-    center, strips = lax.optimization_barrier((center, strips))
-    sums_one = weight_sums(plan, occ, inputs, edges, 1, center, n_bx, n_by, False, True)
-    got_two = after(swap_parts(plan, plane_two, swap_plane), sums_one)
-    low_x, high_x = after(rims_x(*strips[:2]), sums_one)
-    sums_one = [sums_one[0]] + list(after(sums_one[1:], got_two, low_x, high_x))
-    edges_one = (low_x, high_x) + rims_y(*strips_y(low_x, high_x, *strips[2:]))
-    line_two = reduce_plane(plan, plane_two[0], got_two)
-    sums_one = after(sums_one[:1], edges_one, line_two) + sums_one[1:]
-    plane_one = reduce_pair(plan, sums_one)
-    got = swap_parts(plan, line_two, swap_z)
-    grad_one = after(grad_one, plane_one, got)
-    (input_grad,) = data_grad(plan, occ, grad_one, edges_one, 0, pieces_one, n_bx, n_by)
-    own_two = reduce_z(plan, line_two[0], after(got, input_grad))
-    got_one = after(swap_parts(plan, plane_one, swap_plane), input_grad)
-    line_one = reduce_plane(plan, plane_one[0], got_one)
-    own_one = reduce_z(plan, line_one[0], swap_parts(plan, line_one, swap_z))
-    return (input_grad, own_one, own_two)
+    strips = after(strips, sends)
+    low_x, high_x = rims_x(*strips[:2])
+    sent_y = strips_y(low_x, high_x, *strips[2:])
+    halving_one.add(after(got_one, sent_y))
+    while not halving_one.done():
+        sends = halving_one.sends()
+        got_one = halving_one.swaps(sends)
+        if halving_one.step + 1 == len(halving_one.orders[0]):
+            edges_one = (low_x, high_x) + rims_y(*after(sent_y, sends))
+            line_two = after(line_two, sends)
+            while line_two.shape[0] > 1:
+                line_two = halve_z_step(plan, line_two)
+            got_one = after(got_one, edges_one)
+        halving_one.add(got_one)
+    line_one = halving_one.line()
+    pieces = both_cores(plan, one)
+    (input_grad,) = data_grad(
+        plan, occ, inputs.shape, (after(grad_one, line_one),) + edges_one,
+        [part.array for part in pieces], [part.distances for part in pieces], n_bx, n_by,
+    )
+    own_one = spread_z(plan, line_one, input_grad)
+    return (input_grad, finished(plan, own_one), finished(plan, line_two[0]))
 
 
 def solution(mesh):

time: 156 us -> 136 us (0.87)
  between operations: 14.4 us -> 1.19 us
  waiting for transfers between devices: 45.2 us -> 39.1 us
  other arithmetic: 9.1 us -> 5.92 us
  Pallas kernels: 28.1 us -> 30.9 us
    ppermute x24 -> x27, waiting for transfers between devices: 36.6 us -> 27.1 us  [swap(): return lax.ppermute(x, BOTH, pairs)]
    ppermute x4, waiting for transfers between devices: 5.57 us -> 12.1 us  [rims_y(): return (lax.ppermute(last_y, 'gy', up), lax.ppermute(first_y, 'gy', down))]
    ppermute x24 -> x27, starting transfers between devices: 33.5 us -> 36.6 us  [swap(): return lax.ppermute(x, BOTH, pairs)]
    ppermute x4, waiting for transfers between devices: 2.97 us -> 0.01 us  [rims_x(): return (lax.ppermute(last_x, 'gx', up), lax.ppermute(first_x, 'gx', down))]
    pallas_call x4 -> x5, Pallas kernels: 24.8 us -> 27.7 us  [the longest x2 14.2 us: data_grad(): pl.pallas_call(functools.partial(data_kernel, plan, n_bx, n_by, len(sourc...]
    another operation x3 -> x1, other arithmetic: 3.97 us -> 1.09 us
    slice x3 -> x12, local copies, waits for them, and re-layouts: 0.01 us -> 2.5 us  [the longest x6 1.8 us: take(): return jnp.concatenate([array[i:i + 1] for i in indices], axis=0)]
    ppermute x4, starting transfers between devices: 11.9 us -> 9.49 us  [rims_y(): return (lax.ppermute(last_y, 'gy', up), lax.ppermute(first_y, 'gy', down))]
  transfers between devices with their start and end apart: 33 -> 35, of which waited for: 11 -> 14; matrix products, arithmetic and copies ran while one was open for 6% -> 8% of each run, Pallas kernels for 16% -> 18%
where the time goes in v3:
time: 136 us
  starting transfers between devices  51.4 us (38%)
  waiting for transfers between devices  39.1 us (29%)
  Pallas kernels  30.9 us (23%)
  local copies, waits for them, and re-layouts  7.07 us (5%)
  other arithmetic  5.92 us (4%)
    ppermute x27, starting transfers between devices, swap(): return lax.ppermute(x, BOTH, pairs)  36.6 us
    ppermute x27, waiting for transfers between devices, swap(): return lax.ppermute(x, BOTH, pairs)  27.1 us
    pallas_call x2, Pallas kernels, data_grad(): pl.pallas_call(functools.partial(data_kernel, plan, n_bx, n_by, len(sourc...  14.2 us
    ppermute x4, waiting for transfers between devices, rims_y(): return (lax.ppermute(last_y, 'gy', up), lax.ppermute(first_y, 'gy', down))  12.1 us
    pallas_call x2, Pallas kernels, weight_sums(): pl.pallas_call(functools.partial(weight_kernel, plan, field), out_shape=j...  10.8 us
    ppermute x4, starting transfers between devices, rims_y(): return (lax.ppermute(last_y, 'gy', up), lax.ppermute(first_y, 'gy', down))  9.49 us
    ppermute x4, starting transfers between devices, rims_x(): return (lax.ppermute(last_x, 'gx', up), lax.ppermute(first_x, 'gx', down))  5.32 us
    pallas_call x1, Pallas kernels, first_steps(): pl.pallas_call(functools.partial(first_kernel, plan, n_bx, n_by), out_sha...  3.21 us
  transfers between devices with their start and end apart: 35, of which 14 were waited for; matrix products, arithmetic and copies ran while one was open for 8% of the time, Pallas kernels for 18%

profile of v3, /device:TPU:0, one launch (start us, length us, event | category | flops | bytes accessed | tf_op | source)
XLA Modules:
  0.0 135.6 jit_solution(8213633456949826953)
XLA Ops:
  0.6 1.4 %copy.20.occ_ref = s32[2,2,1]{2,1,0:T(2,128)} copy(s32[2,2,1]{1,2,0:T(1,128)} %param.11) | data formatting | bytes 32 | tf_op args[5]
  2.0 3.2 %shard_map.85 = (bf16[32,1792]{1,0:T(8,128)(2,1)}, bf16[32,1792]{1,0:T(8,128)(2,1)}, bf16[3,16,8,256]{3,2,1,0:T(8,128)(2,1)}, bf16[3,16,8,256]{3,2,1,0:T(8,128)(...) custom-call(s32[2,2,1]{2,1,0:T(2,128)} %copy.20.occ_ref, bf16[32,1728]{1,0:T(8,128)(2,1)} %bitcast.56, ...), custom_call_target="tpu_custom_call" | custom-call | flops 1 | bytes 1 | tf_op jit(solution)/shard_map/pallas_call | solution.py:465
  5.2 4.1 %collective-permute-start.2 = (bf16[1,32,1792]{2,1,0:T(8,128)(2,1)}, bf16[1,32,1792]{2,1,0:T(8,128)(2,1)S(1)}, u32[]{:S(2)}, u32[]{:S(2)}) collective-permute-start(bf16[1,32,1792]{2,1,0:T(8,128)(2,1)} %bitcast.49), channel_id=1, source_target_pairs={{0,4},{1,5},{2,6},{3,7},{4,0},{5,1},{6,2},{7,3},{8,12},{9,13},{10,... | collective-permute-start | bytes 344072 | tf_op jit(solution)/shard_map/ppermute | solution.py:51
  9.3 1.5 %collective-permute-start = (bf16[3,16,8,256]{3,2,1,0:T(8,128)(2,1)}, bf16[3,16,8,256]{3,2,1,0:T(8,128)(2,1)S(1)}, u32[]{:S(2)}, u32[]{:S(2)}) collective-permute-start(bf16[3,16,8,256]{3,2,1,0:T(8,128)(2,1)} %get-tuple-element.51), channel_id=1, source_target_pairs={{0,8},{8,16},{16,24},{1,9},{9,17},{17,25},{2,10},{10,18},{18,26},{... | collective-permute-start | bytes 589832 | tf_op jit(solution)/shard_map/ppermute | solution.py:603
  10.8 1.3 collective-permute-start.1
  12.1 3.0 %collective-permute-done.2 = bf16[1,32,1792]{2,1,0:T(8,128)(2,1)S(1)} collective-permute-done((bf16[1,32,1792]{2,1,0:T(8,128)(2,1)}, bf16[1,32,1792]{2,1,0:T(8,128)(2,1)S(1)}, u32[]{:S(2)}, u32[]{:S(2)}) %collective-permute-start.2) | collective-permute-done | bytes 114720 | tf_op jit(solution)/shard_map/ppermute | solution.py:51
  15.1 0.9 pad_maximum_fusion.5
  16.1 0.9 collective-permute-start.8
  17.0 1.1 constant_dynamic-update-slice_fusion.14
  18.1 1.6 %collective-permute-start.5 = (bf16[1,32,1792]{2,1,0:T(8,128)(2,1)}, bf16[1,32,1792]{2,1,0:T(8,128)(2,1)S(1)}, u32[]{:S(2)}, u32[]{:S(2)}) collective-permute-start(bf16[1,32,1792]{2,1,0:T(8,128)(2,1)} %bitcast.53), channel_id=1, source_target_pairs={{0,1},{1,0},{2,3},{3,2},{4,5},{5,4},{6,7},{7,6},{8,9},{9,8},{10,11... | collective-permute-start | bytes 344072 | tf_op jit(solution)/shard_map/ppermute | solution.py:51
  19.6 2.9 %collective-permute-start.6 = (bf16[1,32,1792]{2,1,0:T(8,128)(2,1)}, bf16[1,32,1792]{2,1,0:T(8,128)(2,1)S(1)}, u32[]{:S(2)}, u32[]{:S(2)}) collective-permute-start(bf16[1,32,1792]{2,1,0:T(8,128)(2,1)} %bitcast.54), channel_id=1, source_target_pairs={{0,16},{1,17},{2,18},{3,19},{4,20},{5,21},{6,22},{7,23},{8,24},{9,... | collective-permute-start | bytes 344072 | tf_op jit(solution)/shard_map/ppermute | solution.py:51
  22.5 1.1 pad_maximum_fusion.6
  23.6 3.4 %collective-permute-start.3 = (bf16[3,18,8,256]{3,2,1,0:T(8,128)(2,1)S(1)}, bf16[3,18,8,256]{3,2,1,0:T(8,128)(2,1)S(1)}, u32[]{:S(2)}, u32[]{:S(2)}) collective-permute-start(bf16[3,18,8,256]{3,2,1,0:T(8,128)(2,1)S(1)} %get-tuple-element.56), channel_id=1, source_target_pairs={{0,1},{1,2},{2,3},{3,4},{4,5},{5,6},{6,7},{8,9},{9,10},{10,11},{11... | collective-permute-start | bytes 663560 | tf_op jit(solution)/shard_map/ppermute | solution.py:615
  27.0 1.3 collective-permute-start.4
  28.4 0.6 collective-permute-done.7
  29.1 3.1 %collective-permute-done.3.rest_5_ = bf16[3,18,8,256]{3,2,1,0:T(8,128)(2,1)S(1)} collective-permute-done((bf16[3,18,8,256]{3,2,1,0:T(8,128)(2,1)S(1)}, bf16[3,18,8,256]{3,2,1,0:T(8,128)(2,1)S(1)}, u32[]{:S(2)}, u32[]{:S(2)}) %collective-permute-start.3) | collective-permute-done | bytes 221216 | tf_op jit(solution)/shard_map/ppermute | solution.py:615
  32.2 4.7 %collective-permute-done.4.rest_6_ = bf16[3,18,8,256]{3,2,1,0:T(8,128)(2,1)S(1)} collective-permute-done((bf16[3,18,8,256]{3,2,1,0:T(8,128)(2,1)S(1)}, bf16[3,18,8,256]{3,2,1,0:T(8,128)(2,1)S(1)}, u32[]{:S(2)}, u32[]{:S(2)}) %collective-permute-start.4) | collective-permute-done | bytes 221216 | tf_op jit(solution)/shard_map/ppermute | solution.py:615
  36.9 2.7 %shard_map.86.own_ref.rest_0_ = bf16[3,10,10,16,256]{4,3,2,1,0:T(8,128)(2,1)S(1)} custom-call(s32[2,2,1]{2,1,0:T(2,128)S(1)} %copy-done.3, bf16[16,16,8,256]{3,2,1,0:T(8,128)(2,1)S(1)} %copy-done, bf16[16,16,8,256]{3,2,1,0:T(8,128)(2,1)S(1)} %copy-done.1, bf16[16,16,8,256]{3,2,1,0:T(8,128)(2,1)S(1)} %copy-done.2, ...), custom_call_target="tpu_custom_call" | custom-call | flops 1 | bytes 1 | tf_op jit(solution)/shard_map/pallas_call | solution.py:202
  39.6 0.8 collective-permute-start.10
  40.5 3.9 %collective-permute-start.13 = (bf16[4,32,1792]{2,1,0:T(8,128)(2,1)S(1)}, bf16[4,32,1792]{2,1,0:T(8,128)(2,1)S(1)}, u32[]{:S(2)}, u32[]{:S(2)}) collective-permute-start(bf16[4,32,1792]{2,1,0:T(8,128)(2,1)S(1)} %get-tuple-element.121), channel_id=1, source_target_pairs={{0,4},{1,5},{2,6},{3,7},{4,0},{5,1},{6,2},{7,3},{8,12},{9,13},{10,... | collective-permute-start | bytes 1376264 | tf_op jit(solution)/shard_map/ppermute | solution.py:51
  44.3 0.4 collective-permute-start.11
  44.8 3.1 %collective-permute-start.12 = (bf16[4,32,1792]{2,1,0:T(8,128)(2,1)S(1)}, bf16[4,32,1792]{2,1,0:T(8,128)(2,1)S(1)}, u32[]{:S(2)}, u32[]{:S(2)}) collective-permute-start(bf16[4,32,1792]{2,1,0:T(8,128)(2,1)S(1)} %pad_maximum_fusion.2), channel_id=1, source_target_pairs={{0,17},{1,16},{2,19},{3,18},{4,21},{5,20},{6,23},{7,22},{8,25},{9,... | collective-permute-start | bytes 1376264 | tf_op jit(solution)/shard_map/ppermute | solution.py:51
  47.8 5.5 %shard_map.87 = bf16[4,4,14,32,128]{4,3,2,1,0:T(8,128)(2,1)S(1)} custom-call(bf16[3,10,10,16,256]{4,3,2,1,0:T(8,128)(2,1)S(1)} %shard_map.86.own_ref.rest_0_, bf16[3,10,10,16,256]{4,3,2,1,0:T(8,128)(2,1)S(1)} %collective-permute-done.10.other_ref), custom_call_target="tpu_custom_call" | custom-call | flops 1 | bytes 1 | tf_op jit(solution)/shard_map/pallas_call | solution.py:290
  53.3 12.0 %collective-permute-done.13 = bf16[4,32,1792]{2,1,0:T(8,128)(2,1)S(1)} collective-permute-done((bf16[4,32,1792]{2,1,0:T(8,128)(2,1)S(1)}, bf16[4,32,1792]{2,1,0:T(8,128)(2,1)S(1)}, u32[]{:S(2)}, u32[]{:S(2)}) %collective-permute-start.13) | collective-permute-done | bytes 458784 | tf_op jit(solution)/shard_map/ppermute | solution.py:51
  65.3 1.5 %collective-permute-done.11 = bf16[4,32,1792]{2,1,0:T(8,128)(2,1)S(1)} collective-permute-done((bf16[4,32,1792]{2,1,0:T(8,128)(2,1)S(1)}, bf16[4,32,1792]{2,1,0:T(8,128)(2,1)S(1)}, u32[]{:S(2)}, u32[]{:S(2)}) %collective-permute-start.11) | collective-permute-done | bytes 458784 | tf_op jit(solution)/shard_map/ppermute | solution.py:51
  66.8 0.2 pad_maximum_fusion.rest_1_
  67.3 1.8 %collective-permute-start.15 = (bf16[2,2,14,32,128]{4,3,2,1,0:T(8,128)(2,1)S(1)}, bf16[2,2,14,32,128]{4,3,2,1,0:T(8,128)(2,1)S(1)}, u32[]{:S(2)}, u32[]{:S(2)}) collective-permute-start(bf16[2,2,14,32,128]{4,3,2,1,0:T(8,128)(2,1)S(1)} %pad_maximum_fusion.3), channel_id=1, source_target_pairs={{0,1},{1,0},{2,3},{3,2},{4,5},{5,4},{6,7},{7,6},{8,9},{9,8},{10,11... | collective-permute-start | bytes 1376264 | tf_op jit(solution)/shard_map/ppermute | solution.py:51
  69.1 0.3 collective-permute-start.16
  69.4 0.5 collective-permute-start.26
  70.0 1.0 collective-permute-done.14.rest_2_
  70.9 6.0 %shard_map.88 = (bf16[16,16,8,256]{3,2,1,0:T(8,128)(2,1)S(1)}, bf16[8,8,16,256]{3,2,1,0:T(8,128)(2,1)S(1)}) custom-call(s32[2,2,1]{2,1,0:T(2,128)S(1)} %copy-done.3, bf16[3,10,10,16,256]{4,3,2,1,0:T(8,128)(2,1)S(1)} %shard_map.86.own_ref.rest_0_, bf16[16,32,1792]{2,1,0:T(8,128)(2,1)S(1)} %pad_maximum_fusion.rest_1_, ...), custom_call_target="tpu_custom_call" | custom-call | flops 1 | bytes 1 | tf_op jit(solution)/shard_map/pallas_call | solution.py:394
  76.9 3.4 %collective-permute-done.15 = bf16[2,2,14,32,128]{4,3,2,1,0:T(8,128)(2,1)S(1)} collective-permute-done((bf16[2,2,14,32,128]{4,3,2,1,0:T(8,128)(2,1)S(1)}, bf16[2,2,14,32,128]{4,3,2,1,0:T(8,128)(2,1)S(1)}, u32[]{:S(2)}, u32[]{:S(2)}) %collective-permute-start.15) | collective-permute-done | bytes 458784 | tf_op jit(solution)/shard_map/ppermute | solution.py:51
  80.3 1.5 %collective-permute-done.16 = bf16[2,2,14,32,128]{4,3,2,1,0:T(8,128)(2,1)S(1)} collective-permute-done((bf16[2,2,14,32,128]{4,3,2,1,0:T(8,128)(2,1)S(1)}, bf16[2,2,14,32,128]{4,3,2,1,0:T(8,128)(2,1)S(1)}, u32[]{:S(2)}, u32[]{:S(2)}) %collective-permute-start.16) | collective-permute-done | bytes 458784 | tf_op jit(solution)/shard_map/ppermute | solution.py:51
  82.0 0.1 convert_add_fusion.3
  82.2 0.4 collective-permute-start.19
  82.6 1.4 %collective-permute-start.18 = (bf16[1,2,14,32,128]{4,3,2,1,0:T(8,128)(2,1)S(1)}, bf16[1,2,14,32,128]{4,3,2,1,0:T(8,128)(2,1)S(1)}, u32[]{:S(2)}, u32[]{:S(2)}) collective-permute-start(bf16[1,2,14,32,128]{4,3,2,1,0:T(8,128)(2,1)S(1)} %slice.257), channel_id=1, source_target_pairs={{0,16},{1,17},{2,18},{3,19},{4,20},{5,21},{6,22},{7,23},{8,24},{9,... | collective-permute-start | bytes 688136 | tf_op jit(solution)/shard_map/ppermute | solution.py:51
  84.0 5.3 %shard_map.89 = bf16[4,4,14,32,128]{4,3,2,1,0:T(8,128)(2,1)S(1)} custom-call(bf16[3,10,10,16,256]{4,3,2,1,0:T(8,128)(2,1)S(1)} %shard_map.86.own_ref.rest_0_, bf16[3,10,10,16,256]{4,3,2,1,0:T(8,128)(2,1)S(1)} %collective-permute-done.10.other_ref, bf16[8,8,16,256]{3,2,1,0:T(8,128)(2,1)S(1)} %get-tuple-element.78.rest_0_, ...), custom_call_target="tpu_custom_call" | custom-call | flops 1 | bytes 1 | tf_op jit(solution)/shard_map/pallas_call | solution.py:290
  89.3 0.9 collective-permute-done.19
  90.5 1.7 %collective-permute-start.22 = (bf16[2,2,14,32,128]{4,3,2,1,0:T(8,128)(2,1)S(1)}, bf16[2,2,14,32,128]{4,3,2,1,0:T(8,128)(2,1)S(1)}, u32[]{:S(2)}, u32[]{:S(2)}) collective-permute-start(bf16[2,2,14,32,128]{4,3,2,1,0:T(8,128)(2,1)S(1)} %pad_maximum_fusion.4), channel_id=1, source_target_pairs={{0,1},{1,0},{2,3},{3,2},{4,5},{5,4},{6,7},{7,6},{8,9},{9,8},{10,11... | collective-permute-start | bytes 1376264 | tf_op jit(solution)/shard_map/ppermute | solution.py:51
  92.2 0.3 collective-permute-start.23
  92.8 0.6 collective-permute-start.33
  93.4 1.3 collective-permute-start.20
  94.7 1.3 collective-permute-start.21
  96.0 5.2 %collective-permute-start.27 = (bf16[16,32,1792]{2,1,0:T(8,128)(2,1)S(1)}, bf16[16,32,1792]{2,1,0:T(8,128)(2,1)}, u32[]{:S(2)}, u32[]{:S(2)}) collective-permute-start(bf16[16,32,1792]{2,1,0:T(8,128)(2,1)S(1)} %constant_dynamic-update-slice_fusion.9.rest_5_), channel_id=1, source_target_pairs={{0,8},{1,9},{2,10},{3,11},{4,12},{5,13},{6,14},{7,15},{8,0},{9,1},... | collective-permute-start | bytes 5505032 | tf_op jit(solution)/shard_map/ppermute | solution.py:51
  101.3 0.6 pad_maximum_fusion.8
  101.9 3.1 %collective-permute-done.33 = bf16[2,14,32,128]{3,2,1,0:T(8,128)(2,1)S(1)} collective-permute-done((bf16[2,14,32,128]{3,2,1,0:T(8,128)(2,1)S(1)}, bf16[2,14,32,128]{3,2,1,0:T(8,128)(2,1)S(1)}, u32[]{:S(2)}, u32[]{:S(2)}) %collective-permute-start.33) | collective-permute-done | bytes 229408 | tf_op jit(solution)/shard_map/ppermute | solution.py:51
  105.2 0.1 convert_add_fusion.1
  105.4 0.9 slice.254
  106.3 0.1 copy-done.4
  106.4 0.7 slice.255
  107.1 0.7 slice.258
  107.8 1.2 collective-permute-start.29
  109.0 0.9 collective-permute-start.28
  109.9 3.5 %collective-permute-start.24 = (bf16[1,18,8,256]{3,2,1,0:T(8,128)(2,1)S(1)}, bf16[1,18,8,256]{3,2,1,0:T(8,128)(2,1)S(1)}, u32[]{:S(2)}, u32[]{:S(2)}) collective-permute-start(bf16[1,18,8,256]{3,2,1,0:T(8,128)(2,1)S(1)} %pad_maximum_fusion.9), channel_id=1, source_target_pairs={{0,1},{1,2},{2,3},{3,4},{4,5},{5,6},{6,7},{8,9},{9,10},{10,11},{11... | collective-permute-start | bytes 221192 | tf_op jit(solution)/shard_map/ppermute | solution.py:615
  113.4 1.3 collective-permute-start.25
  114.7 0.9 copy_bitcast_fusion
  115.7 0.2 collective-permute-done.24.rest_3_
  115.8 4.1 %collective-permute-done.25.rest_4_ = bf16[1,18,8,256]{3,2,1,0:T(8,128)(2,1)S(1)} collective-permute-done((bf16[1,18,8,256]{3,2,1,0:T(8,128)(2,1)}, bf16[1,18,8,256]{3,2,1,0:T(8,128)(2,1)S(1)}, u32[]{:S(2)}, u32[]{:S(2)}) %collective-permute-start.25) | collective-permute-done | bytes 73760 | tf_op jit(solution)/shard_map/ppermute | solution.py:615
  119.9 1.1 fusion.2
  121.1 2.0 %collective-permute-start.31 = (bf16[14,32,128]{2,1,0:T(8,128)(2,1)S(1)}, bf16[14,32,128]{2,1,0:T(8,128)(2,1)S(1)}, u32[]{:S(2)}, u32[]{:S(2)}) collective-permute-start(bf16[14,32,128]{2,1,0:T(8,128)(2,1)S(1)} %get-tuple-element.114), channel_id=1, source_target_pairs={{0,4},{1,5},{2,6},{3,7},{4,0},{5,1},{6,2},{7,3},{8,12},{9,13},{10,... | collective-permute-start | bytes 344072 | tf_op jit(solution)/shard_map/ppermute | solution.py:51
  123.1 2.4 %collective-permute-start.32 = (bf16[14,32,128]{2,1,0:T(8,128)(2,1)S(1)}, bf16[14,32,128]{2,1,0:T(8,128)(2,1)S(1)}, u32[]{:S(2)}, u32[]{:S(2)}) collective-permute-start(bf16[14,32,128]{2,1,0:T(8,128)(2,1)S(1)} %get-tuple-element.113), channel_id=1, source_target_pairs={{0,6},{1,7},{2,4},{3,5},{4,2},{5,3},{6,0},{7,1},{8,14},{9,15},{10,... | collective-permute-start | bytes 344072 | tf_op jit(solution)/shard_map/ppermute | solution.py:51
  125.6 0.8 dynamic-slice_bitcast_fusion
  126.5 8.2 %shard_map.90 = bf16[16,16,8,256]{3,2,1,0:T(8,128)(2,1)} custom-call(s32[2,2,1]{2,1,0:T(2,128)S(1)} %copy-done.3, bf16[16,16,8,256]{3,2,1,0:T(8,128)(2,1)S(1)} %get-tuple-element.74.rest_0_, bf16[1,16,8,256]{3,2,1,0:T(8,128)(2,1)S(1)} %collective-permute-done.20.rest_1_, bf16[1,16,8,256]{3,2,1,0:T(8,128)(2,1)S(1)} %collective-permute-done.21.rest_2_, ...), custom_call_target="tpu_custom_call" | custom-call | flops 1 | bytes 1 | tf_op jit(solution)/shard_map/pallas_call | solution.py:394
  134.8 0.8 dynamic-slice_bitcast_fusion.1
  (75 shorter events, 1.7 us)
Async XLA Ops:
  5.2 23.8 %copy-start.7 = (bf16[32,1792]{1,0:T(8,128)(2,1)S(1)}, bf16[32,1792]{1,0:T(8,128)(2,1)}, u32[]{:S(2)}) copy-start(bf16[32,1792]{1,0:T(8,128)(2,1)} %get-tuple-element.55) | copy-start | bytes 344068
  5.2 9.9 %collective-permute-start.2 = (bf16[1,32,1792]{2,1,0:T(8,128)(2,1)}, bf16[1,32,1792]{2,1,0:T(8,128)(2,1)S(1)}, u32[]{:S(2)}, u32[]{:S(2)}) collective-permute-start(bf16[1,32,1792]{2,1,0:T(8,128)(2,1)} %bitcast.49), channel_id=1, source_target_pairs={{0,4},{1,5},{2,6},{3,7},{4,0},{5,1},{6,2},{7,3},{8,12},{9,13},{10,... | collective-permute-start | bytes 344072 | tf_op jit(solution)/shard_map/ppermute | solution.py:51
  9.3 7.6 %collective-permute-start = (bf16[3,16,8,256]{3,2,1,0:T(8,128)(2,1)}, bf16[3,16,8,256]{3,2,1,0:T(8,128)(2,1)S(1)}, u32[]{:S(2)}, u32[]{:S(2)}) collective-permute-start(bf16[3,16,8,256]{3,2,1,0:T(8,128)(2,1)} %get-tuple-element.51), channel_id=1, source_target_pairs={{0,8},{8,16},{16,24},{1,9},{9,17},{17,25},{2,10},{10,18},{18,26},{... | collective-permute-start | bytes 589832 | tf_op jit(solution)/shard_map/ppermute | solution.py:603
  10.8 6.2 %collective-permute-start.1 = (bf16[3,16,8,256]{3,2,1,0:T(8,128)(2,1)}, bf16[3,16,8,256]{3,2,1,0:T(8,128)(2,1)S(1)}, u32[]{:S(2)}, u32[]{:S(2)}) collective-permute-start(bf16[3,16,8,256]{3,2,1,0:T(8,128)(2,1)} %get-tuple-element.52), channel_id=1, source_target_pairs={{8,0},{16,8},{24,16},{9,1},{17,9},{25,17},{10,2},{18,10},{26,18},{... | collective-permute-start | bytes 589832 | tf_op jit(solution)/shard_map/ppermute | solution.py:603
  16.1 13.0 %collective-permute-start.8 = (bf16[2,32,1792]{2,1,0:T(8,128)(2,1)S(1)}, bf16[2,32,1792]{2,1,0:T(8,128)(2,1)S(1)}, u32[]{:S(2)}, u32[]{:S(2)}) collective-permute-start(bf16[2,32,1792]{2,1,0:T(8,128)(2,1)S(1)} %pad_maximum_fusion.5), channel_id=1, source_target_pairs={{0,2},{1,3},{2,0},{3,1},{4,6},{5,7},{6,4},{7,5},{8,10},{9,11},{10,... | collective-permute-start | bytes 688136 | tf_op jit(solution)/shard_map/ppermute | solution.py:51
  17.0 19.9 %copy-start = (bf16[16,16,8,256]{3,2,1,0:T(8,128)(2,1)S(1)}, bf16[16,16,8,256]{3,2,1,0:T(8,128)(2,1)}, u32[]{:S(2)}) copy-start(bf16[16,16,8,256]{3,2,1,0:T(8,128)(2,1)} %rest_3_.1) | copy-start | bytes 3145732
  17.0 19.9 %copy-start.1 = (bf16[16,16,8,256]{3,2,1,0:T(8,128)(2,1)S(1)}, bf16[16,16,8,256]{3,2,1,0:T(8,128)(2,1)}, u32[]{:S(2)}) copy-start(bf16[16,16,8,256]{3,2,1,0:T(8,128)(2,1)} %rest_1_.3) | copy-start | bytes 3145732
  17.0 19.9 %copy-start.2 = (bf16[16,16,8,256]{3,2,1,0:T(8,128)(2,1)S(1)}, bf16[16,16,8,256]{3,2,1,0:T(8,128)(2,1)}, u32[]{:S(2)}) copy-start(bf16[16,16,8,256]{3,2,1,0:T(8,128)(2,1)} %rest_2_.3) | copy-start | bytes 3145732
  17.0 19.9 %copy-start.3 = (s32[2,2,1]{2,1,0:T(2,128)S(1)}, s32[2,2,1]{2,1,0:T(2,128)}, u32[]{:S(2)}) copy-start(s32[2,2,1]{2,1,0:T(2,128)} %copy.20.occ_ref) | copy-start | bytes 52
  18.1 8.9 %collective-permute-start.5 = (bf16[1,32,1792]{2,1,0:T(8,128)(2,1)}, bf16[1,32,1792]{2,1,0:T(8,128)(2,1)S(1)}, u32[]{:S(2)}, u32[]{:S(2)}) collective-permute-start(bf16[1,32,1792]{2,1,0:T(8,128)(2,1)} %bitcast.53), channel_id=1, source_target_pairs={{0,1},{1,0},{2,3},{3,2},{4,5},{5,4},{6,7},{7,6},{8,9},{9,8},{10,11... | collective-permute-start | bytes 344072 | tf_op jit(solution)/shard_map/ppermute | solution.py:51
  19.6 8.7 %collective-permute-start.6 = (bf16[1,32,1792]{2,1,0:T(8,128)(2,1)}, bf16[1,32,1792]{2,1,0:T(8,128)(2,1)S(1)}, u32[]{:S(2)}, u32[]{:S(2)}) collective-permute-start(bf16[1,32,1792]{2,1,0:T(8,128)(2,1)} %bitcast.54), channel_id=1, source_target_pairs={{0,16},{1,17},{2,18},{3,19},{4,20},{5,21},{6,22},{7,23},{8,24},{9,... | collective-permute-start | bytes 344072 | tf_op jit(solution)/shard_map/ppermute | solution.py:51
  22.5 6.5 %collective-permute-start.7 = (bf16[1,32,1792]{2,1,0:T(8,128)(2,1)}, bf16[1,32,1792]{2,1,0:T(8,128)(2,1)S(1)}, u32[]{:S(2)}, u32[]{:S(2)}) collective-permute-start(bf16[1,32,1792]{2,1,0:T(8,128)(2,1)} %bitcast.55), channel_id=1, source_target_pairs={{0,17},{1,16},{2,19},{3,18},{4,21},{5,20},{6,23},{7,22},{8,25},{9,... | collective-permute-start | bytes 344072 | tf_op jit(solution)/shard_map/ppermute | solution.py:51
  23.6 8.5 %collective-permute-start.3 = (bf16[3,18,8,256]{3,2,1,0:T(8,128)(2,1)S(1)}, bf16[3,18,8,256]{3,2,1,0:T(8,128)(2,1)S(1)}, u32[]{:S(2)}, u32[]{:S(2)}) collective-permute-start(bf16[3,18,8,256]{3,2,1,0:T(8,128)(2,1)S(1)} %get-tuple-element.56), channel_id=1, source_target_pairs={{0,1},{1,2},{2,3},{3,4},{4,5},{5,6},{6,7},{8,9},{9,10},{10,11},{11... | collective-permute-start | bytes 663560 | tf_op jit(solution)/shard_map/ppermute | solution.py:615
  27.0 9.9 %collective-permute-start.4 = (bf16[3,18,8,256]{3,2,1,0:T(8,128)(2,1)S(1)}, bf16[3,18,8,256]{3,2,1,0:T(8,128)(2,1)S(1)}, u32[]{:S(2)}, u32[]{:S(2)}) collective-permute-start(bf16[3,18,8,256]{3,2,1,0:T(8,128)(2,1)S(1)} %get-tuple-element.57), channel_id=1, source_target_pairs={{1,0},{2,1},{3,2},{4,3},{5,4},{6,5},{7,6},{9,8},{10,9},{11,10},{12... | collective-permute-start | bytes 663560 | tf_op jit(solution)/shard_map/ppermute | solution.py:615
  39.6 8.2 %collective-permute-start.10 = (bf16[3,10,10,16,256]{4,3,2,1,0:T(8,128)(2,1)S(1)}, bf16[3,10,10,16,256]{4,3,2,1,0:T(8,128)(2,1)S(1)}, u32[]{:S(2)}, u32[]{:S(2)}) collective-permute-start(bf16[3,10,10,16,256]{4,3,2,1,0:T(8,128)(2,1)S(1)} %shard_map.86.own_ref.rest_0_), channel_id=1, source_target_pairs={{0,8},{1,9},{2,10},{3,11},{4,12},{5,13},{6,14},{7,15},{8,0},{9,1},... | collective-permute-start | bytes 7372808 | tf_op jit(solution)/shard_map/ppermute | solution.py:51
  40.5 24.8 %collective-permute-start.13 = (bf16[4,32,1792]{2,1,0:T(8,128)(2,1)S(1)}, bf16[4,32,1792]{2,1,0:T(8,128)(2,1)S(1)}, u32[]{:S(2)}, u32[]{:S(2)}) collective-permute-start(bf16[4,32,1792]{2,1,0:T(8,128)(2,1)S(1)} %get-tuple-element.121), channel_id=1, source_target_pairs={{0,4},{1,5},{2,6},{3,7},{4,0},{5,1},{6,2},{7,3},{8,12},{9,13},{10,... | collective-permute-start | bytes 1376264 | tf_op jit(solution)/shard_map/ppermute | solution.py:51
  44.3 20.9 %collective-permute-start.9 = (bf16[4,32,1792]{2,1,0:T(8,128)(2,1)S(1)}, bf16[4,32,1792]{2,1,0:T(8,128)(2,1)S(1)}, u32[]{:S(2)}, u32[]{:S(2)}) collective-permute-start(bf16[4,32,1792]{2,1,0:T(8,128)(2,1)S(1)} %pad_maximum_fusion.2), channel_id=1, source_target_pairs={{0,1},{1,0},{2,3},{3,2},{4,5},{5,4},{6,7},{7,6},{8,9},{9,8},{10,11... | collective-permute-start | bytes 1376264 | tf_op jit(solution)/shard_map/ppermute | solution.py:51
  44.3 22.4 %collective-permute-start.11 = (bf16[4,32,1792]{2,1,0:T(8,128)(2,1)S(1)}, bf16[4,32,1792]{2,1,0:T(8,128)(2,1)S(1)}, u32[]{:S(2)}, u32[]{:S(2)}) collective-permute-start(bf16[4,32,1792]{2,1,0:T(8,128)(2,1)S(1)} %pad_maximum_fusion.2), channel_id=1, source_target_pairs={{0,16},{1,17},{2,18},{3,19},{4,20},{5,21},{6,22},{7,23},{8,24},{9,... | collective-permute-start | bytes 1376264 | tf_op jit(solution)/shard_map/ppermute | solution.py:51
  44.8 22.0 %collective-permute-start.12 = (bf16[4,32,1792]{2,1,0:T(8,128)(2,1)S(1)}, bf16[4,32,1792]{2,1,0:T(8,128)(2,1)S(1)}, u32[]{:S(2)}, u32[]{:S(2)}) collective-permute-start(bf16[4,32,1792]{2,1,0:T(8,128)(2,1)S(1)} %pad_maximum_fusion.2), channel_id=1, source_target_pairs={{0,17},{1,16},{2,19},{3,18},{4,21},{5,20},{6,23},{7,22},{8,25},{9,... | collective-permute-start | bytes 1376264 | tf_op jit(solution)/shard_map/ppermute | solution.py:51
  67.1 3.9 %collective-permute-start.14 = (bf16[16,32,1792]{2,1,0:T(8,128)(2,1)S(1)}, bf16[16,32,1792]{2,1,0:T(8,128)(2,1)S(1)}, u32[]{:S(2)}, u32[]{:S(2)}) collective-permute-start(bf16[16,32,1792]{2,1,0:T(8,128)(2,1)S(1)} %pad_maximum_fusion.rest_1_), channel_id=1, source_target_pairs={{0,8},{1,9},{2,10},{3,11},{4,12},{5,13},{6,14},{7,15},{8,0},{9,1},... | collective-permute-start | bytes 5505032 | tf_op jit(solution)/shard_map/ppermute | solution.py:51
  67.3 13.0 %collective-permute-start.15 = (bf16[2,2,14,32,128]{4,3,2,1,0:T(8,128)(2,1)S(1)}, bf16[2,2,14,32,128]{4,3,2,1,0:T(8,128)(2,1)S(1)}, u32[]{:S(2)}, u32[]{:S(2)}) collective-permute-start(bf16[2,2,14,32,128]{4,3,2,1,0:T(8,128)(2,1)S(1)} %pad_maximum_fusion.3), channel_id=1, source_target_pairs={{0,1},{1,0},{2,3},{3,2},{4,5},{5,4},{6,7},{7,6},{8,9},{9,8},{10,11... | collective-permute-start | bytes 1376264 | tf_op jit(solution)/shard_map/ppermute | solution.py:51
  69.1 12.6 %collective-permute-start.16 = (bf16[2,2,14,32,128]{4,3,2,1,0:T(8,128)(2,1)S(1)}, bf16[2,2,14,32,128]{4,3,2,1,0:T(8,128)(2,1)S(1)}, u32[]{:S(2)}, u32[]{:S(2)}) collective-permute-start(bf16[2,2,14,32,128]{4,3,2,1,0:T(8,128)(2,1)S(1)} %concatenate.80), channel_id=1, source_target_pairs={{0,16},{1,17},{2,18},{3,19},{4,20},{5,21},{6,22},{7,23},{8,24},{9,... | collective-permute-start | bytes 1376264 | tf_op jit(solution)/shard_map/ppermute | solution.py:51
  69.4 25.2 %collective-permute-start.26 = (bf16[8,32,1792]{2,1,0:T(8,128)(2,1)S(1)}, bf16[8,32,1792]{2,1,0:T(8,128)(2,1)S(1)}, u32[]{:S(2)}, u32[]{:S(2)}) collective-permute-start(bf16[8,32,1792]{2,1,0:T(8,128)(2,1)S(1)} %get-tuple-element.90), channel_id=1, source_target_pairs={{0,2},{1,3},{2,0},{3,1},{4,6},{5,7},{6,4},{7,5},{8,10},{9,11},{10,... | collective-permute-start | bytes 2752520 | tf_op jit(solution)/shard_map/ppermute | solution.py:51
  81.9 2.1 %collective-permute-start.17 = (bf16[8,8,16,256]{3,2,1,0:T(8,128)(2,1)S(1)}, bf16[8,8,16,256]{3,2,1,0:T(8,128)(2,1)S(1)}, u32[]{:S(2)}, u32[]{:S(2)}) collective-permute-start(bf16[8,8,16,256]{3,2,1,0:T(8,128)(2,1)S(1)} %get-tuple-element.78.rest_0_), channel_id=1, source_target_pairs={{0,8},{1,9},{2,10},{3,11},{4,12},{5,13},{6,14},{7,15},{8,0},{9,1},... | collective-permute-start | bytes 1572872 | tf_op jit(solution)/shard_map/ppermute | solution.py:51
  82.2 8.1 %collective-permute-start.19 = (bf16[1,2,14,32,128]{4,3,2,1,0:T(8,128)(2,1)S(1)}, bf16[1,2,14,32,128]{4,3,2,1,0:T(8,128)(2,1)S(1)}, u32[]{:S(2)}, u32[]{:S(2)}) collective-permute-start(bf16[1,2,14,32,128]{4,3,2,1,0:T(8,128)(2,1)S(1)} %slice.256), channel_id=1, source_target_pairs={{0,1},{1,0},{2,3},{3,2},{4,5},{5,4},{6,7},{7,6},{8,9},{9,8},{10,11... | collective-permute-start | bytes 688136 | tf_op jit(solution)/shard_map/ppermute | solution.py:51
  82.6 7.7 %collective-permute-start.18 = (bf16[1,2,14,32,128]{4,3,2,1,0:T(8,128)(2,1)S(1)}, bf16[1,2,14,32,128]{4,3,2,1,0:T(8,128)(2,1)S(1)}, u32[]{:S(2)}, u32[]{:S(2)}) collective-permute-start(bf16[1,2,14,32,128]{4,3,2,1,0:T(8,128)(2,1)S(1)} %slice.257), channel_id=1, source_target_pairs={{0,16},{1,17},{2,18},{3,19},{4,20},{5,21},{6,22},{7,23},{8,24},{9,... | collective-permute-start | bytes 688136 | tf_op jit(solution)/shard_map/ppermute | solution.py:51
  90.5 14.6 %collective-permute-start.22 = (bf16[2,2,14,32,128]{4,3,2,1,0:T(8,128)(2,1)S(1)}, bf16[2,2,14,32,128]{4,3,2,1,0:T(8,128)(2,1)S(1)}, u32[]{:S(2)}, u32[]{:S(2)}) collective-permute-start(bf16[2,2,14,32,128]{4,3,2,1,0:T(8,128)(2,1)S(1)} %pad_maximum_fusion.4), channel_id=1, source_target_pairs={{0,1},{1,0},{2,3},{3,2},{4,5},{5,4},{6,7},{7,6},{8,9},{9,8},{10,11... | collective-permute-start | bytes 1376264 | tf_op jit(solution)/shard_map/ppermute | solution.py:51
  92.2 12.8 %collective-permute-start.23 = (bf16[2,2,14,32,128]{4,3,2,1,0:T(8,128)(2,1)S(1)}, bf16[2,2,14,32,128]{4,3,2,1,0:T(8,128)(2,1)S(1)}, u32[]{:S(2)}, u32[]{:S(2)}) collective-permute-start(bf16[2,2,14,32,128]{4,3,2,1,0:T(8,128)(2,1)S(1)} %concatenate.73), channel_id=1, source_target_pairs={{0,16},{1,17},{2,18},{3,19},{4,20},{5,21},{6,22},{7,23},{8,24},{9,... | collective-permute-start | bytes 1376264 | tf_op jit(solution)/shard_map/ppermute | solution.py:51
  92.8 12.2 %collective-permute-start.33 = (bf16[2,14,32,128]{3,2,1,0:T(8,128)(2,1)S(1)}, bf16[2,14,32,128]{3,2,1,0:T(8,128)(2,1)S(1)}, u32[]{:S(2)}, u32[]{:S(2)}) collective-permute-start(bf16[2,14,32,128]{3,2,1,0:T(8,128)(2,1)S(1)} %slice.253), channel_id=1, source_target_pairs={{0,4},{1,5},{2,6},{3,7},{4,0},{5,1},{6,2},{7,3},{8,12},{9,13},{10,... | collective-permute-start | bytes 688136 | tf_op jit(solution)/shard_map/ppermute | solution.py:51
  93.4 2.7 %collective-permute-start.20 = (bf16[1,16,8,256]{3,2,1,0:T(8,128)(2,1)S(1)}, bf16[1,16,8,256]{3,2,1,0:T(8,128)(2,1)S(1)}, u32[]{:S(2)}, u32[]{:S(2)}) collective-permute-start(bf16[1,16,8,256]{3,2,1,0:T(8,128)(2,1)S(1)} %get-tuple-element.82), channel_id=1, source_target_pairs={{0,8},{8,16},{16,24},{1,9},{9,17},{17,25},{2,10},{10,18},{18,26},{... | collective-permute-start | bytes 196616 | tf_op jit(solution)/shard_map/ppermute | solution.py:603
  94.7 6.6 %collective-permute-start.21 = (bf16[1,16,8,256]{3,2,1,0:T(8,128)(2,1)S(1)}, bf16[1,16,8,256]{3,2,1,0:T(8,128)(2,1)S(1)}, u32[]{:S(2)}, u32[]{:S(2)}) collective-permute-start(bf16[1,16,8,256]{3,2,1,0:T(8,128)(2,1)S(1)} %get-tuple-element.83), channel_id=1, source_target_pairs={{8,0},{16,8},{24,16},{9,1},{17,9},{25,17},{10,2},{18,10},{26,18},{... | collective-permute-start | bytes 196616 | tf_op jit(solution)/shard_map/ppermute | solution.py:603
  96.0 30.4 %collective-permute-start.27 = (bf16[16,32,1792]{2,1,0:T(8,128)(2,1)S(1)}, bf16[16,32,1792]{2,1,0:T(8,128)(2,1)}, u32[]{:S(2)}, u32[]{:S(2)}) collective-permute-start(bf16[16,32,1792]{2,1,0:T(8,128)(2,1)S(1)} %constant_dynamic-update-slice_fusion.9.rest_5_), channel_id=1, source_target_pairs={{0,8},{1,9},{2,10},{3,11},{4,12},{5,13},{6,14},{7,15},{8,0},{9,1},... | collective-permute-start | bytes 5505032 | tf_op jit(solution)/shard_map/ppermute | solution.py:51
  105.2 1.9 %copy-start.6 = (f32[2,2,14,32,128]{4,3,2,1,0:T(8,128)}, f32[2,2,14,32,128]{4,3,2,1,0:T(8,128)S(1)}, u32[]{:S(2)}) copy-start(f32[2,2,14,32,128]{4,3,2,1,0:T(8,128)S(1)} %convert_add_fusion) | copy-start | bytes 2752516
  105.4 1.0 copy-start.4
  107.8 5.6 %collective-permute-start.34 = (bf16[1,14,32,128]{3,2,1,0:T(8,128)(2,1)}, bf16[1,14,32,128]{3,2,1,0:T(8,128)(2,1)}, u32[]{:S(2)}, u32[]{:S(2)}) collective-permute-start(bf16[1,14,32,128]{3,2,1,0:T(8,128)(2,1)} %slice.258), channel_id=1, source_target_pairs={{0,2},{1,3},{2,0},{3,1},{4,6},{5,7},{6,4},{7,5},{8,10},{9,11},{10,... | collective-permute-start | bytes 344072 | tf_op jit(solution)/shard_map/ppermute | solution.py:51
  107.8 17.7 %copy-start.5 = (f32[2,2,14,32,128]{4,3,2,1,0:T(8,128)S(1)}, f32[2,2,14,32,128]{4,3,2,1,0:T(8,128)}, u32[]{:S(2)}) copy-start(f32[2,2,14,32,128]{4,3,2,1,0:T(8,128)} %copy-done.4) | copy-start | bytes 2752516
  107.8 12.1 %collective-permute-start.29 = (bf16[1,2,14,32,128]{4,3,2,1,0:T(8,128)(2,1)}, bf16[1,2,14,32,128]{4,3,2,1,0:T(8,128)(2,1)S(1)}, u32[]{:S(2)}, u32[]{:S(2)}) collective-permute-start(bf16[1,2,14,32,128]{4,3,2,1,0:T(8,128)(2,1)} %slice.254), channel_id=1, source_target_pairs={{0,1},{1,0},{2,3},{3,2},{4,5},{5,4},{6,7},{7,6},{8,9},{9,8},{10,11... | collective-permute-start | bytes 688136 | tf_op jit(solution)/shard_map/ppermute | solution.py:51
  109.0 11.0 %collective-permute-start.28 = (bf16[1,2,14,32,128]{4,3,2,1,0:T(8,128)(2,1)}, bf16[1,2,14,32,128]{4,3,2,1,0:T(8,128)(2,1)S(1)}, u32[]{:S(2)}, u32[]{:S(2)}) collective-permute-start(bf16[1,2,14,32,128]{4,3,2,1,0:T(8,128)(2,1)} %slice.255), channel_id=1, source_target_pairs={{0,16},{1,17},{2,18},{3,19},{4,20},{5,21},{6,22},{7,23},{8,24},{9,... | collective-permute-start | bytes 688136 | tf_op jit(solution)/shard_map/ppermute | solution.py:51
  109.9 5.9 %collective-permute-start.24 = (bf16[1,18,8,256]{3,2,1,0:T(8,128)(2,1)S(1)}, bf16[1,18,8,256]{3,2,1,0:T(8,128)(2,1)S(1)}, u32[]{:S(2)}, u32[]{:S(2)}) collective-permute-start(bf16[1,18,8,256]{3,2,1,0:T(8,128)(2,1)S(1)} %pad_maximum_fusion.9), channel_id=1, source_target_pairs={{0,1},{1,2},{2,3},{3,4},{4,5},{5,6},{6,7},{8,9},{9,10},{10,11},{11... | collective-permute-start | bytes 221192 | tf_op jit(solution)/shard_map/ppermute | solution.py:615
  113.4 6.5 %collective-permute-start.25 = (bf16[1,18,8,256]{3,2,1,0:T(8,128)(2,1)}, bf16[1,18,8,256]{3,2,1,0:T(8,128)(2,1)S(1)}, u32[]{:S(2)}, u32[]{:S(2)}) collective-permute-start(bf16[1,18,8,256]{3,2,1,0:T(8,128)(2,1)} %pad_maximum_fusion.8), channel_id=1, source_target_pairs={{1,0},{2,1},{3,2},{4,3},{5,4},{6,5},{7,6},{9,8},{10,9},{11,10},{12... | collective-permute-start | bytes 221192 | tf_op jit(solution)/shard_map/ppermute | solution.py:615
  121.1 13.6 %collective-permute-start.31 = (bf16[14,32,128]{2,1,0:T(8,128)(2,1)S(1)}, bf16[14,32,128]{2,1,0:T(8,128)(2,1)S(1)}, u32[]{:S(2)}, u32[]{:S(2)}) collective-permute-start(bf16[14,32,128]{2,1,0:T(8,128)(2,1)S(1)} %get-tuple-element.114), channel_id=1, source_target_pairs={{0,4},{1,5},{2,6},{3,7},{4,0},{5,1},{6,2},{7,3},{8,12},{9,13},{10,... | collective-permute-start | bytes 344072 | tf_op jit(solution)/shard_map/ppermute | solution.py:51
  123.1 11.6 %collective-permute-start.32 = (bf16[14,32,128]{2,1,0:T(8,128)(2,1)S(1)}, bf16[14,32,128]{2,1,0:T(8,128)(2,1)S(1)}, u32[]{:S(2)}, u32[]{:S(2)}) collective-permute-start(bf16[14,32,128]{2,1,0:T(8,128)(2,1)S(1)} %get-tuple-element.113), channel_id=1, source_target_pairs={{0,6},{1,7},{2,4},{3,5},{4,2},{5,3},{6,0},{7,1},{8,14},{9,15},{10,... | collective-permute-start | bytes 344072 | tf_op jit(solution)/shard_map/ppermute | solution.py:51
  125.5 9.2 %collective-permute-start.30 = (bf16[14,32,128]{2,1,0:T(8,128)(2,1)S(1)}, bf16[14,32,128]{2,1,0:T(8,128)(2,1)S(1)}, u32[]{:S(2)}, u32[]{:S(2)}) collective-permute-start(bf16[14,32,128]{2,1,0:T(8,128)(2,1)S(1)} %fusion.8), channel_id=1, source_target_pairs={{0,2},{1,3},{2,0},{3,1},{4,6},{5,7},{6,4},{7,5},{8,10},{9,11},{10,... | collective-permute-start | bytes 344072 | tf_op jit(solution)/shard_map/ppermute | solution.py:51

commit v4 on v3

--- a/solution.py
+++ b/solution.py
@@ -64,7 +64,7 @@
     first = jnp.int32(0)
     second = jnp.int32(0)
     for i in range(n_bx * n_by):
-        on = occ_ref[i // n_by, i % n_by, 0] > 0
+        on = occ_ref[i // n_by, 0, i % n_by] > 0
         first = jnp.where(jnp.logical_and(on, count == 0), i, first)
         second = jnp.where(jnp.logical_and(on, count == 1), i, second)
         count = count + on.astype(jnp.int32)
@@ -78,7 +78,7 @@
     bx = block[0] + step_x
     by = block[1] + step_y
     inside = (bx >= 0) & (bx < n_bx) & (by >= 0) & (by < n_by)
-    near = occ_ref[jnp.clip(bx, 0, n_bx - 1), jnp.clip(by, 0, n_by - 1), 0]
+    near = occ_ref[jnp.clip(bx, 0, n_bx - 1), 0, jnp.clip(by, 0, n_by - 1)]
     return jnp.where(inside, near, 1) * block[2]
 
 
@@ -95,14 +95,6 @@
         pltpu.make_async_copy(low_y.at[index], ext_ref.at[:, 0], sems.at[3]),
         pltpu.make_async_copy(high_y.at[index], ext_ref.at[:, size_y + 1], sems.at[4]),
     ]
-
-
-def load_extended(*refs):
-    copies = extended_copies(*refs)
-    for copy in copies:
-        copy.start()
-    for copy in copies:
-        copy.wait()
 
 
 def spread_patches(occ_ref, blocks, ext_ref, shifted_ref, n_bx, n_by):
@@ -317,10 +309,16 @@
     blocks = pick_blocks(occ_ref, n_bx, n_by)
     my_gx = lax.axis_index("gx")
     my_gy = lax.axis_index("gy")
+    copies = [] if n_sources == 1 else extended_copies(0, *source_refs, ext_ref, sems)
+    for copy in copies:
+        copy.start()
     for piece_ref, flips in zip(piece_refs, distances):
         for place, (flip_gx, flip_gy) in enumerate(flips):
             start = pl.multiple_of((my_gy ^ flip_gy) * plan.cols, plan.cols)
             weight_ref[my_gx ^ flip_gx, pl.ds(start, plan.cols)] = piece_ref[place]
+    out_ref[...] = jnp.zeros_like(out_ref)
+    for copy in copies:
+        copy.wait()
     if n_sources == 1:
 
         def put(j, x, y, rows):
@@ -328,9 +326,7 @@
 
         spread_rows(source_refs[0].at[2], put)
     else:
-        load_extended(0, *source_refs, ext_ref, sems)
         spread_patches(occ_ref, blocks, ext_ref, shifted_ref, n_bx, n_by)
-    out_ref[...] = jnp.zeros_like(out_ref)
 
     def kernel_lanes(tile):
         total = None
@@ -450,7 +446,7 @@
                 value = raw_ref[side, index, rows].astype(jnp.float32)
                 if index == 0:
                     value = jnp.maximum(value, 0.0)
-                value = jnp.where(occ_ref[at[0], at[1], 0] > 0, value, 0.0)
+                value = jnp.where(occ_ref[at[0], 0, at[1]] > 0, value, 0.0)
                 strip_ref[index, rows] = value.astype(jnp.bfloat16)
 
 
@@ -558,6 +554,9 @@
             self.slots[half] = [self.slots[half][i] for i in stay]
         self.step += 1
 
+    def last(self):
+        return self.step + 1 == len(self.orders[0])
+
     def done(self):
         return self.step == len(self.orders[0])
 
@@ -569,10 +568,9 @@
     return jnp.concatenate([array[i : i + 1] for i in indices], axis=0)
 
 
-def halve_z_step(plan, line):
-    step = line.shape[0] // 2
-    got = swap_z(line[step:].astype(jnp.bfloat16), plan, step)
-    return line[:step].astype(jnp.float32) + got.astype(jnp.float32)
+def halve_z_step(plan, line, step):
+    got = swap_z(line[1::2].astype(jnp.bfloat16), plan, step)
+    return line[0::2].astype(jnp.float32) + got.astype(jnp.float32)
 
 
 def spread_z(plan, line, *before):
@@ -620,7 +618,7 @@
     plan = Plan(
         lax.axis_size("gx"), lax.axis_size("gy"), weight_one.shape[0], inputs.shape[-1]
     )
-    occ = occupancy
+    occ = occupancy.transpose(0, 2, 1)
 
     own_two, own_one, first_x, last_x, first_y, last_y = first_steps(
         plan, occ, weight_two, weight_one, (preact, inputs, out_grad), n_bx, n_by
@@ -633,7 +631,7 @@
     sent_y = after(strips_y(low_x, high_x, first_y, last_y), two.array)
     for flips in steps[-1:]:
         two = two.joined(two.from_others(plan, flips))
-    one = Gathered(own_one[None], [(0, 0)]).after(low_x, high_x)
+    one = Gathered(own_one[None], [(0, 0)]).after(sent_y)
     one = one.joined(one.from_others(plan, plane_flips(plan)))
     edges = after((low_x, high_x) + rims_y(*sent_y), one.array, two.array)
     two = two.after(edges)
@@ -657,7 +655,7 @@
     while not halving_two.done():
         sends = halving_two.sends()
         got_two = halving_two.swaps(sends)
-        if halving_two.step + 1 == len(halving_two.orders[0]):
+        if halving_two.last():
             sums_one = weight_sums(plan, 1, patches, other, (after(center, sends), other_center))
             got_two = after(got_two, sums_one)
         halving_two.add(got_two)
@@ -669,7 +667,7 @@
     halving_one = Halving(plan, after(sums_one, got_two))
     sends = halving_one.sends()
     got_one = halving_one.swaps(sends)
-    line_two = halve_z_step(plan, after(line_two, sends))
+    line_two = halve_z_step(plan, after(line_two, sends), 1)
     strips = (grad_one[None, 0], grad_one[None, -1], grad_one[None, :, 0], grad_one[None, :, -1])
     strips = after(strips, sends)
     low_x, high_x = rims_x(*strips[:2])
@@ -678,12 +676,12 @@
     while not halving_one.done():
         sends = halving_one.sends()
         got_one = halving_one.swaps(sends)
-        if halving_one.step + 1 == len(halving_one.orders[0]):
-            edges_one = (low_x, high_x) + rims_y(*after(sent_y, sends))
+        if halving_one.last():
             line_two = after(line_two, sends)
             while line_two.shape[0] > 1:
-                line_two = halve_z_step(plan, line_two)
-            got_one = after(got_one, edges_one)
+                line_two = halve_z_step(plan, line_two, plan.n_z // line_two.shape[0])
+            edges_one = (low_x, high_x) + rims_y(*after(sent_y, sends))
+            got_one = after(got_one)
         halving_one.add(got_one)
     line_one = halving_one.line()
     pieces = both_cores(plan, one)

time: 136 us -> 134 us (0.985)
  waiting for transfers between devices: 39.1 us -> 37.2 us
  local copies, waits for them, and re-layouts: 7.07 us -> 5.6 us
    ppermute x4, waiting for transfers between devices: 12.1 us -> 6.91 us  [rims_y(): return (lax.ppermute(last_y, 'gy', up), lax.ppermute(first_y, 'gy', down))]
    ppermute x27, waiting for transfers between devices: 27.1 us -> 30.2 us  [swap(): return lax.ppermute(x, BOTH, pairs)]
    ppermute x27, starting transfers between devices: 36.6 us -> 38.3 us  [swap(): return lax.ppermute(x, BOTH, pairs)]
    unnamed x22 -> x23, local copies, waits for them, and re-layouts: 2.74 us -> 1.26 us
  transfers between devices with their start and end apart: 35 -> 35, of which waited for: 14 -> 15; matrix products, arithmetic and copies ran while one was open for 8% -> 8% of each run, Pallas kernels for 18% -> 19%
where the time goes in v4:
time: 134 us; the launch traced here: 133 us
  starting transfers between devices  52.3 us (39%)
  waiting for transfers between devices  37.2 us (28%)
  Pallas kernels  30.9 us (23%)
  other arithmetic  6.14 us (5%)
  local copies, waits for them, and re-layouts  5.6 us (4%)
    ppermute x27, starting transfers between devices, swap(): return lax.ppermute(x, BOTH, pairs)  38.3 us
    ppermute x27, waiting for transfers between devices, swap(): return lax.ppermute(x, BOTH, pairs)  30.2 us
    pallas_call x2, Pallas kernels, data_grad(): pl.pallas_call(functools.partial(data_kernel, plan, n_bx, n_by, len(sourc...  14.1 us
    pallas_call x2, Pallas kernels, weight_sums(): pl.pallas_call(functools.partial(weight_kernel, plan, field), out_shape=j...  10.8 us
    ppermute x4, starting transfers between devices, rims_y(): return (lax.ppermute(last_y, 'gy', up), lax.ppermute(first_y, 'gy', down))  8.47 us
    ppermute x4, waiting for transfers between devices, rims_y(): return (lax.ppermute(last_y, 'gy', up), lax.ppermute(first_y, 'gy', down))  6.91 us
    ppermute x4, starting transfers between devices, rims_x(): return (lax.ppermute(last_x, 'gx', up), lax.ppermute(first_x, 'gx', down))  5.54 us
    pallas_call x1, Pallas kernels, first_steps(): pl.pallas_call(functools.partial(first_kernel, plan, n_bx, n_by), out_sha...  3.22 us
  transfers between devices with their start and end apart: 35, of which 15 were waited for; matrix products, arithmetic and copies ran while one was open for 8% of the time, Pallas kernels for 19%

profile of v4, /device:TPU:0, one launch (start us, length us, event | category | flops | bytes accessed | tf_op | source)
XLA Modules:
  0.0 133.4 jit_solution(6575455324603558082)
XLA Ops:
  0.6 3.2 %shard_map.85 = (bf16[32,1792]{1,0:T(8,128)(2,1)}, bf16[32,1792]{1,0:T(8,128)(2,1)}, bf16[3,16,8,256]{3,2,1,0:T(8,128)(2,1)}, bf16[3,16,8,256]{3,2,1,0:T(8,128)(...) custom-call(s32[2,1,2]{2,1,0:T(1,128)} %bitcast.52, bf16[32,1728]{1,0:T(8,128)(2,1)} %bitcast.63, ...), custom_call_target="tpu_custom_call" | custom-call | flops 1 | bytes 1 | tf_op jit(solution)/shard_map/pallas_call | solution.py:461
  3.9 4.1 %collective-permute-start.2 = (bf16[1,32,1792]{2,1,0:T(8,128)(2,1)}, bf16[1,32,1792]{2,1,0:T(8,128)(2,1)S(1)}, u32[]{:S(2)}, u32[]{:S(2)}) collective-permute-start(bf16[1,32,1792]{2,1,0:T(8,128)(2,1)} %bitcast.56), channel_id=1, source_target_pairs={{0,4},{1,5},{2,6},{3,7},{4,0},{5,1},{6,2},{7,3},{8,12},{9,13},{10,... | collective-permute-start | bytes 344072 | tf_op jit(solution)/shard_map/ppermute | solution.py:51
  8.0 1.5 %collective-permute-start = (bf16[3,16,8,256]{3,2,1,0:T(8,128)(2,1)}, bf16[3,16,8,256]{3,2,1,0:T(8,128)(2,1)S(1)}, u32[]{:S(2)}, u32[]{:S(2)}) collective-permute-start(bf16[3,16,8,256]{3,2,1,0:T(8,128)(2,1)} %get-tuple-element.51), channel_id=1, source_target_pairs={{0,8},{8,16},{16,24},{1,9},{9,17},{17,25},{2,10},{10,18},{18,26},{... | collective-permute-start | bytes 589832 | tf_op jit(solution)/shard_map/ppermute | solution.py:601
  9.4 1.3 collective-permute-start.1
  10.7 3.0 %collective-permute-done.2 = bf16[1,32,1792]{2,1,0:T(8,128)(2,1)S(1)} collective-permute-done((bf16[1,32,1792]{2,1,0:T(8,128)(2,1)}, bf16[1,32,1792]{2,1,0:T(8,128)(2,1)S(1)}, u32[]{:S(2)}, u32[]{:S(2)}) %collective-permute-start.2) | collective-permute-done | bytes 114720 | tf_op jit(solution)/shard_map/ppermute | solution.py:51
  13.8 0.9 pad_maximum_fusion.5
  14.7 0.9 collective-permute-start.8
  15.7 1.2 pad_maximum_fusion.6
  16.9 1.6 %collective-permute-start.5 = (bf16[1,32,1792]{2,1,0:T(8,128)(2,1)}, bf16[1,32,1792]{2,1,0:T(8,128)(2,1)S(1)}, u32[]{:S(2)}, u32[]{:S(2)}) collective-permute-start(bf16[1,32,1792]{2,1,0:T(8,128)(2,1)} %bitcast.59), channel_id=1, source_target_pairs={{0,1},{1,0},{2,3},{3,2},{4,5},{5,4},{6,7},{7,6},{8,9},{9,8},{10,11... | collective-permute-start | bytes 344072 | tf_op jit(solution)/shard_map/ppermute | solution.py:51
  18.5 1.0 constant_dynamic-update-slice_fusion.14
  19.4 3.0 %collective-permute-start.6 = (bf16[1,32,1792]{2,1,0:T(8,128)(2,1)S(1)}, bf16[1,32,1792]{2,1,0:T(8,128)(2,1)S(1)}, u32[]{:S(2)}, u32[]{:S(2)}) collective-permute-start(bf16[1,32,1792]{2,1,0:T(8,128)(2,1)S(1)} %bitcast.61), channel_id=1, source_target_pairs={{0,16},{1,17},{2,18},{3,19},{4,20},{5,21},{6,22},{7,23},{8,24},{9,... | collective-permute-start | bytes 344072 | tf_op jit(solution)/shard_map/ppermute | solution.py:51
  22.5 3.4 %collective-permute-start.3 = (bf16[3,18,8,256]{3,2,1,0:T(8,128)(2,1)S(1)}, bf16[3,18,8,256]{3,2,1,0:T(8,128)(2,1)S(1)}, u32[]{:S(2)}, u32[]{:S(2)}) collective-permute-start(bf16[3,18,8,256]{3,2,1,0:T(8,128)(2,1)S(1)} %get-tuple-element.56), channel_id=1, source_target_pairs={{0,1},{1,2},{2,3},{3,4},{4,5},{5,6},{6,7},{8,9},{9,10},{10,11},{11... | collective-permute-start | bytes 663560 | tf_op jit(solution)/shard_map/ppermute | solution.py:613
  25.9 1.3 collective-permute-start.4
  27.2 0.7 collective-permute-done.6
  27.9 0.8 collective-permute-done.7
  28.8 2.3 %collective-permute-done.3.rest_5_ = bf16[3,18,8,256]{3,2,1,0:T(8,128)(2,1)S(1)} collective-permute-done((bf16[3,18,8,256]{3,2,1,0:T(8,128)(2,1)S(1)}, bf16[3,18,8,256]{3,2,1,0:T(8,128)(2,1)S(1)}, u32[]{:S(2)}, u32[]{:S(2)}) %collective-permute-start.3) | collective-permute-done | bytes 221216 | tf_op jit(solution)/shard_map/ppermute | solution.py:613
  31.1 4.6 %collective-permute-done.4.rest_6_ = bf16[3,18,8,256]{3,2,1,0:T(8,128)(2,1)S(1)} collective-permute-done((bf16[3,18,8,256]{3,2,1,0:T(8,128)(2,1)S(1)}, bf16[3,18,8,256]{3,2,1,0:T(8,128)(2,1)S(1)}, u32[]{:S(2)}, u32[]{:S(2)}) %collective-permute-start.4) | collective-permute-done | bytes 221216 | tf_op jit(solution)/shard_map/ppermute | solution.py:613
  35.8 2.8 %shard_map.86.own_ref.rest_0_ = bf16[3,10,10,16,256]{4,3,2,1,0:T(8,128)(2,1)S(1)} custom-call(s32[2,1,2]{2,1,0:T(1,128)S(1)} %bitcast.53, bf16[16,16,8,256]{3,2,1,0:T(8,128)(2,1)S(1)} %copy-done, bf16[16,16,8,256]{3,2,1,0:T(8,128)(2,1)S(1)} %copy-done.1, bf16[16,16,8,256]{3,2,1,0:T(8,128)(2,1)S(1)} %copy-done.2, ...), custom_call_target="tpu_custom_call" | custom-call | flops 1 | bytes 1 | tf_op jit(solution)/shard_map/pallas_call | solution.py:194
  38.6 0.8 collective-permute-start.10
  39.4 3.8 %collective-permute-start.13 = (bf16[4,32,1792]{2,1,0:T(8,128)(2,1)S(1)}, bf16[4,32,1792]{2,1,0:T(8,128)(2,1)S(1)}, u32[]{:S(2)}, u32[]{:S(2)}) collective-permute-start(bf16[4,32,1792]{2,1,0:T(8,128)(2,1)S(1)} %get-tuple-element.121), channel_id=1, source_target_pairs={{0,4},{1,5},{2,6},{3,7},{4,0},{5,1},{6,2},{7,3},{8,12},{9,13},{10,... | collective-permute-start | bytes 1376264 | tf_op jit(solution)/shard_map/ppermute | solution.py:51
  43.2 0.4 collective-permute-start.11
  43.7 3.0 %collective-permute-start.12 = (bf16[4,32,1792]{2,1,0:T(8,128)(2,1)S(1)}, bf16[4,32,1792]{2,1,0:T(8,128)(2,1)S(1)}, u32[]{:S(2)}, u32[]{:S(2)}) collective-permute-start(bf16[4,32,1792]{2,1,0:T(8,128)(2,1)S(1)} %pad_maximum_fusion.2), channel_id=1, source_target_pairs={{0,17},{1,16},{2,19},{3,18},{4,21},{5,20},{6,23},{7,22},{8,25},{9,... | collective-permute-start | bytes 1376264 | tf_op jit(solution)/shard_map/ppermute | solution.py:51
  46.7 5.5 %shard_map.87 = bf16[4,4,14,32,128]{4,3,2,1,0:T(8,128)(2,1)S(1)} custom-call(bf16[3,10,10,16,256]{4,3,2,1,0:T(8,128)(2,1)S(1)} %shard_map.86.own_ref.rest_0_, bf16[3,10,10,16,256]{4,3,2,1,0:T(8,128)(2,1)S(1)} %collective-permute-done.10.other_ref), custom_call_target="tpu_custom_call" | custom-call | flops 1 | bytes 1 | tf_op jit(solution)/shard_map/pallas_call | solution.py:282
  52.2 12.0 %collective-permute-done.13 = bf16[4,32,1792]{2,1,0:T(8,128)(2,1)S(1)} collective-permute-done((bf16[4,32,1792]{2,1,0:T(8,128)(2,1)S(1)}, bf16[4,32,1792]{2,1,0:T(8,128)(2,1)S(1)}, u32[]{:S(2)}, u32[]{:S(2)}) %collective-permute-start.13) | collective-permute-done | bytes 458784 | tf_op jit(solution)/shard_map/ppermute | solution.py:51
  64.2 1.5 %collective-permute-done.11 = bf16[4,32,1792]{2,1,0:T(8,128)(2,1)S(1)} collective-permute-done((bf16[4,32,1792]{2,1,0:T(8,128)(2,1)S(1)}, bf16[4,32,1792]{2,1,0:T(8,128)(2,1)S(1)}, u32[]{:S(2)}, u32[]{:S(2)}) %collective-permute-start.11) | collective-permute-done | bytes 458784 | tf_op jit(solution)/shard_map/ppermute | solution.py:51
  65.7 0.2 pad_maximum_fusion.rest_1_
  66.2 1.8 %collective-permute-start.15 = (bf16[2,2,14,32,128]{4,3,2,1,0:T(8,128)(2,1)S(1)}, bf16[2,2,14,32,128]{4,3,2,1,0:T(8,128)(2,1)S(1)}, u32[]{:S(2)}, u32[]{:S(2)}) collective-permute-start(bf16[2,2,14,32,128]{4,3,2,1,0:T(8,128)(2,1)S(1)} %pad_maximum_fusion.3), channel_id=1, source_target_pairs={{0,1},{1,0},{2,3},{3,2},{4,5},{5,4},{6,7},{7,6},{8,9},{9,8},{10,11... | collective-permute-start | bytes 1376264 | tf_op jit(solution)/shard_map/ppermute | solution.py:51
  68.0 0.4 collective-permute-start.16
  68.4 0.5 collective-permute-start.26
  68.9 0.9 collective-permute-done.14.rest_2_
  69.8 5.9 %shard_map.88 = (bf16[16,16,8,256]{3,2,1,0:T(8,128)(2,1)S(1)}, bf16[8,8,16,256]{3,2,1,0:T(8,128)(2,1)S(1)}) custom-call(s32[2,1,2]{2,1,0:T(1,128)S(1)} %bitcast.54, bf16[3,10,10,16,256]{4,3,2,1,0:T(8,128)(2,1)S(1)} %shard_map.86.own_ref.rest_0_, bf16[16,32,1792]{2,1,0:T(8,128)(2,1)S(1)} %pad_maximum_fusion.rest_1_, ...), custom_call_target="tpu_custom_call" | custom-call | flops 1 | bytes 1 | tf_op jit(solution)/shard_map/pallas_call | solution.py:390
  75.8 3.4 %collective-permute-done.15 = bf16[2,2,14,32,128]{4,3,2,1,0:T(8,128)(2,1)S(1)} collective-permute-done((bf16[2,2,14,32,128]{4,3,2,1,0:T(8,128)(2,1)S(1)}, bf16[2,2,14,32,128]{4,3,2,1,0:T(8,128)(2,1)S(1)}, u32[]{:S(2)}, u32[]{:S(2)}) %collective-permute-start.15) | collective-permute-done | bytes 458784 | tf_op jit(solution)/shard_map/ppermute | solution.py:51
  79.2 1.5 %collective-permute-done.16 = bf16[2,2,14,32,128]{4,3,2,1,0:T(8,128)(2,1)S(1)} collective-permute-done((bf16[2,2,14,32,128]{4,3,2,1,0:T(8,128)(2,1)S(1)}, bf16[2,2,14,32,128]{4,3,2,1,0:T(8,128)(2,1)S(1)}, u32[]{:S(2)}, u32[]{:S(2)}) %collective-permute-start.16) | collective-permute-done | bytes 458784 | tf_op jit(solution)/shard_map/ppermute | solution.py:51
  80.9 0.1 convert_add_fusion.3
  81.1 0.4 collective-permute-start.19
  81.5 1.4 %collective-permute-start.18 = (bf16[1,2,14,32,128]{4,3,2,1,0:T(8,128)(2,1)S(1)}, bf16[1,2,14,32,128]{4,3,2,1,0:T(8,128)(2,1)S(1)}, u32[]{:S(2)}, u32[]{:S(2)}) collective-permute-start(bf16[1,2,14,32,128]{4,3,2,1,0:T(8,128)(2,1)S(1)} %slice.256), channel_id=1, source_target_pairs={{0,16},{1,17},{2,18},{3,19},{4,20},{5,21},{6,22},{7,23},{8,24},{9,... | collective-permute-start | bytes 688136 | tf_op jit(solution)/shard_map/ppermute | solution.py:51
  82.9 5.3 %shard_map.89 = bf16[4,4,14,32,128]{4,3,2,1,0:T(8,128)(2,1)S(1)} custom-call(bf16[3,10,10,16,256]{4,3,2,1,0:T(8,128)(2,1)S(1)} %shard_map.86.own_ref.rest_0_, bf16[3,10,10,16,256]{4,3,2,1,0:T(8,128)(2,1)S(1)} %collective-permute-done.10.other_ref, bf16[8,8,16,256]{3,2,1,0:T(8,128)(2,1)S(1)} %get-tuple-element.78.rest_0_, ...), custom_call_target="tpu_custom_call" | custom-call | flops 1 | bytes 1 | tf_op jit(solution)/shard_map/pallas_call | solution.py:282
  88.2 0.9 collective-permute-done.19
  89.4 1.7 %collective-permute-start.22 = (bf16[2,2,14,32,128]{4,3,2,1,0:T(8,128)(2,1)S(1)}, bf16[2,2,14,32,128]{4,3,2,1,0:T(8,128)(2,1)S(1)}, u32[]{:S(2)}, u32[]{:S(2)}) collective-permute-start(bf16[2,2,14,32,128]{4,3,2,1,0:T(8,128)(2,1)S(1)} %pad_maximum_fusion.4), channel_id=1, source_target_pairs={{0,1},{1,0},{2,3},{3,2},{4,5},{5,4},{6,7},{7,6},{8,9},{9,8},{10,11... | collective-permute-start | bytes 1376264 | tf_op jit(solution)/shard_map/ppermute | solution.py:51
  91.1 0.4 collective-permute-start.23
  91.8 0.6 collective-permute-start.33
  92.4 1.3 collective-permute-start.20
  93.7 1.5 %collective-permute-start.21 = (bf16[1,16,8,256]{3,2,1,0:T(8,128)(2,1)S(1)}, bf16[1,16,8,256]{3,2,1,0:T(8,128)(2,1)S(1)}, u32[]{:S(2)}, u32[]{:S(2)}) collective-permute-start(bf16[1,16,8,256]{3,2,1,0:T(8,128)(2,1)S(1)} %get-tuple-element.83), channel_id=1, source_target_pairs={{8,0},{16,8},{24,16},{9,1},{17,9},{25,17},{10,2},{18,10},{26,18},{... | collective-permute-start | bytes 196616 | tf_op jit(solution)/shard_map/ppermute | solution.py:601
  95.3 4.9 %collective-permute-start.27 = (bf16[16,32,1792]{2,1,0:T(8,128)(2,1)S(1)}, bf16[16,32,1792]{2,1,0:T(8,128)(2,1)}, u32[]{:S(2)}, u32[]{:S(2)}) collective-permute-start(bf16[16,32,1792]{2,1,0:T(8,128)(2,1)S(1)} %constant_dynamic-update-slice_fusion.9.rest_5_), channel_id=1, source_target_pairs={{0,8},{1,9},{2,10},{3,11},{4,12},{5,13},{6,14},{7,15},{8,0},{9,1},... | collective-permute-start | bytes 5505032 | tf_op jit(solution)/shard_map/ppermute | solution.py:51
  100.1 0.6 pad_maximum_fusion.9
  100.9 0.6 collective-permute-done.22
  101.5 1.1 collective-permute-done.23
  102.8 0.1 convert_add_fusion.1
  103.0 0.9 slice.253
  104.0 0.7 slice.254
  104.7 0.7 slice.257
  105.4 0.3 collective-permute-start.34
  105.6 0.7 collective-permute-start.29
  106.4 2.3 %collective-permute-start.28 = (bf16[1,2,14,32,128]{4,3,2,1,0:T(8,128)(2,1)}, bf16[1,2,14,32,128]{4,3,2,1,0:T(8,128)(2,1)S(1)}, u32[]{:S(2)}, u32[]{:S(2)}) collective-permute-start(bf16[1,2,14,32,128]{4,3,2,1,0:T(8,128)(2,1)} %slice.254), channel_id=1, source_target_pairs={{0,16},{1,17},{2,18},{3,19},{4,20},{5,21},{6,22},{7,23},{8,24},{9,... | collective-permute-start | bytes 688136 | tf_op jit(solution)/shard_map/ppermute | solution.py:51
  108.6 2.5 %collective-permute-start.24 = (bf16[1,18,8,256]{3,2,1,0:T(8,128)(2,1)}, bf16[1,18,8,256]{3,2,1,0:T(8,128)(2,1)S(1)}, u32[]{:S(2)}, u32[]{:S(2)}) collective-permute-start(bf16[1,18,8,256]{3,2,1,0:T(8,128)(2,1)} %pad_maximum_fusion.9), channel_id=1, source_target_pairs={{0,1},{1,2},{2,3},{3,4},{4,5},{5,6},{6,7},{8,9},{9,10},{10,11},{11... | collective-permute-start | bytes 221192 | tf_op jit(solution)/shard_map/ppermute | solution.py:613
  111.1 3.6 %collective-permute-done.34 = bf16[1,14,32,128]{3,2,1,0:T(8,128)(2,1)} collective-permute-done((bf16[1,14,32,128]{3,2,1,0:T(8,128)(2,1)}, bf16[1,14,32,128]{3,2,1,0:T(8,128)(2,1)}, u32[]{:S(2)}, u32[]{:S(2)}) %collective-permute-start.34) | collective-permute-done | bytes 114720 | tf_op jit(solution)/shard_map/ppermute | solution.py:51
  114.8 1.3 collective-permute-start.25
  116.1 0.9 copy_bitcast_fusion
  117.0 1.1 fusion.2
  118.1 1.6 %collective-permute-start.31 = (bf16[14,32,128]{2,1,0:T(8,128)(2,1)S(1)}, bf16[14,32,128]{2,1,0:T(8,128)(2,1)S(1)}, u32[]{:S(2)}, u32[]{:S(2)}) collective-permute-start(bf16[14,32,128]{2,1,0:T(8,128)(2,1)S(1)} %get-tuple-element.114), channel_id=1, source_target_pairs={{0,4},{1,5},{2,6},{3,7},{4,0},{5,1},{6,2},{7,3},{8,12},{9,13},{10,... | collective-permute-start | bytes 344072 | tf_op jit(solution)/shard_map/ppermute | solution.py:51
  119.7 3.5 %collective-permute-start.32 = (bf16[14,32,128]{2,1,0:T(8,128)(2,1)S(1)}, bf16[14,32,128]{2,1,0:T(8,128)(2,1)S(1)}, u32[]{:S(2)}, u32[]{:S(2)}) collective-permute-start(bf16[14,32,128]{2,1,0:T(8,128)(2,1)S(1)} %get-tuple-element.113), channel_id=1, source_target_pairs={{0,6},{1,7},{2,4},{3,5},{4,2},{5,3},{6,0},{7,1},{8,14},{9,15},{10,... | collective-permute-start | bytes 344072 | tf_op jit(solution)/shard_map/ppermute | solution.py:51
  123.4 0.8 dynamic-slice_bitcast_fusion
  124.2 8.2 %shard_map.90 = bf16[16,16,8,256]{3,2,1,0:T(8,128)(2,1)} custom-call(s32[2,1,2]{2,1,0:T(1,128)S(1)} %bitcast.55, bf16[16,16,8,256]{3,2,1,0:T(8,128)(2,1)S(1)} %get-tuple-element.74.rest_0_, bf16[1,16,8,256]{3,2,1,0:T(8,128)(2,1)S(1)} %collective-permute-done.20.rest_1_, bf16[1,16,8,256]{3,2,1,0:T(8,128)(2,1)S(1)} %collective-permute-done.21.rest_2_, ...), custom_call_target="tpu_custom_call" | custom-call | flops 1 | bytes 1 | tf_op jit(solution)/shard_map/pallas_call | solution.py:390
  132.5 0.8 dynamic-slice_bitcast_fusion.1
  (77 shorter events, 1.9 us)
Async XLA Ops:
  3.9 15.6 %copy-start.8 = (bf16[32,1792]{1,0:T(8,128)(2,1)S(1)}, bf16[32,1792]{1,0:T(8,128)(2,1)}, u32[]{:S(2)}) copy-start(bf16[32,1792]{1,0:T(8,128)(2,1)} %get-tuple-element.58) | copy-start | bytes 344068
  3.9 24.9 %copy-start.7 = (bf16[32,1792]{1,0:T(8,128)(2,1)S(1)}, bf16[32,1792]{1,0:T(8,128)(2,1)}, u32[]{:S(2)}) copy-start(bf16[32,1792]{1,0:T(8,128)(2,1)} %get-tuple-element.55) | copy-start | bytes 344068
  3.9 9.9 %collective-permute-start.2 = (bf16[1,32,1792]{2,1,0:T(8,128)(2,1)}, bf16[1,32,1792]{2,1,0:T(8,128)(2,1)S(1)}, u32[]{:S(2)}, u32[]{:S(2)}) collective-permute-start(bf16[1,32,1792]{2,1,0:T(8,128)(2,1)} %bitcast.56), channel_id=1, source_target_pairs={{0,4},{1,5},{2,6},{3,7},{4,0},{5,1},{6,2},{7,3},{8,12},{9,13},{10,... | collective-permute-start | bytes 344072 | tf_op jit(solution)/shard_map/ppermute | solution.py:51
  8.0 7.6 %collective-permute-start = (bf16[3,16,8,256]{3,2,1,0:T(8,128)(2,1)}, bf16[3,16,8,256]{3,2,1,0:T(8,128)(2,1)S(1)}, u32[]{:S(2)}, u32[]{:S(2)}) collective-permute-start(bf16[3,16,8,256]{3,2,1,0:T(8,128)(2,1)} %get-tuple-element.51), channel_id=1, source_target_pairs={{0,8},{8,16},{16,24},{1,9},{9,17},{17,25},{2,10},{10,18},{18,26},{... | collective-permute-start | bytes 589832 | tf_op jit(solution)/shard_map/ppermute | solution.py:601
  9.4 6.2 %collective-permute-start.1 = (bf16[3,16,8,256]{3,2,1,0:T(8,128)(2,1)}, bf16[3,16,8,256]{3,2,1,0:T(8,128)(2,1)S(1)}, u32[]{:S(2)}, u32[]{:S(2)}) collective-permute-start(bf16[3,16,8,256]{3,2,1,0:T(8,128)(2,1)} %get-tuple-element.52), channel_id=1, source_target_pairs={{8,0},{16,8},{24,16},{9,1},{17,9},{25,17},{10,2},{18,10},{26,18},{... | collective-permute-start | bytes 589832 | tf_op jit(solution)/shard_map/ppermute | solution.py:601
  14.7 14.0 %collective-permute-start.8 = (bf16[2,32,1792]{2,1,0:T(8,128)(2,1)S(1)}, bf16[2,32,1792]{2,1,0:T(8,128)(2,1)S(1)}, u32[]{:S(2)}, u32[]{:S(2)}) collective-permute-start(bf16[2,32,1792]{2,1,0:T(8,128)(2,1)S(1)} %pad_maximum_fusion.5), channel_id=1, source_target_pairs={{0,2},{1,3},{2,0},{3,1},{4,6},{5,7},{6,4},{7,5},{8,10},{9,11},{10,... | collective-permute-start | bytes 688136 | tf_op jit(solution)/shard_map/ppermute | solution.py:51
  15.6 20.1 %copy-start = (bf16[16,16,8,256]{3,2,1,0:T(8,128)(2,1)S(1)}, bf16[16,16,8,256]{3,2,1,0:T(8,128)(2,1)}, u32[]{:S(2)}) copy-start(bf16[16,16,8,256]{3,2,1,0:T(8,128)(2,1)} %rest_3_.1) | copy-start | bytes 3145732
  15.6 20.1 %copy-start.1 = (bf16[16,16,8,256]{3,2,1,0:T(8,128)(2,1)S(1)}, bf16[16,16,8,256]{3,2,1,0:T(8,128)(2,1)}, u32[]{:S(2)}) copy-start(bf16[16,16,8,256]{3,2,1,0:T(8,128)(2,1)} %rest_1_.3) | copy-start | bytes 3145732
  15.7 20.1 %copy-start.2 = (bf16[16,16,8,256]{3,2,1,0:T(8,128)(2,1)S(1)}, bf16[16,16,8,256]{3,2,1,0:T(8,128)(2,1)}, u32[]{:S(2)}) copy-start(bf16[16,16,8,256]{3,2,1,0:T(8,128)(2,1)} %rest_2_.3) | copy-start | bytes 3145732
  15.7 20.1 %copy-start.3 = (s32[2,2,1]{1,2,0:T(1,128)S(1)}, s32[2,2,1]{1,2,0:T(1,128)}, u32[]{:S(2)}) copy-start(s32[2,2,1]{1,2,0:T(1,128)} %param.11) | copy-start | bytes 52
  16.9 8.9 %collective-permute-start.5 = (bf16[1,32,1792]{2,1,0:T(8,128)(2,1)}, bf16[1,32,1792]{2,1,0:T(8,128)(2,1)S(1)}, u32[]{:S(2)}, u32[]{:S(2)}) collective-permute-start(bf16[1,32,1792]{2,1,0:T(8,128)(2,1)} %bitcast.59), channel_id=1, source_target_pairs={{0,1},{1,0},{2,3},{3,2},{4,5},{5,4},{6,7},{7,6},{8,9},{9,8},{10,11... | collective-permute-start | bytes 344072 | tf_op jit(solution)/shard_map/ppermute | solution.py:51
  19.4 8.5 %collective-permute-start.6 = (bf16[1,32,1792]{2,1,0:T(8,128)(2,1)S(1)}, bf16[1,32,1792]{2,1,0:T(8,128)(2,1)S(1)}, u32[]{:S(2)}, u32[]{:S(2)}) collective-permute-start(bf16[1,32,1792]{2,1,0:T(8,128)(2,1)S(1)} %bitcast.61), channel_id=1, source_target_pairs={{0,16},{1,17},{2,18},{3,19},{4,20},{5,21},{6,22},{7,23},{8,24},{9,... | collective-permute-start | bytes 344072 | tf_op jit(solution)/shard_map/ppermute | solution.py:51
  22.4 6.3 %collective-permute-start.7 = (bf16[1,32,1792]{2,1,0:T(8,128)(2,1)S(1)}, bf16[1,32,1792]{2,1,0:T(8,128)(2,1)S(1)}, u32[]{:S(2)}, u32[]{:S(2)}) collective-permute-start(bf16[1,32,1792]{2,1,0:T(8,128)(2,1)S(1)} %bitcast.62), channel_id=1, source_target_pairs={{0,17},{1,16},{2,19},{3,18},{4,21},{5,20},{6,23},{7,22},{8,25},{9,... | collective-permute-start | bytes 344072 | tf_op jit(solution)/shard_map/ppermute | solution.py:51
  22.5 8.6 %collective-permute-start.3 = (bf16[3,18,8,256]{3,2,1,0:T(8,128)(2,1)S(1)}, bf16[3,18,8,256]{3,2,1,0:T(8,128)(2,1)S(1)}, u32[]{:S(2)}, u32[]{:S(2)}) collective-permute-start(bf16[3,18,8,256]{3,2,1,0:T(8,128)(2,1)S(1)} %get-tuple-element.56), channel_id=1, source_target_pairs={{0,1},{1,2},{2,3},{3,4},{4,5},{5,6},{6,7},{8,9},{9,10},{10,11},{11... | collective-permute-start | bytes 663560 | tf_op jit(solution)/shard_map/ppermute | solution.py:613
  25.9 9.9 %collective-permute-start.4 = (bf16[3,18,8,256]{3,2,1,0:T(8,128)(2,1)S(1)}, bf16[3,18,8,256]{3,2,1,0:T(8,128)(2,1)S(1)}, u32[]{:S(2)}, u32[]{:S(2)}) collective-permute-start(bf16[3,18,8,256]{3,2,1,0:T(8,128)(2,1)S(1)} %get-tuple-element.57), channel_id=1, source_target_pairs={{1,0},{2,1},{3,2},{4,3},{5,4},{6,5},{7,6},{9,8},{10,9},{11,10},{12... | collective-permute-start | bytes 663560 | tf_op jit(solution)/shard_map/ppermute | solution.py:613
  38.6 8.1 %collective-permute-start.10 = (bf16[3,10,10,16,256]{4,3,2,1,0:T(8,128)(2,1)S(1)}, bf16[3,10,10,16,256]{4,3,2,1,0:T(8,128)(2,1)S(1)}, u32[]{:S(2)}, u32[]{:S(2)}) collective-permute-start(bf16[3,10,10,16,256]{4,3,2,1,0:T(8,128)(2,1)S(1)} %shard_map.86.own_ref.rest_0_), channel_id=1, source_target_pairs={{0,8},{1,9},{2,10},{3,11},{4,12},{5,13},{6,14},{7,15},{8,0},{9,1},... | collective-permute-start | bytes 7372808 | tf_op jit(solution)/shard_map/ppermute | solution.py:51
  39.4 24.7 %collective-permute-start.13 = (bf16[4,32,1792]{2,1,0:T(8,128)(2,1)S(1)}, bf16[4,32,1792]{2,1,0:T(8,128)(2,1)S(1)}, u32[]{:S(2)}, u32[]{:S(2)}) collective-permute-start(bf16[4,32,1792]{2,1,0:T(8,128)(2,1)S(1)} %get-tuple-element.121), channel_id=1, source_target_pairs={{0,4},{1,5},{2,6},{3,7},{4,0},{5,1},{6,2},{7,3},{8,12},{9,13},{10,... | collective-permute-start | bytes 1376264 | tf_op jit(solution)/shard_map/ppermute | solution.py:51
  43.2 20.9 %collective-permute-start.9 = (bf16[4,32,1792]{2,1,0:T(8,128)(2,1)S(1)}, bf16[4,32,1792]{2,1,0:T(8,128)(2,1)S(1)}, u32[]{:S(2)}, u32[]{:S(2)}) collective-permute-start(bf16[4,32,1792]{2,1,0:T(8,128)(2,1)S(1)} %pad_maximum_fusion.2), channel_id=1, source_target_pairs={{0,1},{1,0},{2,3},{3,2},{4,5},{5,4},{6,7},{7,6},{8,9},{9,8},{10,11... | collective-permute-start | bytes 1376264 | tf_op jit(solution)/shard_map/ppermute | solution.py:51
  43.2 22.4 %collective-permute-start.11 = (bf16[4,32,1792]{2,1,0:T(8,128)(2,1)S(1)}, bf16[4,32,1792]{2,1,0:T(8,128)(2,1)S(1)}, u32[]{:S(2)}, u32[]{:S(2)}) collective-permute-start(bf16[4,32,1792]{2,1,0:T(8,128)(2,1)S(1)} %pad_maximum_fusion.2), channel_id=1, source_target_pairs={{0,16},{1,17},{2,18},{3,19},{4,20},{5,21},{6,22},{7,23},{8,24},{9,... | collective-permute-start | bytes 1376264 | tf_op jit(solution)/shard_map/ppermute | solution.py:51
  43.7 22.0 %collective-permute-start.12 = (bf16[4,32,1792]{2,1,0:T(8,128)(2,1)S(1)}, bf16[4,32,1792]{2,1,0:T(8,128)(2,1)S(1)}, u32[]{:S(2)}, u32[]{:S(2)}) collective-permute-start(bf16[4,32,1792]{2,1,0:T(8,128)(2,1)S(1)} %pad_maximum_fusion.2), channel_id=1, source_target_pairs={{0,17},{1,16},{2,19},{3,18},{4,21},{5,20},{6,23},{7,22},{8,25},{9,... | collective-permute-start | bytes 1376264 | tf_op jit(solution)/shard_map/ppermute | solution.py:51
  66.0 3.9 %collective-permute-start.14 = (bf16[16,32,1792]{2,1,0:T(8,128)(2,1)S(1)}, bf16[16,32,1792]{2,1,0:T(8,128)(2,1)S(1)}, u32[]{:S(2)}, u32[]{:S(2)}) collective-permute-start(bf16[16,32,1792]{2,1,0:T(8,128)(2,1)S(1)} %pad_maximum_fusion.rest_1_), channel_id=1, source_target_pairs={{0,8},{1,9},{2,10},{3,11},{4,12},{5,13},{6,14},{7,15},{8,0},{9,1},... | collective-permute-start | bytes 5505032 | tf_op jit(solution)/shard_map/ppermute | solution.py:51
  66.2 13.0 %collective-permute-start.15 = (bf16[2,2,14,32,128]{4,3,2,1,0:T(8,128)(2,1)S(1)}, bf16[2,2,14,32,128]{4,3,2,1,0:T(8,128)(2,1)S(1)}, u32[]{:S(2)}, u32[]{:S(2)}) collective-permute-start(bf16[2,2,14,32,128]{4,3,2,1,0:T(8,128)(2,1)S(1)} %pad_maximum_fusion.3), channel_id=1, source_target_pairs={{0,1},{1,0},{2,3},{3,2},{4,5},{5,4},{6,7},{7,6},{8,9},{9,8},{10,11... | collective-permute-start | bytes 1376264 | tf_op jit(solution)/shard_map/ppermute | solution.py:51
  68.0 12.6 %collective-permute-start.16 = (bf16[2,2,14,32,128]{4,3,2,1,0:T(8,128)(2,1)S(1)}, bf16[2,2,14,32,128]{4,3,2,1,0:T(8,128)(2,1)S(1)}, u32[]{:S(2)}, u32[]{:S(2)}) collective-permute-start(bf16[2,2,14,32,128]{4,3,2,1,0:T(8,128)(2,1)S(1)} %concatenate.80), channel_id=1, source_target_pairs={{0,16},{1,17},{2,18},{3,19},{4,20},{5,21},{6,22},{7,23},{8,24},{9,... | collective-permute-start | bytes 1376264 | tf_op jit(solution)/shard_map/ppermute | solution.py:51
  68.4 25.3 %collective-permute-start.26 = (bf16[8,32,1792]{2,1,0:T(8,128)(2,1)S(1)}, bf16[8,32,1792]{2,1,0:T(8,128)(2,1)S(1)}, u32[]{:S(2)}, u32[]{:S(2)}) collective-permute-start(bf16[8,32,1792]{2,1,0:T(8,128)(2,1)S(1)} %get-tuple-element.90), channel_id=1, source_target_pairs={{0,2},{1,3},{2,0},{3,1},{4,6},{5,7},{6,4},{7,5},{8,10},{9,11},{10,... | collective-permute-start | bytes 2752520 | tf_op jit(solution)/shard_map/ppermute | solution.py:51
  80.8 2.1 %collective-permute-start.17 = (bf16[8,8,16,256]{3,2,1,0:T(8,128)(2,1)S(1)}, bf16[8,8,16,256]{3,2,1,0:T(8,128)(2,1)S(1)}, u32[]{:S(2)}, u32[]{:S(2)}) collective-permute-start(bf16[8,8,16,256]{3,2,1,0:T(8,128)(2,1)S(1)} %get-tuple-element.78.rest_0_), channel_id=1, source_target_pairs={{0,8},{1,9},{2,10},{3,11},{4,12},{5,13},{6,14},{7,15},{8,0},{9,1},... | collective-permute-start | bytes 1572872 | tf_op jit(solution)/shard_map/ppermute | solution.py:51
  81.1 8.1 %collective-permute-start.19 = (bf16[1,2,14,32,128]{4,3,2,1,0:T(8,128)(2,1)S(1)}, bf16[1,2,14,32,128]{4,3,2,1,0:T(8,128)(2,1)S(1)}, u32[]{:S(2)}, u32[]{:S(2)}) collective-permute-start(bf16[1,2,14,32,128]{4,3,2,1,0:T(8,128)(2,1)S(1)} %slice.255), channel_id=1, source_target_pairs={{0,1},{1,0},{2,3},{3,2},{4,5},{5,4},{6,7},{7,6},{8,9},{9,8},{10,11... | collective-permute-start | bytes 688136 | tf_op jit(solution)/shard_map/ppermute | solution.py:51
  81.5 7.7 %collective-permute-start.18 = (bf16[1,2,14,32,128]{4,3,2,1,0:T(8,128)(2,1)S(1)}, bf16[1,2,14,32,128]{4,3,2,1,0:T(8,128)(2,1)S(1)}, u32[]{:S(2)}, u32[]{:S(2)}) collective-permute-start(bf16[1,2,14,32,128]{4,3,2,1,0:T(8,128)(2,1)S(1)} %slice.256), channel_id=1, source_target_pairs={{0,16},{1,17},{2,18},{3,19},{4,20},{5,21},{6,22},{7,23},{8,24},{9,... | collective-permute-start | bytes 688136 | tf_op jit(solution)/shard_map/ppermute | solution.py:51
  89.4 12.1 %collective-permute-start.22 = (bf16[2,2,14,32,128]{4,3,2,1,0:T(8,128)(2,1)S(1)}, bf16[2,2,14,32,128]{4,3,2,1,0:T(8,128)(2,1)S(1)}, u32[]{:S(2)}, u32[]{:S(2)}) collective-permute-start(bf16[2,2,14,32,128]{4,3,2,1,0:T(8,128)(2,1)S(1)} %pad_maximum_fusion.4), channel_id=1, source_target_pairs={{0,1},{1,0},{2,3},{3,2},{4,5},{5,4},{6,7},{7,6},{8,9},{9,8},{10,11... | collective-permute-start | bytes 1376264 | tf_op jit(solution)/shard_map/ppermute | solution.py:51
  91.1 11.5 %collective-permute-start.23 = (bf16[2,2,14,32,128]{4,3,2,1,0:T(8,128)(2,1)S(1)}, bf16[2,2,14,32,128]{4,3,2,1,0:T(8,128)(2,1)S(1)}, u32[]{:S(2)}, u32[]{:S(2)}) collective-permute-start(bf16[2,2,14,32,128]{4,3,2,1,0:T(8,128)(2,1)S(1)} %concatenate.73), channel_id=1, source_target_pairs={{0,16},{1,17},{2,18},{3,19},{4,20},{5,21},{6,22},{7,23},{8,24},{9,... | collective-permute-start | bytes 1376264 | tf_op jit(solution)/shard_map/ppermute | solution.py:51
  91.8 9.0 %collective-permute-start.33 = (bf16[2,14,32,128]{3,2,1,0:T(8,128)(2,1)S(1)}, bf16[2,14,32,128]{3,2,1,0:T(8,128)(2,1)S(1)}, u32[]{:S(2)}, u32[]{:S(2)}) collective-permute-start(bf16[2,14,32,128]{3,2,1,0:T(8,128)(2,1)S(1)} %slice.188), channel_id=1, source_target_pairs={{0,2},{1,3},{2,0},{3,1},{4,6},{5,7},{6,4},{7,5},{8,10},{9,11},{10,... | collective-permute-start | bytes 688136 | tf_op jit(solution)/shard_map/ppermute | solution.py:51
  92.4 2.9 %collective-permute-start.20 = (bf16[1,16,8,256]{3,2,1,0:T(8,128)(2,1)S(1)}, bf16[1,16,8,256]{3,2,1,0:T(8,128)(2,1)S(1)}, u32[]{:S(2)}, u32[]{:S(2)}) collective-permute-start(bf16[1,16,8,256]{3,2,1,0:T(8,128)(2,1)S(1)} %get-tuple-element.82), channel_id=1, source_target_pairs={{0,8},{8,16},{16,24},{1,9},{9,17},{17,25},{2,10},{10,18},{18,26},{... | collective-permute-start | bytes 196616 | tf_op jit(solution)/shard_map/ppermute | solution.py:601
  93.7 6.5 %collective-permute-start.21 = (bf16[1,16,8,256]{3,2,1,0:T(8,128)(2,1)S(1)}, bf16[1,16,8,256]{3,2,1,0:T(8,128)(2,1)S(1)}, u32[]{:S(2)}, u32[]{:S(2)}) collective-permute-start(bf16[1,16,8,256]{3,2,1,0:T(8,128)(2,1)S(1)} %get-tuple-element.83), channel_id=1, source_target_pairs={{8,0},{16,8},{24,16},{9,1},{17,9},{25,17},{10,2},{18,10},{26,18},{... | collective-permute-start | bytes 196616 | tf_op jit(solution)/shard_map/ppermute | solution.py:601
  95.3 29.0 %collective-permute-start.27 = (bf16[16,32,1792]{2,1,0:T(8,128)(2,1)S(1)}, bf16[16,32,1792]{2,1,0:T(8,128)(2,1)}, u32[]{:S(2)}, u32[]{:S(2)}) collective-permute-start(bf16[16,32,1792]{2,1,0:T(8,128)(2,1)S(1)} %constant_dynamic-update-slice_fusion.9.rest_5_), channel_id=1, source_target_pairs={{0,8},{1,9},{2,10},{3,11},{4,12},{5,13},{6,14},{7,15},{8,0},{9,1},... | collective-permute-start | bytes 5505032 | tf_op jit(solution)/shard_map/ppermute | solution.py:51
  102.8 1.9 %copy-start.6 = (f32[2,2,14,32,128]{4,3,2,1,0:T(8,128)}, f32[2,2,14,32,128]{4,3,2,1,0:T(8,128)S(1)}, u32[]{:S(2)}) copy-start(f32[2,2,14,32,128]{4,3,2,1,0:T(8,128)S(1)} %convert_add_fusion) | copy-start | bytes 2752516
  102.9 1.0 copy-start.4
  105.4 9.4 %collective-permute-start.34 = (bf16[1,14,32,128]{3,2,1,0:T(8,128)(2,1)}, bf16[1,14,32,128]{3,2,1,0:T(8,128)(2,1)}, u32[]{:S(2)}, u32[]{:S(2)}) collective-permute-start(bf16[1,14,32,128]{3,2,1,0:T(8,128)(2,1)} %slice.257), channel_id=1, source_target_pairs={{0,4},{1,5},{2,6},{3,7},{4,0},{5,1},{6,2},{7,3},{8,12},{9,13},{10,... | collective-permute-start | bytes 344072 | tf_op jit(solution)/shard_map/ppermute | solution.py:51
  105.6 17.6 %copy-start.5 = (f32[2,2,14,32,128]{4,3,2,1,0:T(8,128)S(1)}, f32[2,2,14,32,128]{4,3,2,1,0:T(8,128)}, u32[]{:S(2)}) copy-start(f32[2,2,14,32,128]{4,3,2,1,0:T(8,128)} %copy-done.4) | copy-start | bytes 2752516
  105.6 11.3 %collective-permute-start.29 = (bf16[1,2,14,32,128]{4,3,2,1,0:T(8,128)(2,1)}, bf16[1,2,14,32,128]{4,3,2,1,0:T(8,128)(2,1)S(1)}, u32[]{:S(2)}, u32[]{:S(2)}) collective-permute-start(bf16[1,2,14,32,128]{4,3,2,1,0:T(8,128)(2,1)} %slice.253), channel_id=1, source_target_pairs={{0,1},{1,0},{2,3},{3,2},{4,5},{5,4},{6,7},{7,6},{8,9},{9,8},{10,11... | collective-permute-start | bytes 688136 | tf_op jit(solution)/shard_map/ppermute | solution.py:51
  106.4 10.6 %collective-permute-start.28 = (bf16[1,2,14,32,128]{4,3,2,1,0:T(8,128)(2,1)}, bf16[1,2,14,32,128]{4,3,2,1,0:T(8,128)(2,1)S(1)}, u32[]{:S(2)}, u32[]{:S(2)}) collective-permute-start(bf16[1,2,14,32,128]{4,3,2,1,0:T(8,128)(2,1)} %slice.254), channel_id=1, source_target_pairs={{0,16},{1,17},{2,18},{3,19},{4,20},{5,21},{6,22},{7,23},{8,24},{9,... | collective-permute-start | bytes 688136 | tf_op jit(solution)/shard_map/ppermute | solution.py:51
  108.6 14.7 %collective-permute-start.24 = (bf16[1,18,8,256]{3,2,1,0:T(8,128)(2,1)}, bf16[1,18,8,256]{3,2,1,0:T(8,128)(2,1)S(1)}, u32[]{:S(2)}, u32[]{:S(2)}) collective-permute-start(bf16[1,18,8,256]{3,2,1,0:T(8,128)(2,1)} %pad_maximum_fusion.9), channel_id=1, source_target_pairs={{0,1},{1,2},{2,3},{3,4},{4,5},{5,6},{6,7},{8,9},{9,10},{10,11},{11... | collective-permute-start | bytes 221192 | tf_op jit(solution)/shard_map/ppermute | solution.py:613
  114.8 9.5 %collective-permute-start.25 = (bf16[1,18,8,256]{3,2,1,0:T(8,128)(2,1)S(1)}, bf16[1,18,8,256]{3,2,1,0:T(8,128)(2,1)S(1)}, u32[]{:S(2)}, u32[]{:S(2)}) collective-permute-start(bf16[1,18,8,256]{3,2,1,0:T(8,128)(2,1)S(1)} %pad_maximum_fusion.8), channel_id=1, source_target_pairs={{1,0},{2,1},{3,2},{4,3},{5,4},{6,5},{7,6},{9,8},{10,9},{11,10},{12... | collective-permute-start | bytes 221192 | tf_op jit(solution)/shard_map/ppermute | solution.py:613
  118.1 14.3 %collective-permute-start.31 = (bf16[14,32,128]{2,1,0:T(8,128)(2,1)S(1)}, bf16[14,32,128]{2,1,0:T(8,128)(2,1)S(1)}, u32[]{:S(2)}, u32[]{:S(2)}) collective-permute-start(bf16[14,32,128]{2,1,0:T(8,128)(2,1)S(1)} %get-tuple-element.114), channel_id=1, source_target_pairs={{0,4},{1,5},{2,6},{3,7},{4,0},{5,1},{6,2},{7,3},{8,12},{9,13},{10,... | collective-permute-start | bytes 344072 | tf_op jit(solution)/shard_map/ppermute | solution.py:51
  119.7 12.7 %collective-permute-start.32 = (bf16[14,32,128]{2,1,0:T(8,128)(2,1)S(1)}, bf16[14,32,128]{2,1,0:T(8,128)(2,1)S(1)}, u32[]{:S(2)}, u32[]{:S(2)}) collective-permute-start(bf16[14,32,128]{2,1,0:T(8,128)(2,1)S(1)} %get-tuple-element.113), channel_id=1, source_target_pairs={{0,6},{1,7},{2,4},{3,5},{4,2},{5,3},{6,0},{7,1},{8,14},{9,15},{10,... | collective-permute-start | bytes 344072 | tf_op jit(solution)/shard_map/ppermute | solution.py:51
  123.3 9.1 %collective-permute-start.30 = (bf16[14,32,128]{2,1,0:T(8,128)(2,1)S(1)}, bf16[14,32,128]{2,1,0:T(8,128)(2,1)S(1)}, u32[]{:S(2)}, u32[]{:S(2)}) collective-permute-start(bf16[14,32,128]{2,1,0:T(8,128)(2,1)S(1)} %fusion.8), channel_id=1, source_target_pairs={{0,2},{1,3},{2,0},{3,1},{4,6},{5,7},{6,4},{7,5},{8,10},{9,11},{10,... | collective-permute-start | bytes 344072 | tf_op jit(solution)/shard_map/ppermute | solution.py:51

commit v5 on v4

--- a/solution.py
+++ b/solution.py
@@ -304,7 +304,7 @@
     else:
         out_ref = rest[0]
         rest = rest[1:]
-    ext_ref, shifted_ref, weight_ref, total_ref, sems = rest
+    ext_ref, shifted_ref, weight_ref, total_ref, sems, weight_sems = rest
     edge = B
     blocks = pick_blocks(occ_ref, n_bx, n_by)
     my_gx = lax.axis_index("gx")
@@ -312,10 +312,17 @@
     copies = [] if n_sources == 1 else extended_copies(0, *source_refs, ext_ref, sems)
     for copy in copies:
         copy.start()
-    for piece_ref, flips in zip(piece_refs, distances):
+    late = []
+    for piece, (piece_ref, flips) in enumerate(zip(piece_refs, distances)):
         for place, (flip_gx, flip_gy) in enumerate(flips):
             start = pl.multiple_of((my_gy ^ flip_gy) * plan.cols, plan.cols)
-            weight_ref[my_gx ^ flip_gx, pl.ds(start, plan.cols)] = piece_ref[place]
+            rows = weight_ref.at[my_gx ^ flip_gx, pl.ds(start, plan.cols)]
+            if not gated and piece == 1:
+                copy = pltpu.make_async_copy(piece_ref.at[place], rows, weight_sems.at[place])
+                copy.start()
+                late.append(copy)
+            else:
+                rows[...] = piece_ref[place]
     out_ref[...] = jnp.zeros_like(out_ref)
     for copy in copies:
         copy.wait()
@@ -327,6 +334,8 @@
         spread_rows(source_refs[0].at[2], put)
     else:
         spread_patches(occ_ref, blocks, ext_ref, shifted_ref, n_bx, n_by)
+    for copy in late:
+        copy.wait()
 
     def kernel_lanes(tile):
         total = None
@@ -381,7 +390,8 @@
     size_x, size_y, edge, chans = shape
     smem = pl.BlockSpec(memory_space=pltpu.SMEM)
     vmem = pl.BlockSpec(memory_space=pltpu.VMEM)
-    source = vmem if len(sources) == 1 else pl.BlockSpec(memory_space=pl.ANY)
+    anywhere = pl.BlockSpec(memory_space=pl.ANY)
+    source = vmem if len(sources) == 1 else anywhere
     voxels = B * B * AMAX * B
     gated = gate is not None
     out_shape = [jax.ShapeDtypeStruct(shape, jnp.bfloat16)]
@@ -390,7 +400,7 @@
     return pl.pallas_call(
         functools.partial(data_kernel, plan, n_bx, n_by, len(sources), gated, distances),
         out_shape=out_shape,
-        in_specs=[smem] + [source] * len(sources) + [vmem] * (len(pieces) + gated),
+        in_specs=[smem] + [source] * len(sources) + [vmem, vmem if gated else anywhere] + [vmem] * gated,
         out_specs=[vmem] * len(out_shape),
         scratch_shapes=[
             pltpu.VMEM((size_x + 2, size_y + 2, edge, chans), jnp.bfloat16),
@@ -398,6 +408,7 @@
             pltpu.VMEM((plan.n_gx, chans, plan.depth * LANES), jnp.bfloat16),
             pltpu.VMEM((voxels, chans), jnp.float32),
             pltpu.SemaphoreType.DMA((5,)),
+            pltpu.SemaphoreType.DMA((len(distances[1]),)),
         ],
         compiler_params=pltpu.CompilerParams(vmem_limit_bytes=40 * 1024 * 1024),
         cost_estimate=SMALL,

time: 134 us -> 134 us (level)
  no operation moved by 1% of the time
where the time goes in v5:
time: 134 us; the launch traced here: 133 us
  starting transfers between devices  52.3 us (39%)
  waiting for transfers between devices  37.1 us (28%)
  Pallas kernels  31 us (23%)
  other arithmetic  6.14 us (5%)
  local copies, waits for them, and re-layouts  5.6 us (4%)
    ppermute x27, starting transfers between devices, swap(): return lax.ppermute(x, BOTH, pairs)  38.3 us
    ppermute x27, waiting for transfers between devices, swap(): return lax.ppermute(x, BOTH, pairs)  30.2 us
    pallas_call x2, Pallas kernels, data_grad(): pl.pallas_call(functools.partial(data_kernel, plan, n_bx, n_by, len(sourc...  14.1 us
    pallas_call x2, Pallas kernels, weight_sums(): pl.pallas_call(functools.partial(weight_kernel, plan, field), out_shape=j...  10.8 us
    ppermute x4, starting transfers between devices, rims_y(): return (lax.ppermute(last_y, 'gy', up), lax.ppermute(first_y, 'gy', down))  8.47 us
    ppermute x4, waiting for transfers between devices, rims_y(): return (lax.ppermute(last_y, 'gy', up), lax.ppermute(first_y, 'gy', down))  6.91 us
    ppermute x4, starting transfers between devices, rims_x(): return (lax.ppermute(last_x, 'gx', up), lax.ppermute(first_x, 'gx', down))  5.54 us
    pallas_call x1, Pallas kernels, first_steps(): pl.pallas_call(functools.partial(first_kernel, plan, n_bx, n_by), out_sha...  3.22 us
  transfers between devices with their start and end apart: 35, of which 15 were waited for; matrix products, arithmetic and copies ran while one was open for 8% of the time, Pallas kernels for 19%

profile of v5, /device:TPU:0, one launch (start us, length us, event | category | flops | bytes accessed | tf_op | source)
XLA Modules:
  0.0 133.3 jit_solution(16297309995925630302)
XLA Ops:
  0.6 3.2 %shard_map.85 = (bf16[32,1792]{1,0:T(8,128)(2,1)}, bf16[32,1792]{1,0:T(8,128)(2,1)}, bf16[3,16,8,256]{3,2,1,0:T(8,128)(2,1)}, bf16[3,16,8,256]{3,2,1,0:T(8,128)(...) custom-call(s32[2,1,2]{2,1,0:T(1,128)} %bitcast.52, bf16[32,1728]{1,0:T(8,128)(2,1)} %bitcast.63, ...), custom_call_target="tpu_custom_call" | custom-call | flops 1 | bytes 1 | tf_op jit(solution)/shard_map/pallas_call | solution.py:472
  3.9 4.1 %collective-permute-start.2 = (bf16[1,32,1792]{2,1,0:T(8,128)(2,1)}, bf16[1,32,1792]{2,1,0:T(8,128)(2,1)S(1)}, u32[]{:S(2)}, u32[]{:S(2)}) collective-permute-start(bf16[1,32,1792]{2,1,0:T(8,128)(2,1)} %bitcast.56), channel_id=1, source_target_pairs={{0,4},{1,5},{2,6},{3,7},{4,0},{5,1},{6,2},{7,3},{8,12},{9,13},{10,... | collective-permute-start | bytes 344072 | tf_op jit(solution)/shard_map/ppermute | solution.py:51
  8.0 1.5 %collective-permute-start = (bf16[3,16,8,256]{3,2,1,0:T(8,128)(2,1)}, bf16[3,16,8,256]{3,2,1,0:T(8,128)(2,1)S(1)}, u32[]{:S(2)}, u32[]{:S(2)}) collective-permute-start(bf16[3,16,8,256]{3,2,1,0:T(8,128)(2,1)} %get-tuple-element.51), channel_id=1, source_target_pairs={{0,8},{8,16},{16,24},{1,9},{9,17},{17,25},{2,10},{10,18},{18,26},{... | collective-permute-start | bytes 589832 | tf_op jit(solution)/shard_map/ppermute | solution.py:612
  9.4 1.3 collective-permute-start.1
  10.7 3.0 %collective-permute-done.2 = bf16[1,32,1792]{2,1,0:T(8,128)(2,1)S(1)} collective-permute-done((bf16[1,32,1792]{2,1,0:T(8,128)(2,1)}, bf16[1,32,1792]{2,1,0:T(8,128)(2,1)S(1)}, u32[]{:S(2)}, u32[]{:S(2)}) %collective-permute-start.2) | collective-permute-done | bytes 114720 | tf_op jit(solution)/shard_map/ppermute | solution.py:51
  13.8 0.9 pad_maximum_fusion.5
  14.7 0.9 collective-permute-start.8
  15.7 1.2 pad_maximum_fusion.6
  16.9 1.6 %collective-permute-start.5 = (bf16[1,32,1792]{2,1,0:T(8,128)(2,1)}, bf16[1,32,1792]{2,1,0:T(8,128)(2,1)S(1)}, u32[]{:S(2)}, u32[]{:S(2)}) collective-permute-start(bf16[1,32,1792]{2,1,0:T(8,128)(2,1)} %bitcast.59), channel_id=1, source_target_pairs={{0,1},{1,0},{2,3},{3,2},{4,5},{5,4},{6,7},{7,6},{8,9},{9,8},{10,11... | collective-permute-start | bytes 344072 | tf_op jit(solution)/shard_map/ppermute | solution.py:51
  18.5 1.0 constant_dynamic-update-slice_fusion.14
  19.4 3.0 %collective-permute-start.6 = (bf16[1,32,1792]{2,1,0:T(8,128)(2,1)S(1)}, bf16[1,32,1792]{2,1,0:T(8,128)(2,1)S(1)}, u32[]{:S(2)}, u32[]{:S(2)}) collective-permute-start(bf16[1,32,1792]{2,1,0:T(8,128)(2,1)S(1)} %bitcast.61), channel_id=1, source_target_pairs={{0,16},{1,17},{2,18},{3,19},{4,20},{5,21},{6,22},{7,23},{8,24},{9,... | collective-permute-start | bytes 344072 | tf_op jit(solution)/shard_map/ppermute | solution.py:51
  22.5 3.4 %collective-permute-start.3 = (bf16[3,18,8,256]{3,2,1,0:T(8,128)(2,1)S(1)}, bf16[3,18,8,256]{3,2,1,0:T(8,128)(2,1)S(1)}, u32[]{:S(2)}, u32[]{:S(2)}) collective-permute-start(bf16[3,18,8,256]{3,2,1,0:T(8,128)(2,1)S(1)} %get-tuple-element.56), channel_id=1, source_target_pairs={{0,1},{1,2},{2,3},{3,4},{4,5},{5,6},{6,7},{8,9},{9,10},{10,11},{11... | collective-permute-start | bytes 663560 | tf_op jit(solution)/shard_map/ppermute | solution.py:624
  25.9 1.3 collective-permute-start.4
  27.2 0.7 collective-permute-done.6
  27.9 0.8 collective-permute-done.7
  28.8 2.3 %collective-permute-done.3.rest_5_ = bf16[3,18,8,256]{3,2,1,0:T(8,128)(2,1)S(1)} collective-permute-done((bf16[3,18,8,256]{3,2,1,0:T(8,128)(2,1)S(1)}, bf16[3,18,8,256]{3,2,1,0:T(8,128)(2,1)S(1)}, u32[]{:S(2)}, u32[]{:S(2)}) %collective-permute-start.3) | collective-permute-done | bytes 221216 | tf_op jit(solution)/shard_map/ppermute | solution.py:624
  31.1 4.6 %collective-permute-done.4.rest_6_ = bf16[3,18,8,256]{3,2,1,0:T(8,128)(2,1)S(1)} collective-permute-done((bf16[3,18,8,256]{3,2,1,0:T(8,128)(2,1)S(1)}, bf16[3,18,8,256]{3,2,1,0:T(8,128)(2,1)S(1)}, u32[]{:S(2)}, u32[]{:S(2)}) %collective-permute-start.4) | collective-permute-done | bytes 221216 | tf_op jit(solution)/shard_map/ppermute | solution.py:624
  35.8 2.8 %shard_map.86.own_ref.rest_0_ = bf16[3,10,10,16,256]{4,3,2,1,0:T(8,128)(2,1)S(1)} custom-call(s32[2,1,2]{2,1,0:T(1,128)S(1)} %bitcast.53, bf16[16,16,8,256]{3,2,1,0:T(8,128)(2,1)S(1)} %copy-done, bf16[16,16,8,256]{3,2,1,0:T(8,128)(2,1)S(1)} %copy-done.1, bf16[16,16,8,256]{3,2,1,0:T(8,128)(2,1)S(1)} %copy-done.2, ...), custom_call_target="tpu_custom_call" | custom-call | flops 1 | bytes 1 | tf_op jit(solution)/shard_map/pallas_call | solution.py:194
  38.6 0.8 collective-permute-start.10
  39.4 3.8 %collective-permute-start.13 = (bf16[4,32,1792]{2,1,0:T(8,128)(2,1)S(1)}, bf16[4,32,1792]{2,1,0:T(8,128)(2,1)S(1)}, u32[]{:S(2)}, u32[]{:S(2)}) collective-permute-start(bf16[4,32,1792]{2,1,0:T(8,128)(2,1)S(1)} %get-tuple-element.121), channel_id=1, source_target_pairs={{0,4},{1,5},{2,6},{3,7},{4,0},{5,1},{6,2},{7,3},{8,12},{9,13},{10,... | collective-permute-start | bytes 1376264 | tf_op jit(solution)/shard_map/ppermute | solution.py:51
  43.2 0.4 collective-permute-start.11
  43.7 3.0 %collective-permute-start.12 = (bf16[4,32,1792]{2,1,0:T(8,128)(2,1)S(1)}, bf16[4,32,1792]{2,1,0:T(8,128)(2,1)S(1)}, u32[]{:S(2)}, u32[]{:S(2)}) collective-permute-start(bf16[4,32,1792]{2,1,0:T(8,128)(2,1)S(1)} %pad_maximum_fusion.2), channel_id=1, source_target_pairs={{0,17},{1,16},{2,19},{3,18},{4,21},{5,20},{6,23},{7,22},{8,25},{9,... | collective-permute-start | bytes 1376264 | tf_op jit(solution)/shard_map/ppermute | solution.py:51
  46.7 5.5 %shard_map.87 = bf16[4,4,14,32,128]{4,3,2,1,0:T(8,128)(2,1)S(1)} custom-call(bf16[3,10,10,16,256]{4,3,2,1,0:T(8,128)(2,1)S(1)} %shard_map.86.own_ref.rest_0_, bf16[3,10,10,16,256]{4,3,2,1,0:T(8,128)(2,1)S(1)} %collective-permute-done.10.other_ref), custom_call_target="tpu_custom_call" | custom-call | flops 1 | bytes 1 | tf_op jit(solution)/shard_map/pallas_call | solution.py:282
  52.2 12.0 %collective-permute-done.13 = bf16[4,32,1792]{2,1,0:T(8,128)(2,1)S(1)} collective-permute-done((bf16[4,32,1792]{2,1,0:T(8,128)(2,1)S(1)}, bf16[4,32,1792]{2,1,0:T(8,128)(2,1)S(1)}, u32[]{:S(2)}, u32[]{:S(2)}) %collective-permute-start.13) | collective-permute-done | bytes 458784 | tf_op jit(solution)/shard_map/ppermute | solution.py:51
  64.2 1.5 %collective-permute-done.11 = bf16[4,32,1792]{2,1,0:T(8,128)(2,1)S(1)} collective-permute-done((bf16[4,32,1792]{2,1,0:T(8,128)(2,1)S(1)}, bf16[4,32,1792]{2,1,0:T(8,128)(2,1)S(1)}, u32[]{:S(2)}, u32[]{:S(2)}) %collective-permute-start.11) | collective-permute-done | bytes 458784 | tf_op jit(solution)/shard_map/ppermute | solution.py:51
  65.7 0.2 pad_maximum_fusion.rest_1_
  66.2 1.8 %collective-permute-start.15 = (bf16[2,2,14,32,128]{4,3,2,1,0:T(8,128)(2,1)S(1)}, bf16[2,2,14,32,128]{4,3,2,1,0:T(8,128)(2,1)S(1)}, u32[]{:S(2)}, u32[]{:S(2)}) collective-permute-start(bf16[2,2,14,32,128]{4,3,2,1,0:T(8,128)(2,1)S(1)} %pad_maximum_fusion.3), channel_id=1, source_target_pairs={{0,1},{1,0},{2,3},{3,2},{4,5},{5,4},{6,7},{7,6},{8,9},{9,8},{10,11... | collective-permute-start | bytes 1376264 | tf_op jit(solution)/shard_map/ppermute | solution.py:51
  68.0 0.4 collective-permute-start.16
  68.4 0.5 collective-permute-start.26
  68.9 0.9 collective-permute-done.14.rest_2_
  69.8 6.0 %shard_map.88 = (bf16[16,16,8,256]{3,2,1,0:T(8,128)(2,1)S(1)}, bf16[8,8,16,256]{3,2,1,0:T(8,128)(2,1)S(1)}) custom-call(s32[2,1,2]{2,1,0:T(1,128)S(1)} %bitcast.54, bf16[3,10,10,16,256]{4,3,2,1,0:T(8,128)(2,1)S(1)} %shard_map.86.own_ref.rest_0_, bf16[16,32,1792]{2,1,0:T(8,128)(2,1)S(1)} %pad_maximum_fusion.rest_1_, ...), custom_call_target="tpu_custom_call" | custom-call | flops 1 | bytes 1 | tf_op jit(solution)/shard_map/pallas_call | solution.py:400
  75.8 3.3 %collective-permute-done.15 = bf16[2,2,14,32,128]{4,3,2,1,0:T(8,128)(2,1)S(1)} collective-permute-done((bf16[2,2,14,32,128]{4,3,2,1,0:T(8,128)(2,1)S(1)}, bf16[2,2,14,32,128]{4,3,2,1,0:T(8,128)(2,1)S(1)}, u32[]{:S(2)}, u32[]{:S(2)}) %collective-permute-start.15) | collective-permute-done | bytes 458784 | tf_op jit(solution)/shard_map/ppermute | solution.py:51
  79.2 1.5 %collective-permute-done.16 = bf16[2,2,14,32,128]{4,3,2,1,0:T(8,128)(2,1)S(1)} collective-permute-done((bf16[2,2,14,32,128]{4,3,2,1,0:T(8,128)(2,1)S(1)}, bf16[2,2,14,32,128]{4,3,2,1,0:T(8,128)(2,1)S(1)}, u32[]{:S(2)}, u32[]{:S(2)}) %collective-permute-start.16) | collective-permute-done | bytes 458784 | tf_op jit(solution)/shard_map/ppermute | solution.py:51
  80.9 0.1 convert_add_fusion.3
  81.1 0.4 collective-permute-start.19
  81.5 1.4 %collective-permute-start.18 = (bf16[1,2,14,32,128]{4,3,2,1,0:T(8,128)(2,1)S(1)}, bf16[1,2,14,32,128]{4,3,2,1,0:T(8,128)(2,1)S(1)}, u32[]{:S(2)}, u32[]{:S(2)}) collective-permute-start(bf16[1,2,14,32,128]{4,3,2,1,0:T(8,128)(2,1)S(1)} %slice.256), channel_id=1, source_target_pairs={{0,16},{1,17},{2,18},{3,19},{4,20},{5,21},{6,22},{7,23},{8,24},{9,... | collective-permute-start | bytes 688136 | tf_op jit(solution)/shard_map/ppermute | solution.py:51
  82.9 5.3 %shard_map.89 = bf16[4,4,14,32,128]{4,3,2,1,0:T(8,128)(2,1)S(1)} custom-call(bf16[3,10,10,16,256]{4,3,2,1,0:T(8,128)(2,1)S(1)} %shard_map.86.own_ref.rest_0_, bf16[3,10,10,16,256]{4,3,2,1,0:T(8,128)(2,1)S(1)} %collective-permute-done.10.other_ref, bf16[8,8,16,256]{3,2,1,0:T(8,128)(2,1)S(1)} %get-tuple-element.78.rest_0_, ...), custom_call_target="tpu_custom_call" | custom-call | flops 1 | bytes 1 | tf_op jit(solution)/shard_map/pallas_call | solution.py:282
  88.2 0.9 collective-permute-done.19
  89.4 1.7 %collective-permute-start.22 = (bf16[2,2,14,32,128]{4,3,2,1,0:T(8,128)(2,1)S(1)}, bf16[2,2,14,32,128]{4,3,2,1,0:T(8,128)(2,1)S(1)}, u32[]{:S(2)}, u32[]{:S(2)}) collective-permute-start(bf16[2,2,14,32,128]{4,3,2,1,0:T(8,128)(2,1)S(1)} %pad_maximum_fusion.4), channel_id=1, source_target_pairs={{0,1},{1,0},{2,3},{3,2},{4,5},{5,4},{6,7},{7,6},{8,9},{9,8},{10,11... | collective-permute-start | bytes 1376264 | tf_op jit(solution)/shard_map/ppermute | solution.py:51
  91.1 0.4 collective-permute-start.23
  91.8 0.6 collective-permute-start.33
  92.4 1.3 collective-permute-start.20
  93.7 1.5 %collective-permute-start.21 = (bf16[1,16,8,256]{3,2,1,0:T(8,128)(2,1)S(1)}, bf16[1,16,8,256]{3,2,1,0:T(8,128)(2,1)S(1)}, u32[]{:S(2)}, u32[]{:S(2)}) collective-permute-start(bf16[1,16,8,256]{3,2,1,0:T(8,128)(2,1)S(1)} %get-tuple-element.83), channel_id=1, source_target_pairs={{8,0},{16,8},{24,16},{9,1},{17,9},{25,17},{10,2},{18,10},{26,18},{... | collective-permute-start | bytes 196616 | tf_op jit(solution)/shard_map/ppermute | solution.py:612
  95.3 4.9 %collective-permute-start.27 = (bf16[16,32,1792]{2,1,0:T(8,128)(2,1)S(1)}, bf16[16,32,1792]{2,1,0:T(8,128)(2,1)}, u32[]{:S(2)}, u32[]{:S(2)}) collective-permute-start(bf16[16,32,1792]{2,1,0:T(8,128)(2,1)S(1)} %constant_dynamic-update-slice_fusion.9.rest_5_), channel_id=1, source_target_pairs={{0,8},{1,9},{2,10},{3,11},{4,12},{5,13},{6,14},{7,15},{8,0},{9,1},... | collective-permute-start | bytes 5505032 | tf_op jit(solution)/shard_map/ppermute | solution.py:51
  100.1 0.6 pad_maximum_fusion.9
  100.9 0.6 collective-permute-done.22
  101.5 1.1 collective-permute-done.23
  102.8 0.1 convert_add_fusion.1
  103.0 0.9 slice.253
  104.0 0.7 slice.254
  104.7 0.7 slice.257
  105.4 0.3 collective-permute-start.34
  105.6 0.7 collective-permute-start.29
  106.4 2.3 %collective-permute-start.28 = (bf16[1,2,14,32,128]{4,3,2,1,0:T(8,128)(2,1)}, bf16[1,2,14,32,128]{4,3,2,1,0:T(8,128)(2,1)S(1)}, u32[]{:S(2)}, u32[]{:S(2)}) collective-permute-start(bf16[1,2,14,32,128]{4,3,2,1,0:T(8,128)(2,1)} %slice.254), channel_id=1, source_target_pairs={{0,16},{1,17},{2,18},{3,19},{4,20},{5,21},{6,22},{7,23},{8,24},{9,... | collective-permute-start | bytes 688136 | tf_op jit(solution)/shard_map/ppermute | solution.py:51
  108.6 2.5 %collective-permute-start.24 = (bf16[1,18,8,256]{3,2,1,0:T(8,128)(2,1)}, bf16[1,18,8,256]{3,2,1,0:T(8,128)(2,1)S(1)}, u32[]{:S(2)}, u32[]{:S(2)}) collective-permute-start(bf16[1,18,8,256]{3,2,1,0:T(8,128)(2,1)} %pad_maximum_fusion.9), channel_id=1, source_target_pairs={{0,1},{1,2},{2,3},{3,4},{4,5},{5,6},{6,7},{8,9},{9,10},{10,11},{11... | collective-permute-start | bytes 221192 | tf_op jit(solution)/shard_map/ppermute | solution.py:624
  111.1 3.6 %collective-permute-done.34 = bf16[1,14,32,128]{3,2,1,0:T(8,128)(2,1)} collective-permute-done((bf16[1,14,32,128]{3,2,1,0:T(8,128)(2,1)}, bf16[1,14,32,128]{3,2,1,0:T(8,128)(2,1)}, u32[]{:S(2)}, u32[]{:S(2)}) %collective-permute-start.34) | collective-permute-done | bytes 114720 | tf_op jit(solution)/shard_map/ppermute | solution.py:51
  114.8 1.3 collective-permute-start.25
  116.1 0.9 copy_bitcast_fusion
  117.0 1.1 fusion.2
  118.1 1.6 %collective-permute-start.31 = (bf16[14,32,128]{2,1,0:T(8,128)(2,1)S(1)}, bf16[14,32,128]{2,1,0:T(8,128)(2,1)S(1)}, u32[]{:S(2)}, u32[]{:S(2)}) collective-permute-start(bf16[14,32,128]{2,1,0:T(8,128)(2,1)S(1)} %get-tuple-element.114), channel_id=1, source_target_pairs={{0,4},{1,5},{2,6},{3,7},{4,0},{5,1},{6,2},{7,3},{8,12},{9,13},{10,... | collective-permute-start | bytes 344072 | tf_op jit(solution)/shard_map/ppermute | solution.py:51
  119.7 3.5 %collective-permute-start.32 = (bf16[14,32,128]{2,1,0:T(8,128)(2,1)S(1)}, bf16[14,32,128]{2,1,0:T(8,128)(2,1)S(1)}, u32[]{:S(2)}, u32[]{:S(2)}) collective-permute-start(bf16[14,32,128]{2,1,0:T(8,128)(2,1)S(1)} %get-tuple-element.113), channel_id=1, source_target_pairs={{0,6},{1,7},{2,4},{3,5},{4,2},{5,3},{6,0},{7,1},{8,14},{9,15},{10,... | collective-permute-start | bytes 344072 | tf_op jit(solution)/shard_map/ppermute | solution.py:51
  123.4 0.8 dynamic-slice_bitcast_fusion
  124.2 8.1 %shard_map.90 = bf16[16,16,8,256]{3,2,1,0:T(8,128)(2,1)} custom-call(s32[2,1,2]{2,1,0:T(1,128)S(1)} %bitcast.55, bf16[16,16,8,256]{3,2,1,0:T(8,128)(2,1)S(1)} %get-tuple-element.74.rest_0_, bf16[1,16,8,256]{3,2,1,0:T(8,128)(2,1)S(1)} %collective-permute-done.20.rest_1_, bf16[1,16,8,256]{3,2,1,0:T(8,128)(2,1)S(1)} %collective-permute-done.21.rest_2_, ...), custom_call_target="tpu_custom_call" | custom-call | flops 1 | bytes 1 | tf_op jit(solution)/shard_map/pallas_call | solution.py:400
  132.5 0.8 dynamic-slice_bitcast_fusion.1
  (77 shorter events, 1.9 us)
Async XLA Ops:
  3.9 15.6 %copy-start.8 = (bf16[32,1792]{1,0:T(8,128)(2,1)S(1)}, bf16[32,1792]{1,0:T(8,128)(2,1)}, u32[]{:S(2)}) copy-start(bf16[32,1792]{1,0:T(8,128)(2,1)} %get-tuple-element.58) | copy-start | bytes 344068
  3.9 24.9 %copy-start.7 = (bf16[32,1792]{1,0:T(8,128)(2,1)S(1)}, bf16[32,1792]{1,0:T(8,128)(2,1)}, u32[]{:S(2)}) copy-start(bf16[32,1792]{1,0:T(8,128)(2,1)} %get-tuple-element.55) | copy-start | bytes 344068
  3.9 9.9 %collective-permute-start.2 = (bf16[1,32,1792]{2,1,0:T(8,128)(2,1)}, bf16[1,32,1792]{2,1,0:T(8,128)(2,1)S(1)}, u32[]{:S(2)}, u32[]{:S(2)}) collective-permute-start(bf16[1,32,1792]{2,1,0:T(8,128)(2,1)} %bitcast.56), channel_id=1, source_target_pairs={{0,4},{1,5},{2,6},{3,7},{4,0},{5,1},{6,2},{7,3},{8,12},{9,13},{10,... | collective-permute-start | bytes 344072 | tf_op jit(solution)/shard_map/ppermute | solution.py:51
  8.0 7.6 %collective-permute-start = (bf16[3,16,8,256]{3,2,1,0:T(8,128)(2,1)}, bf16[3,16,8,256]{3,2,1,0:T(8,128)(2,1)S(1)}, u32[]{:S(2)}, u32[]{:S(2)}) collective-permute-start(bf16[3,16,8,256]{3,2,1,0:T(8,128)(2,1)} %get-tuple-element.51), channel_id=1, source_target_pairs={{0,8},{8,16},{16,24},{1,9},{9,17},{17,25},{2,10},{10,18},{18,26},{... | collective-permute-start | bytes 589832 | tf_op jit(solution)/shard_map/ppermute | solution.py:612
  9.4 6.2 %collective-permute-start.1 = (bf16[3,16,8,256]{3,2,1,0:T(8,128)(2,1)}, bf16[3,16,8,256]{3,2,1,0:T(8,128)(2,1)S(1)}, u32[]{:S(2)}, u32[]{:S(2)}) collective-permute-start(bf16[3,16,8,256]{3,2,1,0:T(8,128)(2,1)} %get-tuple-element.52), channel_id=1, source_target_pairs={{8,0},{16,8},{24,16},{9,1},{17,9},{25,17},{10,2},{18,10},{26,18},{... | collective-permute-start | bytes 589832 | tf_op jit(solution)/shard_map/ppermute | solution.py:612
  14.7 14.0 %collective-permute-start.8 = (bf16[2,32,1792]{2,1,0:T(8,128)(2,1)S(1)}, bf16[2,32,1792]{2,1,0:T(8,128)(2,1)S(1)}, u32[]{:S(2)}, u32[]{:S(2)}) collective-permute-start(bf16[2,32,1792]{2,1,0:T(8,128)(2,1)S(1)} %pad_maximum_fusion.5), channel_id=1, source_target_pairs={{0,2},{1,3},{2,0},{3,1},{4,6},{5,7},{6,4},{7,5},{8,10},{9,11},{10,... | collective-permute-start | bytes 688136 | tf_op jit(solution)/shard_map/ppermute | solution.py:51
  15.6 20.1 %copy-start = (bf16[16,16,8,256]{3,2,1,0:T(8,128)(2,1)S(1)}, bf16[16,16,8,256]{3,2,1,0:T(8,128)(2,1)}, u32[]{:S(2)}) copy-start(bf16[16,16,8,256]{3,2,1,0:T(8,128)(2,1)} %rest_3_.1) | copy-start | bytes 3145732
  15.6 20.1 %copy-start.1 = (bf16[16,16,8,256]{3,2,1,0:T(8,128)(2,1)S(1)}, bf16[16,16,8,256]{3,2,1,0:T(8,128)(2,1)}, u32[]{:S(2)}) copy-start(bf16[16,16,8,256]{3,2,1,0:T(8,128)(2,1)} %rest_1_.3) | copy-start | bytes 3145732
  15.7 20.1 %copy-start.2 = (bf16[16,16,8,256]{3,2,1,0:T(8,128)(2,1)S(1)}, bf16[16,16,8,256]{3,2,1,0:T(8,128)(2,1)}, u32[]{:S(2)}) copy-start(bf16[16,16,8,256]{3,2,1,0:T(8,128)(2,1)} %rest_2_.3) | copy-start | bytes 3145732
  15.7 20.1 %copy-start.3 = (s32[2,2,1]{1,2,0:T(1,128)S(1)}, s32[2,2,1]{1,2,0:T(1,128)}, u32[]{:S(2)}) copy-start(s32[2,2,1]{1,2,0:T(1,128)} %param.11) | copy-start | bytes 52
  16.9 8.9 %collective-permute-start.5 = (bf16[1,32,1792]{2,1,0:T(8,128)(2,1)}, bf16[1,32,1792]{2,1,0:T(8,128)(2,1)S(1)}, u32[]{:S(2)}, u32[]{:S(2)}) collective-permute-start(bf16[1,32,1792]{2,1,0:T(8,128)(2,1)} %bitcast.59), channel_id=1, source_target_pairs={{0,1},{1,0},{2,3},{3,2},{4,5},{5,4},{6,7},{7,6},{8,9},{9,8},{10,11... | collective-permute-start | bytes 344072 | tf_op jit(solution)/shard_map/ppermute | solution.py:51
  19.4 8.5 %collective-permute-start.6 = (bf16[1,32,1792]{2,1,0:T(8,128)(2,1)S(1)}, bf16[1,32,1792]{2,1,0:T(8,128)(2,1)S(1)}, u32[]{:S(2)}, u32[]{:S(2)}) collective-permute-start(bf16[1,32,1792]{2,1,0:T(8,128)(2,1)S(1)} %bitcast.61), channel_id=1, source_target_pairs={{0,16},{1,17},{2,18},{3,19},{4,20},{5,21},{6,22},{7,23},{8,24},{9,... | collective-permute-start | bytes 344072 | tf_op jit(solution)/shard_map/ppermute | solution.py:51
  22.4 6.3 %collective-permute-start.7 = (bf16[1,32,1792]{2,1,0:T(8,128)(2,1)S(1)}, bf16[1,32,1792]{2,1,0:T(8,128)(2,1)S(1)}, u32[]{:S(2)}, u32[]{:S(2)}) collective-permute-start(bf16[1,32,1792]{2,1,0:T(8,128)(2,1)S(1)} %bitcast.62), channel_id=1, source_target_pairs={{0,17},{1,16},{2,19},{3,18},{4,21},{5,20},{6,23},{7,22},{8,25},{9,... | collective-permute-start | bytes 344072 | tf_op jit(solution)/shard_map/ppermute | solution.py:51
  22.5 8.6 %collective-permute-start.3 = (bf16[3,18,8,256]{3,2,1,0:T(8,128)(2,1)S(1)}, bf16[3,18,8,256]{3,2,1,0:T(8,128)(2,1)S(1)}, u32[]{:S(2)}, u32[]{:S(2)}) collective-permute-start(bf16[3,18,8,256]{3,2,1,0:T(8,128)(2,1)S(1)} %get-tuple-element.56), channel_id=1, source_target_pairs={{0,1},{1,2},{2,3},{3,4},{4,5},{5,6},{6,7},{8,9},{9,10},{10,11},{11... | collective-permute-start | bytes 663560 | tf_op jit(solution)/shard_map/ppermute | solution.py:624
  25.9 9.9 %collective-permute-start.4 = (bf16[3,18,8,256]{3,2,1,0:T(8,128)(2,1)S(1)}, bf16[3,18,8,256]{3,2,1,0:T(8,128)(2,1)S(1)}, u32[]{:S(2)}, u32[]{:S(2)}) collective-permute-start(bf16[3,18,8,256]{3,2,1,0:T(8,128)(2,1)S(1)} %get-tuple-element.57), channel_id=1, source_target_pairs={{1,0},{2,1},{3,2},{4,3},{5,4},{6,5},{7,6},{9,8},{10,9},{11,10},{12... | collective-permute-start | bytes 663560 | tf_op jit(solution)/shard_map/ppermute | solution.py:624
  38.6 8.1 %collective-permute-start.10 = (bf16[3,10,10,16,256]{4,3,2,1,0:T(8,128)(2,1)S(1)}, bf16[3,10,10,16,256]{4,3,2,1,0:T(8,128)(2,1)S(1)}, u32[]{:S(2)}, u32[]{:S(2)}) collective-permute-start(bf16[3,10,10,16,256]{4,3,2,1,0:T(8,128)(2,1)S(1)} %shard_map.86.own_ref.rest_0_), channel_id=1, source_target_pairs={{0,8},{1,9},{2,10},{3,11},{4,12},{5,13},{6,14},{7,15},{8,0},{9,1},... | collective-permute-start | bytes 7372808 | tf_op jit(solution)/shard_map/ppermute | solution.py:51
  39.4 24.7 %collective-permute-start.13 = (bf16[4,32,1792]{2,1,0:T(8,128)(2,1)S(1)}, bf16[4,32,1792]{2,1,0:T(8,128)(2,1)S(1)}, u32[]{:S(2)}, u32[]{:S(2)}) collective-permute-start(bf16[4,32,1792]{2,1,0:T(8,128)(2,1)S(1)} %get-tuple-element.121), channel_id=1, source_target_pairs={{0,4},{1,5},{2,6},{3,7},{4,0},{5,1},{6,2},{7,3},{8,12},{9,13},{10,... | collective-permute-start | bytes 1376264 | tf_op jit(solution)/shard_map/ppermute | solution.py:51
  43.2 20.9 %collective-permute-start.9 = (bf16[4,32,1792]{2,1,0:T(8,128)(2,1)S(1)}, bf16[4,32,1792]{2,1,0:T(8,128)(2,1)S(1)}, u32[]{:S(2)}, u32[]{:S(2)}) collective-permute-start(bf16[4,32,1792]{2,1,0:T(8,128)(2,1)S(1)} %pad_maximum_fusion.2), channel_id=1, source_target_pairs={{0,1},{1,0},{2,3},{3,2},{4,5},{5,4},{6,7},{7,6},{8,9},{9,8},{10,11... | collective-permute-start | bytes 1376264 | tf_op jit(solution)/shard_map/ppermute | solution.py:51
  43.2 22.4 %collective-permute-start.11 = (bf16[4,32,1792]{2,1,0:T(8,128)(2,1)S(1)}, bf16[4,32,1792]{2,1,0:T(8,128)(2,1)S(1)}, u32[]{:S(2)}, u32[]{:S(2)}) collective-permute-start(bf16[4,32,1792]{2,1,0:T(8,128)(2,1)S(1)} %pad_maximum_fusion.2), channel_id=1, source_target_pairs={{0,16},{1,17},{2,18},{3,19},{4,20},{5,21},{6,22},{7,23},{8,24},{9,... | collective-permute-start | bytes 1376264 | tf_op jit(solution)/shard_map/ppermute | solution.py:51
  43.7 22.0 %collective-permute-start.12 = (bf16[4,32,1792]{2,1,0:T(8,128)(2,1)S(1)}, bf16[4,32,1792]{2,1,0:T(8,128)(2,1)S(1)}, u32[]{:S(2)}, u32[]{:S(2)}) collective-permute-start(bf16[4,32,1792]{2,1,0:T(8,128)(2,1)S(1)} %pad_maximum_fusion.2), channel_id=1, source_target_pairs={{0,17},{1,16},{2,19},{3,18},{4,21},{5,20},{6,23},{7,22},{8,25},{9,... | collective-permute-start | bytes 1376264 | tf_op jit(solution)/shard_map/ppermute | solution.py:51
  66.0 3.9 %collective-permute-start.14 = (bf16[16,32,1792]{2,1,0:T(8,128)(2,1)S(1)}, bf16[16,32,1792]{2,1,0:T(8,128)(2,1)S(1)}, u32[]{:S(2)}, u32[]{:S(2)}) collective-permute-start(bf16[16,32,1792]{2,1,0:T(8,128)(2,1)S(1)} %pad_maximum_fusion.rest_1_), channel_id=1, source_target_pairs={{0,8},{1,9},{2,10},{3,11},{4,12},{5,13},{6,14},{7,15},{8,0},{9,1},... | collective-permute-start | bytes 5505032 | tf_op jit(solution)/shard_map/ppermute | solution.py:51
  66.2 13.0 %collective-permute-start.15 = (bf16[2,2,14,32,128]{4,3,2,1,0:T(8,128)(2,1)S(1)}, bf16[2,2,14,32,128]{4,3,2,1,0:T(8,128)(2,1)S(1)}, u32[]{:S(2)}, u32[]{:S(2)}) collective-permute-start(bf16[2,2,14,32,128]{4,3,2,1,0:T(8,128)(2,1)S(1)} %pad_maximum_fusion.3), channel_id=1, source_target_pairs={{0,1},{1,0},{2,3},{3,2},{4,5},{5,4},{6,7},{7,6},{8,9},{9,8},{10,11... | collective-permute-start | bytes 1376264 | tf_op jit(solution)/shard_map/ppermute | solution.py:51
  68.0 12.6 %collective-permute-start.16 = (bf16[2,2,14,32,128]{4,3,2,1,0:T(8,128)(2,1)S(1)}, bf16[2,2,14,32,128]{4,3,2,1,0:T(8,128)(2,1)S(1)}, u32[]{:S(2)}, u32[]{:S(2)}) collective-permute-start(bf16[2,2,14,32,128]{4,3,2,1,0:T(8,128)(2,1)S(1)} %concatenate.80), channel_id=1, source_target_pairs={{0,16},{1,17},{2,18},{3,19},{4,20},{5,21},{6,22},{7,23},{8,24},{9,... | collective-permute-start | bytes 1376264 | tf_op jit(solution)/shard_map/ppermute | solution.py:51
  68.4 25.3 %collective-permute-start.26 = (bf16[8,32,1792]{2,1,0:T(8,128)(2,1)S(1)}, bf16[8,32,1792]{2,1,0:T(8,128)(2,1)S(1)}, u32[]{:S(2)}, u32[]{:S(2)}) collective-permute-start(bf16[8,32,1792]{2,1,0:T(8,128)(2,1)S(1)} %get-tuple-element.90), channel_id=1, source_target_pairs={{0,2},{1,3},{2,0},{3,1},{4,6},{5,7},{6,4},{7,5},{8,10},{9,11},{10,... | collective-permute-start | bytes 2752520 | tf_op jit(solution)/shard_map/ppermute | solution.py:51
  80.8 2.1 %collective-permute-start.17 = (bf16[8,8,16,256]{3,2,1,0:T(8,128)(2,1)S(1)}, bf16[8,8,16,256]{3,2,1,0:T(8,128)(2,1)S(1)}, u32[]{:S(2)}, u32[]{:S(2)}) collective-permute-start(bf16[8,8,16,256]{3,2,1,0:T(8,128)(2,1)S(1)} %get-tuple-element.78.rest_0_), channel_id=1, source_target_pairs={{0,8},{1,9},{2,10},{3,11},{4,12},{5,13},{6,14},{7,15},{8,0},{9,1},... | collective-permute-start | bytes 1572872 | tf_op jit(solution)/shard_map/ppermute | solution.py:51
  81.1 8.1 %collective-permute-start.19 = (bf16[1,2,14,32,128]{4,3,2,1,0:T(8,128)(2,1)S(1)}, bf16[1,2,14,32,128]{4,3,2,1,0:T(8,128)(2,1)S(1)}, u32[]{:S(2)}, u32[]{:S(2)}) collective-permute-start(bf16[1,2,14,32,128]{4,3,2,1,0:T(8,128)(2,1)S(1)} %slice.255), channel_id=1, source_target_pairs={{0,1},{1,0},{2,3},{3,2},{4,5},{5,4},{6,7},{7,6},{8,9},{9,8},{10,11... | collective-permute-start | bytes 688136 | tf_op jit(solution)/shard_map/ppermute | solution.py:51
  81.5 7.7 %collective-permute-start.18 = (bf16[1,2,14,32,128]{4,3,2,1,0:T(8,128)(2,1)S(1)}, bf16[1,2,14,32,128]{4,3,2,1,0:T(8,128)(2,1)S(1)}, u32[]{:S(2)}, u32[]{:S(2)}) collective-permute-start(bf16[1,2,14,32,128]{4,3,2,1,0:T(8,128)(2,1)S(1)} %slice.256), channel_id=1, source_target_pairs={{0,16},{1,17},{2,18},{3,19},{4,20},{5,21},{6,22},{7,23},{8,24},{9,... | collective-permute-start | bytes 688136 | tf_op jit(solution)/shard_map/ppermute | solution.py:51
  89.4 12.1 %collective-permute-start.22 = (bf16[2,2,14,32,128]{4,3,2,1,0:T(8,128)(2,1)S(1)}, bf16[2,2,14,32,128]{4,3,2,1,0:T(8,128)(2,1)S(1)}, u32[]{:S(2)}, u32[]{:S(2)}) collective-permute-start(bf16[2,2,14,32,128]{4,3,2,1,0:T(8,128)(2,1)S(1)} %pad_maximum_fusion.4), channel_id=1, source_target_pairs={{0,1},{1,0},{2,3},{3,2},{4,5},{5,4},{6,7},{7,6},{8,9},{9,8},{10,11... | collective-permute-start | bytes 1376264 | tf_op jit(solution)/shard_map/ppermute | solution.py:51
  91.1 11.5 %collective-permute-start.23 = (bf16[2,2,14,32,128]{4,3,2,1,0:T(8,128)(2,1)S(1)}, bf16[2,2,14,32,128]{4,3,2,1,0:T(8,128)(2,1)S(1)}, u32[]{:S(2)}, u32[]{:S(2)}) collective-permute-start(bf16[2,2,14,32,128]{4,3,2,1,0:T(8,128)(2,1)S(1)} %concatenate.73), channel_id=1, source_target_pairs={{0,16},{1,17},{2,18},{3,19},{4,20},{5,21},{6,22},{7,23},{8,24},{9,... | collective-permute-start | bytes 1376264 | tf_op jit(solution)/shard_map/ppermute | solution.py:51
  91.8 9.0 %collective-permute-start.33 = (bf16[2,14,32,128]{3,2,1,0:T(8,128)(2,1)S(1)}, bf16[2,14,32,128]{3,2,1,0:T(8,128)(2,1)S(1)}, u32[]{:S(2)}, u32[]{:S(2)}) collective-permute-start(bf16[2,14,32,128]{3,2,1,0:T(8,128)(2,1)S(1)} %slice.188), channel_id=1, source_target_pairs={{0,2},{1,3},{2,0},{3,1},{4,6},{5,7},{6,4},{7,5},{8,10},{9,11},{10,... | collective-permute-start | bytes 688136 | tf_op jit(solution)/shard_map/ppermute | solution.py:51
  92.4 2.9 %collective-permute-start.20 = (bf16[1,16,8,256]{3,2,1,0:T(8,128)(2,1)S(1)}, bf16[1,16,8,256]{3,2,1,0:T(8,128)(2,1)S(1)}, u32[]{:S(2)}, u32[]{:S(2)}) collective-permute-start(bf16[1,16,8,256]{3,2,1,0:T(8,128)(2,1)S(1)} %get-tuple-element.82), channel_id=1, source_target_pairs={{0,8},{8,16},{16,24},{1,9},{9,17},{17,25},{2,10},{10,18},{18,26},{... | collective-permute-start | bytes 196616 | tf_op jit(solution)/shard_map/ppermute | solution.py:612
  93.7 6.5 %collective-permute-start.21 = (bf16[1,16,8,256]{3,2,1,0:T(8,128)(2,1)S(1)}, bf16[1,16,8,256]{3,2,1,0:T(8,128)(2,1)S(1)}, u32[]{:S(2)}, u32[]{:S(2)}) collective-permute-start(bf16[1,16,8,256]{3,2,1,0:T(8,128)(2,1)S(1)} %get-tuple-element.83), channel_id=1, source_target_pairs={{8,0},{16,8},{24,16},{9,1},{17,9},{25,17},{10,2},{18,10},{26,18},{... | collective-permute-start | bytes 196616 | tf_op jit(solution)/shard_map/ppermute | solution.py:612
  95.3 29.0 %collective-permute-start.27 = (bf16[16,32,1792]{2,1,0:T(8,128)(2,1)S(1)}, bf16[16,32,1792]{2,1,0:T(8,128)(2,1)}, u32[]{:S(2)}, u32[]{:S(2)}) collective-permute-start(bf16[16,32,1792]{2,1,0:T(8,128)(2,1)S(1)} %constant_dynamic-update-slice_fusion.9.rest_5_), channel_id=1, source_target_pairs={{0,8},{1,9},{2,10},{3,11},{4,12},{5,13},{6,14},{7,15},{8,0},{9,1},... | collective-permute-start | bytes 5505032 | tf_op jit(solution)/shard_map/ppermute | solution.py:51
  102.8 1.9 %copy-start.6 = (f32[2,2,14,32,128]{4,3,2,1,0:T(8,128)}, f32[2,2,14,32,128]{4,3,2,1,0:T(8,128)S(1)}, u32[]{:S(2)}) copy-start(f32[2,2,14,32,128]{4,3,2,1,0:T(8,128)S(1)} %convert_add_fusion) | copy-start | bytes 2752516
  102.9 1.0 copy-start.4
  105.4 9.4 %collective-permute-start.34 = (bf16[1,14,32,128]{3,2,1,0:T(8,128)(2,1)}, bf16[1,14,32,128]{3,2,1,0:T(8,128)(2,1)}, u32[]{:S(2)}, u32[]{:S(2)}) collective-permute-start(bf16[1,14,32,128]{3,2,1,0:T(8,128)(2,1)} %slice.257), channel_id=1, source_target_pairs={{0,4},{1,5},{2,6},{3,7},{4,0},{5,1},{6,2},{7,3},{8,12},{9,13},{10,... | collective-permute-start | bytes 344072 | tf_op jit(solution)/shard_map/ppermute | solution.py:51
  105.6 17.6 %copy-start.5 = (f32[2,2,14,32,128]{4,3,2,1,0:T(8,128)S(1)}, f32[2,2,14,32,128]{4,3,2,1,0:T(8,128)}, u32[]{:S(2)}) copy-start(f32[2,2,14,32,128]{4,3,2,1,0:T(8,128)} %copy-done.4) | copy-start | bytes 2752516
  105.6 11.3 %collective-permute-start.29 = (bf16[1,2,14,32,128]{4,3,2,1,0:T(8,128)(2,1)}, bf16[1,2,14,32,128]{4,3,2,1,0:T(8,128)(2,1)S(1)}, u32[]{:S(2)}, u32[]{:S(2)}) collective-permute-start(bf16[1,2,14,32,128]{4,3,2,1,0:T(8,128)(2,1)} %slice.253), channel_id=1, source_target_pairs={{0,1},{1,0},{2,3},{3,2},{4,5},{5,4},{6,7},{7,6},{8,9},{9,8},{10,11... | collective-permute-start | bytes 688136 | tf_op jit(solution)/shard_map/ppermute | solution.py:51
  106.4 10.6 %collective-permute-start.28 = (bf16[1,2,14,32,128]{4,3,2,1,0:T(8,128)(2,1)}, bf16[1,2,14,32,128]{4,3,2,1,0:T(8,128)(2,1)S(1)}, u32[]{:S(2)}, u32[]{:S(2)}) collective-permute-start(bf16[1,2,14,32,128]{4,3,2,1,0:T(8,128)(2,1)} %slice.254), channel_id=1, source_target_pairs={{0,16},{1,17},{2,18},{3,19},{4,20},{5,21},{6,22},{7,23},{8,24},{9,... | collective-permute-start | bytes 688136 | tf_op jit(solution)/shard_map/ppermute | solution.py:51
  108.6 14.7 %collective-permute-start.24 = (bf16[1,18,8,256]{3,2,1,0:T(8,128)(2,1)}, bf16[1,18,8,256]{3,2,1,0:T(8,128)(2,1)S(1)}, u32[]{:S(2)}, u32[]{:S(2)}) collective-permute-start(bf16[1,18,8,256]{3,2,1,0:T(8,128)(2,1)} %pad_maximum_fusion.9), channel_id=1, source_target_pairs={{0,1},{1,2},{2,3},{3,4},{4,5},{5,6},{6,7},{8,9},{9,10},{10,11},{11... | collective-permute-start | bytes 221192 | tf_op jit(solution)/shard_map/ppermute | solution.py:624
  114.8 9.5 %collective-permute-start.25 = (bf16[1,18,8,256]{3,2,1,0:T(8,128)(2,1)S(1)}, bf16[1,18,8,256]{3,2,1,0:T(8,128)(2,1)S(1)}, u32[]{:S(2)}, u32[]{:S(2)}) collective-permute-start(bf16[1,18,8,256]{3,2,1,0:T(8,128)(2,1)S(1)} %pad_maximum_fusion.8), channel_id=1, source_target_pairs={{1,0},{2,1},{3,2},{4,3},{5,4},{6,5},{7,6},{9,8},{10,9},{11,10},{12... | collective-permute-start | bytes 221192 | tf_op jit(solution)/shard_map/ppermute | solution.py:624
  118.1 14.2 %collective-permute-start.31 = (bf16[14,32,128]{2,1,0:T(8,128)(2,1)S(1)}, bf16[14,32,128]{2,1,0:T(8,128)(2,1)S(1)}, u32[]{:S(2)}, u32[]{:S(2)}) collective-permute-start(bf16[14,32,128]{2,1,0:T(8,128)(2,1)S(1)} %get-tuple-element.114), channel_id=1, source_target_pairs={{0,4},{1,5},{2,6},{3,7},{4,0},{5,1},{6,2},{7,3},{8,12},{9,13},{10,... | collective-permute-start | bytes 344072 | tf_op jit(solution)/shard_map/ppermute | solution.py:51
  119.7 12.6 %collective-permute-start.32 = (bf16[14,32,128]{2,1,0:T(8,128)(2,1)S(1)}, bf16[14,32,128]{2,1,0:T(8,128)(2,1)S(1)}, u32[]{:S(2)}, u32[]{:S(2)}) collective-permute-start(bf16[14,32,128]{2,1,0:T(8,128)(2,1)S(1)} %get-tuple-element.113), channel_id=1, source_target_pairs={{0,6},{1,7},{2,4},{3,5},{4,2},{5,3},{6,0},{7,1},{8,14},{9,15},{10,... | collective-permute-start | bytes 344072 | tf_op jit(solution)/shard_map/ppermute | solution.py:51
  123.3 9.1 %collective-permute-start.30 = (bf16[14,32,128]{2,1,0:T(8,128)(2,1)S(1)}, bf16[14,32,128]{2,1,0:T(8,128)(2,1)S(1)}, u32[]{:S(2)}, u32[]{:S(2)}) collective-permute-start(bf16[14,32,128]{2,1,0:T(8,128)(2,1)S(1)} %fusion.8), channel_id=1, source_target_pairs={{0,2},{1,3},{2,0},{3,1},{4,6},{5,7},{6,4},{7,5},{8,10},{9,11},{10,... | collective-permute-start | bytes 344072 | tf_op jit(solution)/shard_map/ppermute | solution.py:51
